TPU v7x, 128 devices: a whole 4x4x4 slice. The times are simulated.
128 devices in a mesh: pat: 32 (over y, z_hi, x), feat: 2 (over core), tm: 2 (over z_lo).
Axes of the slice: x: 4, y: 4, z: 4 (z_hi: 2, z_lo: 2; z = z_hi * 2 + z_lo), core: 2. Of those that a mesh axis runs over, the one named last changes fastest.
Arguments:
- tensor: float32 [256, 16, 131072], P('feat', 'tm', 'pat'), may hold values from -200 to 200
- feat_init: float32 [32, 256], P(None, 'feat'), may hold values from -6 to 6
- time_init: float32 [32, 16], P(None, 'tm'), may hold values from -6 to 6
Outputs:
- factor_pat: float32 [32, 131072], P(None, 'pat')
- factor_feat: float32 [32, 256], P(None, 'feat')
- factor_time: float32 [32, 16], P(None, 'tm')
All inputs are finite; a program needn't handle non-finite values.
Results may differ from a plain program's by a relative error of at most 0.000075.
Values sent between devices are 32-bit elements; how exact they have to be, the bound alone decides.
No kernel may reach another device: no remote copies, remote signals or barrier semaphores. Data moves between devices by JAX's collectives and lax.ppermute only.
A program may use at most 64 MiB of HBM per device.

v0:
```python
import math

import jax
import jax.numpy as jnp
from jax import lax
from jax.sharding import PartitionSpec as P

highest = lax.Precision.HIGHEST
epsilon = 1e-06


def gram_of(factor):
    return jnp.dot(factor, factor.T, precision=highest)


def solve_system(system, terms):
    lower = jnp.linalg.cholesky(system)
    return jax.scipy.linalg.cho_solve((lower, True), terms)


def scale_by_sums(raw_factor, square_sums, total):
    inverse_norm = 1.0 / jnp.sqrt(square_sums / total + epsilon)
    return raw_factor * inverse_norm[:, None]


def per_device(tensor, feat_init, time_init):
    feat_dev, time_dev, rows_dev = tensor.shape
    rank_count = feat_init.shape[0]
    total_pat = rows_dev * lax.axis_size("pat")
    total_feat = feat_dev * lax.axis_size("feat")
    flat = tensor.reshape(feat_dev * time_dev, rows_dev)
    start_feat = lax.psum(gram_of(feat_init), "feat")
    start_time = lax.psum(gram_of(time_init), "tm")
    khatri_rao = (feat_init[:, :, None] * time_init[:, None, :]).reshape(
        rank_count, feat_dev * time_dev
    )
    pat_terms = jnp.dot(khatri_rao, flat, precision=highest)
    pat_system = start_feat * start_time
    summed = lax.psum(pat_terms, ("feat", "tm"))
    local_raw = solve_system(pat_system, summed)
    copy_weight = 1.0 / (lax.axis_size("feat") * lax.axis_size("tm"))
    square_sums = lax.psum(
        jnp.sum(local_raw * local_raw, axis=1) * copy_weight, ("pat", "feat", "tm")
    )
    local_scaled = scale_by_sums(local_raw, square_sums, total_pat)
    pat_gram = lax.psum(gram_of(local_scaled) * copy_weight, ("pat", "feat", "tm")) / total_pat
    weighted = lax.dot_general(
        local_scaled, flat, (((1,), (1,)), ((), ())), precision=highest
    ).reshape(rank_count, feat_dev, time_dev)
    feat_terms = lax.psum(jnp.sum(weighted * time_init[:, None, :], axis=2), ("pat", "tm"))
    feat_raw = solve_system(pat_gram * start_time, feat_terms)
    square_sums = lax.psum(jnp.sum(feat_raw * feat_raw, axis=1), "feat")
    factor_feat = scale_by_sums(feat_raw, square_sums, total_feat)
    feat_gram = lax.psum(gram_of(factor_feat), "feat") / total_feat
    time_terms = lax.psum(jnp.sum(weighted * factor_feat[:, :, None], axis=1), ("pat", "feat"))
    factor_time = solve_system(pat_gram * feat_gram, time_terms) * (
        1.0 / math.sqrt(total_pat * total_feat)
    )
    return (local_scaled, factor_feat, factor_time)


def solution(mesh):
    placed = (P("feat", "tm", "pat"), P(None, "feat"), P(None, "tm"))
    return jax.shard_map(
        per_device,
        mesh=mesh,
        in_specs=placed,
        out_specs=(P(None, "pat"), P(None, "feat"), P(None, "tm")),
        check_vma=False,
    )
```

profile of v0, /device:TPU:1, one launch (start us, length us, event | category | flops | bytes accessed | tf_op | source)
XLA Modules:
  0.0 773.7 jit_solution(12282244122623873367)
XLA Ops:
  7.2 0.0 copy-start.2
  7.2 0.0 copy-start.1
  7.2 0.0 all-reduce.2.cloned.1.call-start
  7.2 25.5 %fusion.4 = f32[32,4096]{1,0:T(8,128)} fusion(f32[128,8,4096]{2,1,0:T(8,128)} %param.4, f32[32,8]{0,1:T(8,128)} %param.6, f32[32,128]{1,0:T(8,128)} %param.5), kind=kOutput, calls=%fused_computation.4 | convolution fusion | flops 1610645504 | bytes 17318912 | tf_op jit(solution)/shard_map/dot_general | solution.py:37
  32.7 0.0 all-reduce.2.cloned.1.call-update
  32.8 0.0 copy-done.1
  32.8 0.1 fusion.28
  32.9 0.0 copy-done.2
  32.9 0.2 fusion.29
  33.1 4.6 psum.63
  37.8 6.6 psum.64
  44.4 0.1 copy.16
  44.5 2.9 cholesky.59
  47.4 0.6 compare_reduce_fusion.2
  48.1 0.7 fusion.11
  48.7 2.4 custom-call.23
  51.2 27.1 %all-reduce.2.cloned.1.call-done = f32[32,4096]{1,0:T(8,128)} async-done(((f32[32,4096]{1,0:T(8,128)}), f32[32,4096]{1,0:T(8,128)}) %all-reduce.2.cloned.1.call-update) | async-done | bytes 524304 | tf_op jit(solution)/shard_map/psum | solution.py:39
  78.3 1.7 fusion.25
  80.0 0.7 multiply_reduce_fusion
  80.7 66.4 %psum.66 = f32[32]{0:T(128)S(1)} all-reduce(f32[32]{0:T(128)S(1)} %broadcast_multiply_fusion.2), channel_id=1, replica_groups=mesh['pat'=32,'feat'=2,'tm'=2] {'pat','feat','tm'}, use_global_device_ids=true, to_apply=%region_6.8 | all-reduce | flops 32 | bytes 256 | tf_op jit(solution)/shard_map/psum | solution.py:42
  147.1 0.1 broadcast_multiply_fusion
  147.2 0.0 copy-start
  147.3 0.6 convolution_multiply_fusion
  147.8 27.3 %multiply_reduce_fusion.2 = (f32[32,128]{1,0:T(8,128)S(1)}, f32[32,128,8]{1,0,2:T(8,128)S(1)}) fusion(f32[32,8]{0,1:T(8,128)S(1)} %copy-done.2, f32[128,8,4096]{2,1,0:T(8,128)} %param.4, f32[32,4096]{1,0:T(8,128)S(1)} %broadcast_multiply_fusion), kind=kOutput, calls=%fused_computation.11 | convolution fusion | flops 1610674176 | bytes 17449984 | tf_op jit(solution)/shard_map/dot_general | solution.py:47
  175.2 62.6 %psum.67 = f32[32,32]{0,1:T(8,128)S(1)} all-reduce(f32[32,32]{0,1:T(8,128)S(1)} %convolution_multiply_fusion), channel_id=1, replica_groups=mesh['pat'=32,'feat'=2,'tm'=2] {'pat','feat','tm'}, use_global_device_ids=true, to_apply=%region_7.9 | all-reduce | flops 1024 | bytes 8192 | tf_op jit(solution)/shard_map/psum | solution.py:46
  237.8 0.1 copy.18
  237.9 2.9 cholesky.70
  240.8 0.6 compare_reduce_fusion.1
  241.5 0.7 fusion.12
  242.1 2.4 custom-call.24
  244.5 290.1 %psum.68 = f32[32,128]{1,0:T(8,128)S(1)} all-reduce(f32[32,128]{1,0:T(8,128)S(1)} %get-tuple-element.6), channel_id=1, replica_groups=mesh['pat'=32,'feat'=2,'tm'=2] {'pat','tm'}, use_global_device_ids=true, to_apply=%region_9.11 | all-reduce | flops 4096 | bytes 32768 | tf_op jit(solution)/shard_map/psum | solution.py:50
  534.7 0.2 fusion.20
  534.9 0.3 multiply_reduce_fusion.3
  535.1 57.4 %psum.69 = f32[32]{0:T(128)S(1)} all-reduce(f32[32]{0:T(128)S(1)} %get-tuple-element.8), channel_id=1, replica_groups=mesh['pat'=32,'feat'=2,'tm'=2] {'feat'}, use_global_device_ids=true, to_apply=%region_11.13 | all-reduce | flops 32 | bytes 256 | tf_op jit(solution)/shard_map/psum | solution.py:52
  592.5 0.1 broadcast_multiply_fusion.1
  592.6 0.0 copy-start.3
  592.6 0.1 fusion.30
  592.8 0.1 multiply_reduce_fusion.1
  592.9 162.2 %psum.71 = f32[32,8]{0,1:T(8,128)S(1)} all-reduce(f32[32,8]{0,1:T(8,128)S(1)} %multiply_reduce_fusion.1), channel_id=1, replica_groups=mesh['pat'=32,'feat'=2,'tm'=2] {'pat','feat'}, use_global_device_ids=true, to_apply=%region_14.16 | all-reduce | flops 256 | bytes 2048 | tf_op jit(solution)/shard_map/psum | solution.py:55
  755.1 4.0 psum.70
  759.1 0.1 copy.21
  759.2 2.9 cholesky.81
  762.1 0.6 compare_reduce_fusion
  762.8 0.7 fusion.13
  763.4 2.4 custom-call.25
  765.8 0.2 fusion.15
  766.1 0.8 convolution_multiply_fusion.1
  766.9 0.0 copy-done
  766.9 0.0 copy-done.3
  (12 shorter events, 0.2 us)
Async XLA Ops:
  7.2 25.8 %copy-start.2 = (f32[32,8]{0,1:T(8,128)S(1)}, f32[32,8]{0,1:T(8,128)}, u32[]{:S(2)}) copy-start(f32[32,8]{0,1:T(8,128)} %param.6) | copy-start | bytes 3076
  7.2 25.6 %copy-start.1 = (f32[32,128]{1,0:T(8,128)S(1)}, f32[32,128]{1,0:T(8,128)}, u32[]{:S(2)}) copy-start(f32[32,128]{1,0:T(8,128)} %param.5) | copy-start | bytes 49156
  7.2 71.1 %all-reduce.2.cloned.1.call-start = ((), (), s32[]{:S(2)}) async-start(), calls=%async_computation | async-start | bytes 1048576 | tf_op jit(solution)/shard_map/psum | solution.py:39
  147.2 619.7 %copy-start = (f32[32,4096]{1,0:T(8,128)}, f32[32,4096]{1,0:T(8,128)S(1)}, u32[]{:S(2)}) copy-start(f32[32,4096]{1,0:T(8,128)S(1)} %broadcast_multiply_fusion) | copy-start | bytes 1572868
  592.6 174.3 %copy-start.3 = (f32[32,128]{1,0:T(8,128)}, f32[32,128]{1,0:T(8,128)S(1)}, u32[]{:S(2)}) copy-start(f32[32,128]{1,0:T(8,128)S(1)} %broadcast_multiply_fusion.1) | copy-start | bytes 49156
Sparse Core Ops, SparseCore 0:
  32.9 45.3 all-reduce.1
where the time goes:
time: 774 us
  blocking collectives  654 us (84%)
  matrix products  57.7 us (7%)
  waiting for transfers between devices  27.2 us (4%)
  other arithmetic  20.4 us (3%)
  between operations  14.2 us (2%)
    psum x1, blocking collectives, per_device(): lax.psum(jnp.sum(weighted * time_init[:, None, :], axis=2), ('pat', 'tm'))  290 us
    psum x1, blocking collectives, per_device(): lax.psum(jnp.sum(weighted * factor_feat[:, :, None], axis=1), ('pat', 'fe...  162 us
    psum x1, blocking collectives, per_device(): lax.psum(jnp.sum(local_raw * local_raw, axis=1) * copy_weight, ('pat', 'f...  66.4 us
    psum x1, blocking collectives, per_device(): lax.psum(gram_of(local_scaled) * copy_weight, ('pat', 'feat', 'tm'))  62.6 us
    psum x1, blocking collectives, per_device(): square_sums = lax.psum(jnp.sum(feat_raw * feat_raw, axis=1), 'feat')  57.4 us
    dot_general x1, matrix products, per_device(): lax.dot_general(local_scaled, flat, (((1,), (1,)), ((), ())), precision=h...  27.3 us
    psum x1, waiting for transfers between devices, per_device(): summed = lax.psum(pat_terms, ('feat', 'tm'))  27.1 us
    dot_general x1, matrix products, per_device(): pat_terms = jnp.dot(khatri_rao, flat, precision=highest)  25.5 us
  transfers between devices with their start and end apart: 1, of which 1 were waited for; matrix products, arithmetic and copies ran while one was open for 1% of the time, Pallas kernels for 0%

commit v1 on v0

v1 whole, which is shorter than its diff:
```python
import math

import jax
import jax.numpy as jnp
from jax import lax
from jax.experimental import pallas as pl
from jax.experimental.pallas import tpu as pltpu
from jax.sharding import PartitionSpec as P

f32, bf16 = jnp.float32, jnp.bfloat16
highest = lax.Precision.HIGHEST
epsilon = 1e-06
VMEM = pl.BlockSpec(memory_space=pltpu.VMEM)
HBM = pl.BlockSpec(memory_space=pltpu.HBM)
NN = (((1,), (0,)), ((), ()))
NT = (((1,), (1,)), ((), ()))
LANES = 128


def exact(a, b, dims=NN):
    return lax.dot_general(a, b, dims, precision=highest, preferred_element_type=f32)


def quick(a, b, dims=NN):
    return lax.dot_general(a, b, dims, preferred_element_type=f32)


def split(x):
    hi = x.astype(bf16)
    return hi, (x - hi.astype(f32)).astype(bf16)


def iota(shape, dim):
    return lax.broadcasted_iota(jnp.int32, shape, dim)


def one_hot_feat(feat, time):
    shape = (feat, feat * time)
    return jnp.where(lax.div(iota(shape, 1), time) == iota(shape, 0), 1.0, 0.0).astype(f32)


def one_hot_time(feat, time):
    shape = (time, feat * time)
    return jnp.where(lax.rem(iota(shape, 1), time) == iota(shape, 0), 1.0, 0.0).astype(f32)


def eliminate(tiles, group=8):
    rank = tiles[0].shape[0]
    rows = iota((rank, LANES), 0)
    for start in range(0, rank, group):
        columns = [
            jnp.broadcast_to(tiles[0][:, start + t : start + t + 1], (rank, LANES)) for t in range(group)
        ]
        for t in range(group):
            at = start + t
            column = columns[t]
            inverse = 1.0 / column[at : at + 1, :]
            here = rows == at
            for later in range(t + 1, group):
                scaled = columns[later][at : at + 1, :] * inverse
                columns[later] = jnp.where(here, scaled, columns[later] - column * scaled)
            new = []
            for tile in tiles:
                scaled = tile[at : at + 1, :] * inverse
                new.append(jnp.where(here, scaled, tile - column * scaled))
            tiles = new
    return tiles


def wide(x, columns=LANES):
    return jnp.concatenate([x, jnp.zeros((x.shape[0], columns - x.shape[1]), f32)], axis=1)


def call(body, out_shape, name, specs, scratch=(), limit=24, flops=0, moved=0):
    return pl.pallas_call(
        body,
        out_shape=[jax.ShapeDtypeStruct(s, d) for s, d in out_shape],
        in_specs=specs,
        out_specs=[VMEM] * len(out_shape),
        scratch_shapes=list(scratch),
        compiler_params=pltpu.CompilerParams(vmem_limit_bytes=limit * 2**20),
        cost_estimate=pl.CostEstimate(flops=flops, bytes_accessed=moved, transcendentals=0),
        name=name,
    )


CHUNK = 256
DEPTH = 256


def terms_of_half(hl_ref, block_ref, kept_ref, terms_ref, sems, first, build=None):
    rank = terms_ref.shape[0]
    cells, half = kept_ref.shape
    copies = []
    for c in range(half // CHUNK):
        start = pl.multiple_of(first + c * CHUNK, CHUNK)
        copies.append(
            pltpu.make_async_copy(
                block_ref.at[:, pl.ds(start, CHUNK)], kept_ref.at[:, pl.ds(c * CHUNK, CHUNK)], sems.at[c]
            )
        )
    for copy in copies:
        copy.start()
    if build is not None:
        build()
    for c, copy in enumerate(copies):
        copy.wait()
        total = None
        for d in range(0, cells, DEPTH):
            hi, lo = split(kept_ref[d : d + DEPTH, c * CHUNK : (c + 1) * CHUNK])
            both = quick(hl_ref[:, d : d + DEPTH], hi)
            part = both[:rank] + both[rank:] + quick(hl_ref[:rank, d : d + DEPTH], lo)
            total = part if total is None else total + part
        terms_ref[:, c * CHUNK : (c + 1) * CHUNK] = total


def first_half(feat_ref, time_ref, block_ref, terms_ref, kept_ref, hl_ref, sems):
    half = kept_ref.shape[1]

    def build():
        feat, time = feat_ref[...], time_ref[...]
        count = (feat.shape[1], time.shape[1])
        product = exact(feat, one_hot_feat(*count)) * exact(time, one_hot_time(*count))
        hi, lo = split(product)
        hl_ref[...] = jnp.concatenate([hi, lo], axis=0)

    other = 1 - lax.axis_index("feat")
    terms_of_half(hl_ref, block_ref, kept_ref, terms_ref, sems, other * half, build)


def second_half(hl_ref, block_ref, terms_ref, kept_ref, sems):
    half = kept_ref.shape[1]
    terms_of_half(hl_ref, block_ref, kept_ref, terms_ref, sems, lax.axis_index("feat") * half)


def start_system(feat_ref, feat_other_ref, time_ref, time_other_ref, inverse_ref, time_gram_ref):
    rank = feat_ref.shape[0]
    feat, feat_other = feat_ref[...], feat_other_ref[...]
    time, time_other = time_ref[...], time_other_ref[...]
    time_gram = exact(time, time, NT) + exact(time_other, time_other, NT)
    system = (exact(feat, feat, NT) + exact(feat_other, feat_other, NT)) * time_gram
    eye = jnp.where(iota((rank, rank), 0) == iota((rank, rank), 1), 1.0, 0.0).astype(f32)
    (solved,) = eliminate([wide(jnp.concatenate([system, eye], axis=1))])
    inverse_ref[...] = solved[:, rank : 2 * rank]
    time_gram_ref[...] = time_gram


def solve_pat(inverse_ref, *refs):
    ins, (out_ref,) = refs[:-1], refs[-1:]
    pairs = len(ins) // 2
    width = out_ref.shape[1] // pairs
    for i in range(pairs):
        out_ref[:, i * width : (i + 1) * width] = exact(inverse_ref[...], ins[i][...] + ins[pairs + i][...])


def weigh(raw_ref, kept_ref, *refs):
    before, out_ref = (refs[0], refs[1]) if len(refs) == 2 else (None, refs[0])
    rank, half = raw_ref.shape
    cells = kept_ref.shape[0]
    hi, lo = split(raw_ref[...])
    hl = jnp.concatenate([hi, lo], axis=0)
    total = None
    for c in range(0, half, 512):
        kept_hi, kept_lo = split(kept_ref[:, c : c + 512])
        both = quick(kept_hi, hl[:, c : c + 512], NT)
        part = both[:, :rank] + both[:, rank:] + quick(kept_lo, hl[:rank, c : c + 512], NT)
        total = part if total is None else total + part
    weighted = total.T
    gram = wide(exact(raw_ref[...], raw_ref[...], NT))
    if before is not None:
        weighted = weighted + before[:, :cells]
        gram = gram + before[:, cells:]
    out_ref[:, :cells] = weighted
    out_ref[:, cells:] = gram


def add_four(a_ref, b_ref, c_ref, d_ref, out_ref):
    out_ref[...] = (a_ref[...] + b_ref[...]) + (c_ref[...] + d_ref[...])


def add_and_project(a_ref, b_ref, c_ref, d_ref, time_ref, out_ref, feat_terms_ref):
    total = (a_ref[...] + b_ref[...]) + (c_ref[...] + d_ref[...])
    out_ref[...] = total
    feat_count, time_count = feat_terms_ref.shape[1], time_ref.shape[1]
    cells = feat_count * time_count
    spread = exact(time_ref[...], one_hot_time(feat_count, time_count))
    feat_terms_ref[...] = exact(total[:, :cells] * spread, one_hot_feat(feat_count, time_count), NT)


def diagonal(square):
    kept = jnp.where(iota(square.shape, 0) == iota(square.shape, 1), square, 0.0)
    return jnp.sum(kept, axis=1, keepdims=True), jnp.sum(kept, axis=0, keepdims=True)


def norms(square):
    column, row = diagonal(square)
    return 1.0 / jnp.sqrt(column + epsilon), 1.0 / jnp.sqrt(row + epsilon)


def solve_feat(total_pat, a_ref, b_ref, t0_ref, t1_ref, t2_ref, t3_ref, time_gram_ref, raw_ref, sums_ref, gram_ref, scale_ref):
    rank, feat_count = raw_ref.shape
    cells = a_ref.shape[1] - LANES
    time_count = cells // feat_count
    gram = (a_ref[:, cells:] + b_ref[:, cells:])[:, :rank] / total_pat
    column, row = norms(gram)
    pat_gram = gram * column * row
    feat_terms = ((t0_ref[...] + t1_ref[...]) + (t2_ref[...] + t3_ref[...])) * column
    _, raw = eliminate([wide(pat_gram * time_gram_ref[...]), feat_terms])
    weighted = (a_ref[:, :cells] + b_ref[:, :cells]) * column
    spread = exact(raw, one_hot_feat(feat_count, time_count))
    time_terms = exact(weighted * spread, one_hot_time(feat_count, time_count), NT)
    raw_ref[...] = raw
    sums_ref[...] = wide(jnp.concatenate([exact(raw, raw, NT), time_terms], axis=1))
    gram_ref[...] = pat_gram
    scale_ref[...] = jnp.broadcast_to(column, scale_ref.shape)


def solve_time(total_pat, total_feat, a_ref, b_ref, raw_ref, gram_ref, feat_ref, time_ref):
    rank, time_count = time_ref.shape
    total = a_ref[...] + b_ref[...]
    gram = total[:, :rank] / total_feat
    column, row = norms(gram)
    feat_ref[...] = raw_ref[...] * column
    system = gram_ref[...] * (gram * column * row)
    terms = total[:, rank : rank + time_count] * column
    (solved,) = eliminate([wide(jnp.concatenate([system, terms], axis=1))])
    time_ref[...] = solved[:, rank : rank + time_count] * (1.0 / math.sqrt(total_pat * total_feat))


def scale_pat(own_ref, other_ref, scale_ref, out_ref):
    half = own_ref.shape[1]
    scale = scale_ref[:, :1]
    me = lax.axis_index("feat")
    out_ref[:, pl.ds(pl.multiple_of(me * half, half), half)] = own_ref[...] * scale
    out_ref[:, pl.ds(pl.multiple_of((1 - me) * half, half), half)] = other_ref[...] * scale


def per_device(tensor, feat_init, time_init):
    feat_dev, time_dev, rows_dev = tensor.shape
    rank = feat_init.shape[0]
    total_pat = rows_dev * lax.axis_size("pat")
    total_feat = feat_dev * lax.axis_size("feat")
    cells, half = feat_dev * time_dev, rows_dev // 2
    flat = tensor.reshape(cells, rows_dev)
    swap = [(0, 1), (1, 0)]

    def from_core(x):
        return lax.ppermute(x, "feat", swap)

    def from_tm(x):
        return lax.ppermute(x, "tm", swap)

    def from_pat(x, flip):
        return lax.ppermute(x, "pat", [(i, i ^ flip) for i in range(lax.axis_size("pat"))])

    def from_both(x, flip):
        count = 2 * lax.axis_size("pat")
        return lax.ppermute(x, ("pat", "tm"), [(i, i ^ (2 * flip + 1)) for i in range(count)])

    feat_other = from_core(feat_init)
    time_other = from_tm(time_init)

    sems = [pltpu.SemaphoreType.DMA((half // CHUNK,))]
    work = dict(flops=2 * 3 * rank * cells * half, moved=4 * cells * half)
    terms_for_core, kept_other, hl = call(
        first_half,
        [((rank, half), f32), ((cells, half), f32), ((2 * rank, cells), bf16)],
        "first_half", [VMEM, VMEM, HBM], sems, 44, **work,
    )(feat_init, time_init, flat)
    arrived = from_core(terms_for_core)
    hl, feat_other, time_other = lax.optimization_barrier((hl, feat_other, time_other))
    terms_own, kept_own = call(
        second_half, [((rank, half), f32), ((cells, half), f32)], "second_half", [VMEM, HBM], sems, 40, **work
    )(hl, flat)

    pieces = 2
    width = half // pieces
    mine = [terms_own[:, i * width : (i + 1) * width] + arrived[:, i * width : (i + 1) * width] for i in range(pieces)]
    theirs = [from_tm(x) for x in mine]
    inverse, time_gram = call(
        start_system, [((rank, rank), f32), ((rank, rank), f32)], "start_system", [VMEM] * 4, flops=2**21, moved=2**16
    )(feat_init, feat_other, time_init, time_other)
    (raw_own,) = call(solve_pat, [((rank, half), f32)], "solve_pat", [VMEM] * (1 + 2 * pieces), flops=2**26, moved=2**20)(
        inverse, *mine, *theirs
    )
    raw_other = from_core(raw_own)
    payload = [((rank, cells + LANES), f32)]
    (part,) = call(weigh, payload, "weigh_own", [VMEM] * 2, **work)(raw_own, kept_own)
    (part,) = call(weigh, payload, "weigh_other", [VMEM] * 3, **work)(raw_other, kept_other, part)

    x_parts = [from_pat(part, flip) for flip in (1, 2, 3)]
    (part,) = call(add_four, payload, "add_x", [VMEM] * 4, flops=2**18, moved=2**20)(part, *x_parts)
    y_parts = [from_pat(part, flip) for flip in (8, 16, 24)]
    part, feat_terms = call(
        add_and_project, payload + [((rank, feat_dev), f32)], "add_y", [VMEM] * 5, flops=2**26, moved=2**20
    )(part, *y_parts, time_init)
    part_hi = from_pat(part, 4)
    terms_hi = from_pat(feat_terms, 4)
    terms_tm = from_tm(feat_terms)
    terms_far = from_both(feat_terms, 4)
    feat_raw, sums, pat_gram, scale = call(
        lambda *refs: solve_feat(total_pat, *refs),
        [((rank, feat_dev), f32), ((rank, LANES), f32), ((rank, rank), f32), ((rank, LANES), f32)],
        "solve_feat", [VMEM] * 7, flops=2**26, moved=2**20,
    )(part, part_hi, feat_terms, terms_tm, terms_hi, terms_far, time_gram)
    sums_core = from_core(sums)
    (factor_pat,) = call(scale_pat, [((rank, rows_dev), f32)], "scale_pat", [VMEM] * 3, flops=2**18, moved=2**20)(
        raw_own, raw_other, scale
    )
    factor_feat, factor_time = call(
        lambda *refs: solve_time(total_pat, total_feat, *refs),
        [((rank, feat_dev), f32), ((rank, time_dev), f32)],
        "solve_time", [VMEM] * 4, flops=2**22, moved=2**17,
    )(sums, sums_core, feat_raw, pat_gram)
    return (factor_pat, factor_feat, factor_time)


def solution(mesh):
    placed = (P("feat", "tm", "pat"), P(None, "feat"), P(None, "tm"))
    return jax.shard_map(
        per_device,
        mesh=mesh,
        in_specs=placed,
        out_specs=(P(None, "pat"), P(None, "feat"), P(None, "tm")),
        check_vma=False,
    )
```

time: 774 us -> 68.5 us (0.09)
  blocking collectives: 654 us -> 0 us
  matrix products: 57.7 us -> 0 us
  starting transfers between devices: 0.04 us -> 25.3 us
  other arithmetic: 20.4 us -> 0.03 us
  Pallas kernels: 0 us -> 20 us
  between operations: 14.2 us -> 0.69 us
    psum x8 -> x0, blocking collectives: 654 us -> none  [the longest x1 290 us: per_device(): lax.psum(jnp.sum(weighted * time_init[:, None, :], axis=2), ('pat', 'tm'))]
    dot_general x6 -> x0, matrix products: 53.9 us -> none  [the longest x1 27.3 us: per_device(): lax.dot_general(local_scaled, flat, (((1,), (1,)), ((), ())), precision=h...]
    psum x1 -> x0, waiting for transfers between devices: 27.1 us -> none  [per_device(): summed = lax.psum(pat_terms, ('feat', 'tm'))]
    ppermute x0 -> x17, starting transfers between devices: none -> 25.3 us  [the longest x8 12.3 us: from_pat(): lax.ppermute(x, 'pat', [(i, i ^ flip) for i in range(lax.axis_size('pat'))])]
    ppermute x0 -> x17, waiting for transfers between devices: none -> 20.2 us  [the longest x8 13.9 us: from_pat(): lax.ppermute(x, 'pat', [(i, i ^ flip) for i in range(lax.axis_size('pat'))])]
    another operation x15 -> x0, other arithmetic: 20 us -> none  [the longest x9 10.8 us: solve_system(): lower = jnp.linalg.cholesky(system)]
    pallas_call x0 -> x11, Pallas kernels: none -> 20 us  [the longest x1 4.71 us: per_device(): call(first_half, [((rank, half), f32), ((cells, half), f32), ((2 * rank,...]
  transfers between devices with their start and end apart: 1 -> 17, of which waited for: 1 -> 11; matrix products, arithmetic and copies ran while one was open for 1% -> 0% of each run, Pallas kernels for 0% -> 13%
where the time goes in v1:
time: 68.5 us; the launch traced here: 68.4 us
  starting transfers between devices  25.3 us (37%)
  waiting for transfers between devices  20.2 us (29%)
  Pallas kernels  20 us (29%)
  local copies, waits for them, and re-layouts  2.14 us (3%)
  between operations  0.69 us (1%)
    ppermute x8, waiting for transfers between devices, from_pat(): lax.ppermute(x, 'pat', [(i, i ^ flip) for i in range(lax.axis_size('pat'))])  13.9 us
    ppermute x8, starting transfers between devices, from_pat(): lax.ppermute(x, 'pat', [(i, i ^ flip) for i in range(lax.axis_size('pat'))])  12.3 us
    ppermute x4, starting transfers between devices, from_core(): return lax.ppermute(x, 'feat', swap)  8.44 us
    ppermute x4, waiting for transfers between devices, from_tm(): return lax.ppermute(x, 'tm', swap)  5.79 us
    pallas_call x1, Pallas kernels, per_device(): call(first_half, [((rank, half), f32), ((cells, half), f32), ((2 * rank,...  4.71 us
    pallas_call x1, Pallas kernels, per_device(): call(second_half, [((rank, half), f32), ((cells, half), f32)], 'second_ha...  4.56 us
    ppermute x4, starting transfers between devices, from_tm(): return lax.ppermute(x, 'tm', swap)  4.1 us
    pallas_call x1, Pallas kernels, per_device(): call(weigh, payload, 'weigh_other', [VMEM] * 3, **work)  2.59 us
  transfers between devices with their start and end apart: 17, of which 11 were waited for; matrix products, arithmetic and copies ran while one was open for 0% of the time, Pallas kernels for 13%

profile of v1, /device:TPU:1, one launch (start us, length us, event | category | flops | bytes accessed | tf_op | source)
XLA Modules:
  0.0 68.4 jit_solution(4993729946108461124)
XLA Ops:
  0.6 0.8 %copy.6.time_ref = f32[32,8]{1,0:T(8,128)S(1)} copy(f32[32,8]{0,1:T(8,128)} %param.5) | data formatting | bytes 2048 | tf_op args[2]
  1.4 0.0 copy-start
  1.4 0.7 %copy-done = f32[32,128]{1,0:T(8,128)S(1)} copy-done((f32[32,128]{1,0:T(8,128)S(1)}, f32[32,128]{1,0:T(8,128)}, u32[]{:S(2)}) %copy-start) | copy-done | bytes 16408
  2.1 4.7 %first_half.1 = (f32[32,2048]{1,0:T(8,128)S(1)}, f32[1024,2048]{1,0:T(8,128)S(1)}, bf16[64,1024]{1,0:T(8,128)(2,1)S(1)}) custom-call(f32[32,128]{1,0:T(8,128)S(1)} %copy-done, f32[32,8]{1,0:T(8,128)S(1)} %copy.6.time_ref, f32[1024,4096]{1,0:T(8,128)} %bitcast.1), custom_call_target="tpu_custom_call" | custom-call | flops 402653184 | bytes 8388608 | tf_op jit(solution)/shard_map/first_half/pallas_call | solution.py:265
  6.8 1.5 %collective-permute-start.2 = (f32[32,2048]{1,0:T(8,128)S(1)}, f32[32,2048]{1,0:T(8,128)S(1)}, u32[]{:S(2)}, u32[]{:S(2)}) collective-permute-start(f32[32,2048]{1,0:T(8,128)S(1)} %get-tuple-element.27), channel_id=1, source_target_pairs={{0,2},{2,0},{1,3},{3,1},{4,6},{6,4},{5,7},{7,5},{8,10},{10,8},{9,1... | collective-permute-start | bytes 786440 | tf_op jit(solution)/shard_map/ppermute | solution.py:248
  8.3 0.1 collective-permute-start
  8.4 1.7 %collective-permute-start.1 = (f32[32,8]{1,0:T(8,128)S(1)}, f32[32,8]{1,0:T(8,128)S(1)}, u32[]{:S(2)}, u32[]{:S(2)}) collective-permute-start(f32[32,8]{1,0:T(8,128)S(1)} %copy.6.time_ref), channel_id=1, source_target_pairs={{0,1},{1,0},{2,3},{3,2},{4,5},{5,4},{6,7},{7,6},{8,9},{9,8},{10,11... | collective-permute-start | bytes 3080 | tf_op jit(solution)/shard_map/ppermute | solution.py:251
  10.1 1.1 %collective-permute-done.1.time_other_ref = f32[32,8]{1,0:T(8,128)S(1)} collective-permute-done((f32[32,8]{1,0:T(8,128)S(1)}, f32[32,8]{1,0:T(8,128)S(1)}, u32[]{:S(2)}, u32[]{:S(2)}) %collective-permute-start.1) | collective-permute-done | bytes 1056 | tf_op jit(solution)/shard_map/ppermute | solution.py:251
  11.3 0.0 collective-permute-done.feat_other_ref
  11.3 4.6 %second_half.1 = (f32[32,2048]{1,0:T(8,128)S(1)}, f32[1024,2048]{1,0:T(8,128)S(1)}) custom-call(bf16[64,1024]{1,0:T(8,128)(2,1)S(1)} %get-tuple-element.25.hl_ref, f32[1024,4096]{1,0:T(8,128)} %bitcast.2), custom_call_target="tpu_custom_call" | custom-call | flops 402653184 | bytes 8388608 | tf_op jit(solution)/shard_map/second_half/pallas_call | solution.py:272
  15.8 0.0 collective-permute-done.2
  15.9 1.5 %collective-permute-start.4 = (f32[32,1024]{1,0:T(8,128)S(1)}, f32[32,1024]{1,0:T(8,128)S(1)}, u32[]{:S(2)}, u32[]{:S(2)}) collective-permute-start(f32[32,1024]{1,0:T(8,128)S(1)} %get-tuple-element.42.refs_1_), channel_id=1, source_target_pairs={{0,1},{1,0},{2,3},{3,2},{4,5},{5,4},{6,7},{7,6},{8,9},{9,8},{10,11... | collective-permute-start | bytes 393224 | tf_op jit(solution)/shard_map/ppermute | solution.py:251
  17.4 0.1 collective-permute-start.3
  17.5 1.1 %start_system.1 = (f32[32,32]{1,0:T(8,128)S(1)}, f32[32,32]{1,0:T(8,128)S(1)}) custom-call(f32[32,128]{1,0:T(8,128)S(1)} %copy-done, f32[32,128]{1,0:T(8,128)S(1)} %collective-permute-done.feat_other_ref, f32[32,8]{1,0:T(8,128)S(1)} %copy.6.time_ref, f32[32,8]{1,0:T(8,128)S(1)} %collective-permute-done.1.time_other_ref), custom_call_target="tpu_custom_call" | custom-call | flops 2097152 | bytes 65536 | tf_op jit(solution)/shard_map/start_system/pallas_call | solution.py:280
  18.6 1.2 %collective-permute-done.4.refs_3_ = f32[32,1024]{1,0:T(8,128)S(1)} collective-permute-done((f32[32,1024]{1,0:T(8,128)S(1)}, f32[32,1024]{1,0:T(8,128)S(1)}, u32[]{:S(2)}, u32[]{:S(2)}) %collective-permute-start.4) | collective-permute-done | bytes 131104 | tf_op jit(solution)/shard_map/ppermute | solution.py:251
  19.8 2.8 %collective-permute-done.3.refs_2_ = f32[32,1024]{1,0:T(8,128)S(1)} collective-permute-done((f32[32,1024]{1,0:T(8,128)S(1)}, f32[32,1024]{1,0:T(8,128)S(1)}, u32[]{:S(2)}, u32[]{:S(2)}) %collective-permute-start.3) | collective-permute-done | bytes 131104 | tf_op jit(solution)/shard_map/ppermute | solution.py:251
  22.6 0.3 solve_pat.1.raw_ref.own_ref
  23.0 2.4 %collective-permute-start.5 = (f32[32,2048]{1,0:T(8,128)S(1)}, f32[32,2048]{1,0:T(8,128)S(1)}, u32[]{:S(2)}, u32[]{:S(2)}) collective-permute-start(f32[32,2048]{1,0:T(8,128)S(1)} %solve_pat.1.raw_ref.own_ref), channel_id=1, source_target_pairs={{0,2},{2,0},{1,3},{3,1},{4,6},{6,4},{5,7},{7,5},{8,10},{10,8},{9,1... | collective-permute-start | bytes 786440 | tf_op jit(solution)/shard_map/ppermute | solution.py:248
  25.3 2.6 %weigh_own.1.refs_0_ = f32[32,1152]{1,0:T(8,128)S(1)} custom-call(f32[32,2048]{1,0:T(8,128)S(1)} %solve_pat.1.raw_ref.own_ref, f32[1024,2048]{1,0:T(8,128)S(1)} %get-tuple-element.29.kept_ref), custom_call_target="tpu_custom_call" | custom-call | flops 402653184 | bytes 8388608 | tf_op jit(solution)/shard_map/weigh_own/pallas_call | solution.py:288
  27.9 0.0 collective-permute-done.5.raw_ref.other_ref
  27.9 2.6 %weigh_other.1.a_ref = f32[32,1152]{1,0:T(8,128)S(1)} custom-call(f32[32,2048]{1,0:T(8,128)S(1)} %collective-permute-done.5.raw_ref.other_ref, f32[1024,2048]{1,0:T(8,128)S(1)} %get-tuple-element.28.kept_ref, f32[32,1152]{1,0:T(8,128)S(1)} %weigh_own.1.refs_0_), custom_call_target="tpu_custom_call" | custom-call | flops 402653184 | bytes 8388608 | tf_op jit(solution)/shard_map/weigh_other/pallas_call | solution.py:289
  30.5 2.5 %collective-permute-start.8 = (f32[32,1152]{1,0:T(8,128)S(1)}, f32[32,1152]{1,0:T(8,128)S(1)}, u32[]{:S(2)}, u32[]{:S(2)}) collective-permute-start(f32[32,1152]{1,0:T(8,128)S(1)} %weigh_other.1.a_ref), channel_id=1, source_target_pairs={{0,12},{4,8},{8,4},{12,0},{16,28},{20,24},{24,20},{28,16},{32,44},... | collective-permute-start | bytes 442376 | tf_op jit(solution)/shard_map/ppermute | solution.py:254
  33.0 0.5 collective-permute-start.7
  33.6 0.3 collective-permute-start.6
  33.8 5.7 %collective-permute-done.8.d_ref = f32[32,1152]{1,0:T(8,128)S(1)} collective-permute-done((f32[32,1152]{1,0:T(8,128)S(1)}, f32[32,1152]{1,0:T(8,128)S(1)}, u32[]{:S(2)}, u32[]{:S(2)}) %collective-permute-start.8) | collective-permute-done | bytes 147488 | tf_op jit(solution)/shard_map/ppermute | solution.py:254
  39.5 0.3 collective-permute-done.7.c_ref
  39.7 1.0 %collective-permute-done.6.b_ref = f32[32,1152]{1,0:T(8,128)S(1)} collective-permute-done((f32[32,1152]{1,0:T(8,128)S(1)}, f32[32,1152]{1,0:T(8,128)S(1)}, u32[]{:S(2)}, u32[]{:S(2)}) %collective-permute-start.6) | collective-permute-done | bytes 147488 | tf_op jit(solution)/shard_map/ppermute | solution.py:254
  40.7 2.8 %collective-permute-start.11 = (f32[32,1152]{1,0:T(8,128)S(1)}, f32[32,1152]{1,0:T(8,128)S(1)}, u32[]{:S(2)}, u32[]{:S(2)}) collective-permute-start(f32[32,1152]{1,0:T(8,128)S(1)} %add_x.1.a_ref), channel_id=1, source_target_pairs={{0,96},{4,100},{8,104},{12,108},{16,112},{20,116},{24,120},{28,124... | collective-permute-start | bytes 442376 | tf_op jit(solution)/shard_map/ppermute | solution.py:254
  43.6 0.4 collective-permute-start.10
  43.9 0.3 collective-permute-start.9
  44.2 5.5 %collective-permute-done.11.d_ref = f32[32,1152]{1,0:T(8,128)S(1)} collective-permute-done((f32[32,1152]{1,0:T(8,128)S(1)}, f32[32,1152]{1,0:T(8,128)S(1)}, u32[]{:S(2)}, u32[]{:S(2)}) %collective-permute-start.11) | collective-permute-done | bytes 147488 | tf_op jit(solution)/shard_map/ppermute | solution.py:254
  49.7 0.0 collective-permute-done.10.c_ref
  49.7 0.4 collective-permute-done.9.b_ref
  50.1 0.6 add_y.1
  50.7 3.5 %collective-permute-start.12 = (f32[32,1152]{1,0:T(8,128)S(1)}, f32[32,1152]{1,0:T(8,128)S(1)}, u32[]{:S(2)}, u32[]{:S(2)}) collective-permute-start(f32[32,1152]{1,0:T(8,128)S(1)} %get-tuple-element.30.refs_0_), channel_id=1, source_target_pairs={{0,16},{4,20},{8,24},{12,28},{16,0},{20,4},{24,8},{28,12},{32,48},... | collective-permute-start | bytes 442376 | tf_op jit(solution)/shard_map/ppermute | solution.py:254
  54.1 0.4 collective-permute-start.15
  54.6 2.1 %collective-permute-start.14 = (f32[32,128]{1,0:T(8,128)S(1)}, f32[32,128]{1,0:T(8,128)S(1)}, u32[]{:S(2)}, u32[]{:S(2)}) collective-permute-start(f32[32,128]{1,0:T(8,128)S(1)} %get-tuple-element.31.refs_2_), channel_id=1, source_target_pairs={{0,16},{4,20},{8,24},{12,28},{16,0},{20,4},{24,8},{28,12},{32,48},... | collective-permute-start | bytes 49160 | tf_op jit(solution)/shard_map/ppermute | solution.py:254
  56.6 0.7 %collective-permute-start.13 = (f32[32,128]{1,0:T(8,128)S(1)}, f32[32,128]{1,0:T(8,128)S(1)}, u32[]{:S(2)}, u32[]{:S(2)}) collective-permute-start(f32[32,128]{1,0:T(8,128)S(1)} %get-tuple-element.31.refs_2_), channel_id=1, source_target_pairs={{0,1},{1,0},{2,3},{3,2},{4,5},{5,4},{6,7},{7,6},{8,9},{9,8},{10,11... | collective-permute-start | bytes 49160 | tf_op jit(solution)/shard_map/ppermute | solution.py:251
  57.4 0.5 collective-permute-done.15.refs_5_
  57.9 1.1 %collective-permute-done.14.refs_4_ = f32[32,128]{1,0:T(8,128)S(1)} collective-permute-done((f32[32,128]{1,0:T(8,128)S(1)}, f32[32,128]{1,0:T(8,128)S(1)}, u32[]{:S(2)}, u32[]{:S(2)}) %collective-permute-start.14) | collective-permute-done | bytes 16416 | tf_op jit(solution)/shard_map/ppermute | solution.py:254
  59.0 0.6 collective-permute-done.13.refs_3_
  59.7 0.0 collective-permute-done.12.refs_1_
  59.7 1.5 %solve_feat.1 = (f32[32,128]{1,0:T(8,128)S(1)}, f32[32,128]{1,0:T(8,128)S(1)}, f32[32,32]{1,0:T(8,128)S(1)}, f32[32,128]{1,0:T(8,128)S(1)}) custom-call(f32[32,1152]{1,0:T(8,128)S(1)} %get-tuple-element.30.refs_0_, f32[32,1152]{1,0:T(8,128)S(1)} %collective-permute-done.12.refs_1_, f32[32,128]{1,0:T(8,128)S(1)} %get-tuple-element.31.refs_2_, ...), custom_call_target="tpu_custom_call" | custom-call | flops 67108864 | bytes 1048576 | tf_op jit(solution)/shard_map/solve_feat/pallas_call | solution.py:301
  61.2 4.5 %collective-permute-start.16 = (f32[32,128]{1,0:T(8,128)S(1)}, f32[32,128]{1,0:T(8,128)S(1)}, u32[]{:S(2)}, u32[]{:S(2)}) collective-permute-start(f32[32,128]{1,0:T(8,128)S(1)} %get-tuple-element.34.refs_0_), channel_id=1, source_target_pairs={{0,2},{2,0},{1,3},{3,1},{4,6},{6,4},{5,7},{7,5},{8,10},{10,8},{9,1... | collective-permute-start | bytes 49160 | tf_op jit(solution)/shard_map/ppermute | solution.py:248
  65.7 0.9 %scale_pat.1 = f32[32,4096]{1,0:T(8,128)} custom-call(f32[32,2048]{1,0:T(8,128)S(1)} %solve_pat.1.raw_ref.own_ref, f32[32,2048]{1,0:T(8,128)S(1)} %collective-permute-done.5.raw_ref.other_ref, f32[32,128]{1,0:T(8,128)S(1)} %get-tuple-element.33.scale_ref), custom_call_target="tpu_custom_call" | custom-call | flops 262144 | bytes 1048576 | tf_op jit(solution)/shard_map/scale_pat/pallas_call | solution.py:307
  66.6 0.0 collective-permute-done.16.refs_1_
  66.6 1.1 %solve_time.1 = (f32[32,128]{1,0:T(8,128)}, f32[32,8]{1,0:T(8,128)S(1)}) custom-call(f32[32,128]{1,0:T(8,128)S(1)} %get-tuple-element.34.refs_0_, f32[32,128]{1,0:T(8,128)S(1)} %collective-permute-done.16.refs_1_, f32[32,128]{1,0:T(8,128)S(1)} %get-tuple-element.35.refs_2_, f32[32,32]{1,0:T(8,128)S(1)} %get-tuple-element.36.refs_3_), custom_call_target="tpu_custom_call" | custom-call | flops 4194304 | bytes 131072 | tf_op jit(solution)/shard_map/solve_time/pallas_call | solution.py:310
  67.7 0.7 copy.10
  (2 shorter events, 0.1 us)
Async XLA Ops:
  1.4 0.7 %copy-start = (f32[32,128]{1,0:T(8,128)S(1)}, f32[32,128]{1,0:T(8,128)}, u32[]{:S(2)}) copy-start(f32[32,128]{1,0:T(8,128)} %feat_ref.3) | copy-start | bytes 49156
  6.8 9.0 %collective-permute-start.2 = (f32[32,2048]{1,0:T(8,128)S(1)}, f32[32,2048]{1,0:T(8,128)S(1)}, u32[]{:S(2)}, u32[]{:S(2)}) collective-permute-start(f32[32,2048]{1,0:T(8,128)S(1)} %get-tuple-element.27), channel_id=1, source_target_pairs={{0,2},{2,0},{1,3},{3,1},{4,6},{6,4},{5,7},{7,5},{8,10},{10,8},{9,1... | collective-permute-start | bytes 786440 | tf_op jit(solution)/shard_map/ppermute | solution.py:248
  8.3 2.9 %collective-permute-start = (f32[32,128]{1,0:T(8,128)S(1)}, f32[32,128]{1,0:T(8,128)S(1)}, u32[]{:S(2)}, u32[]{:S(2)}) collective-permute-start(f32[32,128]{1,0:T(8,128)S(1)} %copy-done), channel_id=1, source_target_pairs={{0,2},{2,0},{1,3},{3,1},{4,6},{6,4},{5,7},{7,5},{8,10},{10,8},{9,1... | collective-permute-start | bytes 49160 | tf_op jit(solution)/shard_map/ppermute | solution.py:248
  8.4 2.8 %collective-permute-start.1 = (f32[32,8]{1,0:T(8,128)S(1)}, f32[32,8]{1,0:T(8,128)S(1)}, u32[]{:S(2)}, u32[]{:S(2)}) collective-permute-start(f32[32,8]{1,0:T(8,128)S(1)} %copy.6.time_ref), channel_id=1, source_target_pairs={{0,1},{1,0},{2,3},{3,2},{4,5},{5,4},{6,7},{7,6},{8,9},{9,8},{10,11... | collective-permute-start | bytes 3080 | tf_op jit(solution)/shard_map/ppermute | solution.py:251
  15.9 3.9 %collective-permute-start.4 = (f32[32,1024]{1,0:T(8,128)S(1)}, f32[32,1024]{1,0:T(8,128)S(1)}, u32[]{:S(2)}, u32[]{:S(2)}) collective-permute-start(f32[32,1024]{1,0:T(8,128)S(1)} %get-tuple-element.42.refs_1_), channel_id=1, source_target_pairs={{0,1},{1,0},{2,3},{3,2},{4,5},{5,4},{6,7},{7,6},{8,9},{9,8},{10,11... | collective-permute-start | bytes 393224 | tf_op jit(solution)/shard_map/ppermute | solution.py:251
  17.4 5.2 %collective-permute-start.3 = (f32[32,1024]{1,0:T(8,128)S(1)}, f32[32,1024]{1,0:T(8,128)S(1)}, u32[]{:S(2)}, u32[]{:S(2)}) collective-permute-start(f32[32,1024]{1,0:T(8,128)S(1)} %get-tuple-element.43.refs_0_), channel_id=1, source_target_pairs={{0,1},{1,0},{2,3},{3,2},{4,5},{5,4},{6,7},{7,6},{8,9},{9,8},{10,11... | collective-permute-start | bytes 393224 | tf_op jit(solution)/shard_map/ppermute | solution.py:251
  23.0 4.9 %collective-permute-start.5 = (f32[32,2048]{1,0:T(8,128)S(1)}, f32[32,2048]{1,0:T(8,128)S(1)}, u32[]{:S(2)}, u32[]{:S(2)}) collective-permute-start(f32[32,2048]{1,0:T(8,128)S(1)} %solve_pat.1.raw_ref.own_ref), channel_id=1, source_target_pairs={{0,2},{2,0},{1,3},{3,1},{4,6},{6,4},{5,7},{7,5},{8,10},{10,8},{9,1... | collective-permute-start | bytes 786440 | tf_op jit(solution)/shard_map/ppermute | solution.py:248
  30.5 9.0 %collective-permute-start.8 = (f32[32,1152]{1,0:T(8,128)S(1)}, f32[32,1152]{1,0:T(8,128)S(1)}, u32[]{:S(2)}, u32[]{:S(2)}) collective-permute-start(f32[32,1152]{1,0:T(8,128)S(1)} %weigh_other.1.a_ref), channel_id=1, source_target_pairs={{0,12},{4,8},{8,4},{12,0},{16,28},{20,24},{24,20},{28,16},{32,44},... | collective-permute-start | bytes 442376 | tf_op jit(solution)/shard_map/ppermute | solution.py:254
  33.0 6.7 %collective-permute-start.7 = (f32[32,1152]{1,0:T(8,128)S(1)}, f32[32,1152]{1,0:T(8,128)S(1)}, u32[]{:S(2)}, u32[]{:S(2)}) collective-permute-start(f32[32,1152]{1,0:T(8,128)S(1)} %weigh_other.1.a_ref), channel_id=1, source_target_pairs={{0,8},{4,12},{8,0},{12,4},{16,24},{20,28},{24,16},{28,20},{32,40},... | collective-permute-start | bytes 442376 | tf_op jit(solution)/shard_map/ppermute | solution.py:254
  33.6 7.1 %collective-permute-start.6 = (f32[32,1152]{1,0:T(8,128)S(1)}, f32[32,1152]{1,0:T(8,128)S(1)}, u32[]{:S(2)}, u32[]{:S(2)}) collective-permute-start(f32[32,1152]{1,0:T(8,128)S(1)} %weigh_other.1.a_ref), channel_id=1, source_target_pairs={{0,4},{4,0},{8,12},{12,8},{16,20},{20,16},{24,28},{28,24},{32,36},... | collective-permute-start | bytes 442376 | tf_op jit(solution)/shard_map/ppermute | solution.py:254
  40.7 8.9 %collective-permute-start.11 = (f32[32,1152]{1,0:T(8,128)S(1)}, f32[32,1152]{1,0:T(8,128)S(1)}, u32[]{:S(2)}, u32[]{:S(2)}) collective-permute-start(f32[32,1152]{1,0:T(8,128)S(1)} %add_x.1.a_ref), channel_id=1, source_target_pairs={{0,96},{4,100},{8,104},{12,108},{16,112},{20,116},{24,120},{28,124... | collective-permute-start | bytes 442376 | tf_op jit(solution)/shard_map/ppermute | solution.py:254
  43.6 6.1 %collective-permute-start.10 = (f32[32,1152]{1,0:T(8,128)S(1)}, f32[32,1152]{1,0:T(8,128)S(1)}, u32[]{:S(2)}, u32[]{:S(2)}) collective-permute-start(f32[32,1152]{1,0:T(8,128)S(1)} %add_x.1.a_ref), channel_id=1, source_target_pairs={{0,64},{4,68},{8,72},{12,76},{16,80},{20,84},{24,88},{28,92},{32,9... | collective-permute-start | bytes 442376 | tf_op jit(solution)/shard_map/ppermute | solution.py:254
  43.9 6.2 %collective-permute-start.9 = (f32[32,1152]{1,0:T(8,128)S(1)}, f32[32,1152]{1,0:T(8,128)S(1)}, u32[]{:S(2)}, u32[]{:S(2)}) collective-permute-start(f32[32,1152]{1,0:T(8,128)S(1)} %add_x.1.a_ref), channel_id=1, source_target_pairs={{0,32},{4,36},{8,40},{12,44},{16,48},{20,52},{24,56},{28,60},{32,0... | collective-permute-start | bytes 442376 | tf_op jit(solution)/shard_map/ppermute | solution.py:254
  50.7 9.0 %collective-permute-start.12 = (f32[32,1152]{1,0:T(8,128)S(1)}, f32[32,1152]{1,0:T(8,128)S(1)}, u32[]{:S(2)}, u32[]{:S(2)}) collective-permute-start(f32[32,1152]{1,0:T(8,128)S(1)} %get-tuple-element.30.refs_0_), channel_id=1, source_target_pairs={{0,16},{4,20},{8,24},{12,28},{16,0},{20,4},{24,8},{28,12},{32,48},... | collective-permute-start | bytes 442376 | tf_op jit(solution)/shard_map/ppermute | solution.py:254
  54.1 3.8 %collective-permute-start.15 = (f32[32,128]{1,0:T(8,128)S(1)}, f32[32,128]{1,0:T(8,128)S(1)}, u32[]{:S(2)}, u32[]{:S(2)}) collective-permute-start(f32[32,128]{1,0:T(8,128)S(1)} %get-tuple-element.31.refs_2_), channel_id=1, source_target_pairs={{0,17},{1,16},{4,21},{5,20},{8,25},{9,24},{12,29},{13,28},{16,1},{... | collective-permute-start | bytes 49160 | tf_op jit(solution)/shard_map/ppermute | solution.py:258
  54.6 4.5 %collective-permute-start.14 = (f32[32,128]{1,0:T(8,128)S(1)}, f32[32,128]{1,0:T(8,128)S(1)}, u32[]{:S(2)}, u32[]{:S(2)}) collective-permute-start(f32[32,128]{1,0:T(8,128)S(1)} %get-tuple-element.31.refs_2_), channel_id=1, source_target_pairs={{0,16},{4,20},{8,24},{12,28},{16,0},{20,4},{24,8},{28,12},{32,48},... | collective-permute-start | bytes 49160 | tf_op jit(solution)/shard_map/ppermute | solution.py:254
  56.6 3.0 %collective-permute-start.13 = (f32[32,128]{1,0:T(8,128)S(1)}, f32[32,128]{1,0:T(8,128)S(1)}, u32[]{:S(2)}, u32[]{:S(2)}) collective-permute-start(f32[32,128]{1,0:T(8,128)S(1)} %get-tuple-element.31.refs_2_), channel_id=1, source_target_pairs={{0,1},{1,0},{2,3},{3,2},{4,5},{5,4},{6,7},{7,6},{8,9},{9,8},{10,11... | collective-permute-start | bytes 49160 | tf_op jit(solution)/shard_map/ppermute | solution.py:251
  61.2 5.4 %collective-permute-start.16 = (f32[32,128]{1,0:T(8,128)S(1)}, f32[32,128]{1,0:T(8,128)S(1)}, u32[]{:S(2)}, u32[]{:S(2)}) collective-permute-start(f32[32,128]{1,0:T(8,128)S(1)} %get-tuple-element.34.refs_0_), channel_id=1, source_target_pairs={{0,2},{2,0},{1,3},{3,1},{4,6},{6,4},{5,7},{7,5},{8,10},{10,8},{9,1... | collective-permute-start | bytes 49160 | tf_op jit(solution)/shard_map/ppermute | solution.py:248

commit v2 on v1

v2 whole, which is shorter than its diff:
```python
import math

import jax
import jax.numpy as jnp
from jax import lax
from jax.experimental import pallas as pl
from jax.experimental.pallas import tpu as pltpu
from jax.sharding import PartitionSpec as P

f32, bf16 = jnp.float32, jnp.bfloat16
highest = lax.Precision.HIGHEST
epsilon = 1e-06
VMEM = pl.BlockSpec(memory_space=pltpu.VMEM)
HBM = pl.BlockSpec(memory_space=pltpu.HBM)
NN = (((1,), (0,)), ((), ()))
NT = (((1,), (1,)), ((), ()))
TN = (((0,), (0,)), ((), ()))
LANES = 128


def exact(a, b, dims=NN):
    return lax.dot_general(a, b, dims, precision=highest, preferred_element_type=f32)


def quick(a, b, dims=NN):
    return lax.dot_general(a, b, dims, preferred_element_type=f32)


def split(x):
    hi = x.astype(bf16)
    return hi, (x - hi.astype(f32)).astype(bf16)


def iota(shape, dim):
    return lax.broadcasted_iota(jnp.int32, shape, dim)


def one_hot_feat(feat, time):
    shape = (feat, feat * time)
    return jnp.where(lax.div(iota(shape, 1), time) == iota(shape, 0), 1.0, 0.0).astype(f32)


def one_hot_time(feat, time):
    shape = (time, feat * time)
    return jnp.where(lax.rem(iota(shape, 1), time) == iota(shape, 0), 1.0, 0.0).astype(f32)


def eliminate(tiles, group=8):
    rank = tiles[0].shape[0]
    rows = iota((rank, LANES), 0)
    for start in range(0, rank, group):
        columns = [
            jnp.broadcast_to(tiles[0][:, start + t : start + t + 1], (rank, LANES)) for t in range(group)
        ]
        for t in range(group):
            at = start + t
            column = columns[t]
            inverse = 1.0 / column[at : at + 1, :]
            here = rows == at
            for later in range(t + 1, group):
                scaled = columns[later][at : at + 1, :] * inverse
                columns[later] = jnp.where(here, scaled, columns[later] - column * scaled)
            new = []
            for tile in tiles:
                scaled = tile[at : at + 1, :] * inverse
                new.append(jnp.where(here, scaled, tile - column * scaled))
            tiles = new
    return tiles


def invert(system):
    rank = system.shape[0]
    eye = jnp.where(iota((rank, rank), 0) == iota((rank, rank), 1), 1.0, 0.0).astype(f32)
    (solved,) = eliminate([wide(jnp.concatenate([system, eye], axis=1))])
    return solved[:, rank : 2 * rank]


def wide(x, columns=LANES):
    return jnp.concatenate([x, jnp.zeros((x.shape[0], columns - x.shape[1]), f32)], axis=1)


def call(body, out_shape, name, specs, scratch=(), limit=24, flops=0, moved=0):
    return pl.pallas_call(
        body,
        out_shape=[jax.ShapeDtypeStruct(s, d) for s, d in out_shape],
        in_specs=specs,
        out_specs=[VMEM] * len(out_shape),
        scratch_shapes=list(scratch),
        compiler_params=pltpu.CompilerParams(vmem_limit_bytes=limit * 2**20),
        cost_estimate=pl.CostEstimate(flops=flops, bytes_accessed=moved, transcendentals=0),
        name=name,
    )


CHUNK = 256
DEPTH = 256
SHARES = (1280, 768)


def terms_of(hl_ref, block_ref, kept_ref, terms_ref, sems, first, build=None):
    rank = terms_ref.shape[0]
    cells, patients = kept_ref.shape
    copies = []
    for c in range(patients // CHUNK):
        start = pl.multiple_of(first + c * CHUNK, CHUNK)
        copies.append(
            pltpu.make_async_copy(
                block_ref.at[:, pl.ds(start, CHUNK)], kept_ref.at[:, pl.ds(c * CHUNK, CHUNK)], sems.at[c]
            )
        )
    for copy in copies:
        copy.start()
    if build is not None:
        build()
    for c, copy in enumerate(copies):
        copy.wait()
        total = None
        for d in range(0, cells, DEPTH):
            hi, lo = split(kept_ref[d : d + DEPTH, c * CHUNK : (c + 1) * CHUNK])
            both = quick(hl_ref[:, d : d + DEPTH], hi)
            part = both[:rank] + both[rank:] + quick(hl_ref[:rank, d : d + DEPTH], lo)
            total = part if total is None else total + part
        terms_ref[:, c * CHUNK : (c + 1) * CHUNK] = total


def factors(init):
    rank = init.shape[0] - 8
    return init[:rank, :], init[rank:, :rank]


def first_terms(half, offset, init_ref, block_ref, terms_ref, kept_ref, hl_ref, time_ref, sems):
    def build():
        feat, time = factors(init_ref[...])
        count = (feat.shape[1], time.shape[0])
        product = exact(feat, one_hot_feat(*count)) * exact(time, one_hot_time(*count), TN)
        hi, lo = split(product)
        hl_ref[...] = jnp.concatenate([hi, lo], axis=0)
        time_ref[...] = jnp.concatenate([init_ref[init_ref.shape[0] - 8 :, :]] * (time_ref.shape[1] // LANES), axis=1)

    other = 1 - lax.axis_index("feat")
    terms_of(hl_ref, block_ref, kept_ref, terms_ref, sems, other * half + offset, build)


def more_terms(mine, half, offset, hl_ref, before_ref, block_ref, terms_ref, kept_ref, sems):
    me = lax.axis_index("feat")
    terms_of(hl_ref, block_ref, kept_ref, terms_ref, sems, (me if mine else 1 - me) * half + offset)


def start_system(init_ref, core_ref, piece_ref, inverse_ref, time_gram_ref):
    rank = inverse_ref.shape[0]
    feat, time = factors(init_ref[...])
    feat_other, _ = factors(core_ref[...])
    time_other = piece_ref[rank:, :rank]
    time_gram = exact(time, time, TN) + exact(time_other, time_other, TN)
    system = (exact(feat, feat, NT) + exact(feat_other, feat_other, NT)) * time_gram
    inverse_ref[...] = invert(system)
    time_gram_ref[...] = time_gram


def add_piece(mine_ref, theirs_ref, *refs):
    out_ref = refs[-1]
    out_ref[...] = mine_ref[...] + theirs_ref[: mine_ref.shape[0], :]


def pack(square):
    return jnp.concatenate([square[i : i + 8, :] for i in range(0, 32, 8)], axis=1)


def unpack(packed):
    return jnp.concatenate([packed[:, i : i + 32] for i in range(0, 128, 32)], axis=0)


def weigh(columns, *refs):
    pairs, (*before, out_ref, gram_ref) = refs[: 2 * len(columns)], refs[2 * len(columns) :]
    rank = gram_ref.shape[0]
    total = gram = None
    for i, first in enumerate(columns):
        terms_ref, kept_ref = pairs[2 * i : 2 * i + 2]
        hi, lo = split(terms_ref[...])
        hl = jnp.concatenate([hi, lo], axis=0)
        for c in range(0, terms_ref.shape[1], DEPTH):
            kept_hi, kept_lo = split(kept_ref[:, first + c : first + c + DEPTH])
            both = quick(kept_hi, hl[:, c : c + DEPTH], NT)
            part = both[:, :rank] + both[:, rank:] + quick(kept_lo, hl[:rank, c : c + DEPTH], NT)
            total = part if total is None else total + part
        square = exact(terms_ref[...], terms_ref[...], NT)
        gram = square if gram is None else gram + square
    weighted = total.T
    if before:
        weighted, gram = weighted + before[0][...], gram + before[1][...]
    out_ref[...] = weighted
    gram_ref[...] = gram


def weigh_last(columns, *refs):
    *ins, q0, q1, q2, q3, total_ref, gram_ref = refs
    weigh(columns, *ins, total_ref, gram_ref)
    rank, cells = q0.shape[0] - 8, q0.shape[1]
    gram = wide(pack(gram_ref[...]), cells)
    me = lax.rem(lax.axis_index("pat"), 4)
    for flip, out_ref in enumerate((q0, q1, q2, q3)):
        first = pl.multiple_of(lax.bitwise_xor(me, flip) * cells, cells)
        out_ref[:rank, :] = total_ref[:, pl.ds(first, cells)]
        out_ref[rank:, :] = gram


def pair(a_ref, b_ref, *refs):
    refs[-1][...] = a_ref[...] + b_ref[...]


def hold(a_ref, first_ref, out_ref):
    out_ref[...] = a_ref[...]


def add_and_project(a_ref, b_ref, c_ref, init_ref, inverse_ref, out_ref, far_ref, tail_ref):
    total = a_ref[...] + (b_ref[...] + c_ref[...])
    cells = total.shape[1]
    rank, feat_count = init_ref.shape[0] - 8, 32
    inverse = inverse_ref[...]
    weighted = exact(inverse, total[:rank, :])
    gram = pack(exact(exact(inverse, unpack(total[rank:, :LANES])), inverse, NT))
    time_count = cells // feat_count
    _, time = factors(init_ref[...])
    spread = exact(time, one_hot_time(feat_count, time_count), TN)
    terms = pack(exact(weighted * spread, one_hot_feat(feat_count, time_count), NT))
    tails = jnp.concatenate([gram, terms], axis=1)
    out_ref[:rank, :] = weighted
    out_ref[rank:, :] = tails
    far_ref[...] = tails
    tail_ref[...] = terms


def diagonal(square):
    kept = jnp.where(iota(square.shape, 0) == iota(square.shape, 1), square, 0.0)
    return jnp.sum(kept, axis=1, keepdims=True), jnp.sum(kept, axis=0, keepdims=True)


def norms(square):
    column, row = diagonal(square)
    return 1.0 / jnp.sqrt(column + epsilon), 1.0 / jnp.sqrt(row + epsilon)


def feat_system(total_pat, own_ref, far_ref, inverse_ref, time_gram_ref, gram_ref, scaled_ref, scale_ref, solver_ref):
    gram = unpack(own_ref[:, :LANES] + far_ref[:, :LANES]) / total_pat
    column, row = norms(gram)
    pat_gram = gram * column * row
    gram_ref[...] = pat_gram
    scaled_ref[...] = inverse_ref[...] * column
    scale_ref[...] = jnp.broadcast_to(column, scale_ref.shape)
    solver_ref[...] = invert(pat_gram * time_gram_ref[...]) * row


def scale_weighted(own_ref, high_ref, scale_ref, solver_ref, out_ref):
    rank = out_ref.shape[0]
    out_ref[...] = (own_ref[:rank, :] + high_ref[:rank, :]) * scale_ref[:, :1]


def solve_feat(own_ref, far_ref, high_ref, tm_ref, weighted_ref, solver_ref, out_ref):
    rank, cells = weighted_ref.shape
    feat_count = 32
    time_count = cells // feat_count
    terms = (own_ref[:, LANES:] + tm_ref[...]) + (high_ref[rank:, LANES:] + far_ref[:, LANES:])
    raw = exact(solver_ref[...], unpack(terms))
    spread = exact(raw, one_hot_feat(feat_count, time_count))
    time_terms = exact(weighted_ref[...] * spread, one_hot_time(feat_count, time_count), NT)
    out_ref[:, :LANES] = wide(jnp.concatenate([exact(raw, raw, NT), time_terms], axis=1))
    here = lax.div(iota((rank, LANES), 1), feat_count) == lax.rem(lax.axis_index("pat"), 4)
    out_ref[:, LANES:] = jnp.where(here, jnp.concatenate([raw] * 4, axis=1), 0.0)


def solve_time(total_pat, total_feat, a_ref, b_ref, raw_ref, gram_ref, feat_ref, time_ref):
    time_count, rank = time_ref.shape
    total = a_ref[...] + b_ref[...]
    gram = total[:, :rank] / total_feat
    column, row = norms(gram)
    feat_ref[...] = raw_ref[...] * column
    system = gram_ref[...] * (gram * column * row)
    terms = total[:, rank : rank + time_count] * column
    (solved,) = eliminate([wide(jnp.concatenate([system, terms], axis=1))])
    place = jnp.where(iota((time_count, LANES), 1) == iota((time_count, LANES), 0) + rank, 1.0, 0.0).astype(f32)
    factor = exact(place, solved, NT)
    time_ref[...] = factor * (1.0 / math.sqrt(total_pat * total_feat))


def scale_pat(scaled_ref, *refs):
    *terms, out_ref, ran_ref = refs
    me = lax.axis_index("feat")
    half = out_ref.shape[1] // 2
    offset = 0
    for i, terms_ref in enumerate(terms):
        who = me if i % 2 == 0 else 1 - me
        patients = terms_ref.shape[1]
        first = pl.multiple_of(who * half + offset, CHUNK)
        out_ref[:, pl.ds(first, patients)] = exact(scaled_ref[...], terms_ref[...])
        offset += patients * (i % 2)
    ran_ref[...] = jnp.zeros(ran_ref.shape, f32)


def per_device(tensor, feat_init, time_init):
    feat_dev, time_dev, rows_dev = tensor.shape
    rank = feat_init.shape[0]
    total_pat = rows_dev * lax.axis_size("pat")
    total_feat = feat_dev * lax.axis_size("feat")
    cells, half = feat_dev * time_dev, rows_dev // 2
    flat = tensor.reshape(cells, rows_dev)
    swap = [(0, 1), (1, 0)]

    def from_core(x):
        return lax.ppermute(x, "feat", swap)

    def from_tm(x):
        return lax.ppermute(x, "tm", swap)

    def from_pat(x, flip):
        return lax.ppermute(x, "pat", [(i, i ^ flip) for i in range(lax.axis_size("pat"))])

    def from_both(x, flip):
        count = 2 * lax.axis_size("pat")
        return lax.ppermute(x, ("pat", "tm"), [(i, i ^ (2 * flip + 1)) for i in range(count)])

    square = ((rank, rank), f32)
    init = jnp.concatenate([feat_init, jnp.pad(time_init.T, ((0, 0), (0, feat_dev - rank)))], axis=0)

    def load(patients):
        return dict(flops=2 * 3 * rank * cells * patients, moved=4 * cells * patients)

    def bring(body, patients, name, *operands, more=()):
        return call(
            body, [((rank, patients), f32), ((cells, patients), f32), *more], name,
            [VMEM] * (len(operands) - 1) + [HBM], [pltpu.SemaphoreType.DMA((patients // CHUNK,))], 45, **load(patients),
        )(*operands)

    offset, before, kept, mine, theirs = 0, None, [], [], []
    for count, patients in enumerate(SHARES):
        if count == 0:
            away, kept_other, hl, time_rows = bring(
                lambda *refs: first_terms(half, 0, *refs), patients, "first_terms", init, flat,
                more=[((2 * rank, cells), bf16), ((8, patients), f32)],
            )
            arrived, init_core = lax.optimization_barrier((from_core(away), from_core(init)))
        else:
            away, kept_other = bring(
                lambda *refs, offset=offset: more_terms(False, half, offset, *refs), patients, "terms_for_core", hl, before, flat
            )
            arrived = from_core(away)
        before, kept_own = bring(
            lambda *refs, offset=offset: more_terms(True, half, offset, *refs), patients, "terms_own", hl, away, flat
        )
        mine.append(before + arrived)
        theirs.append(from_tm(jnp.concatenate([mine[0], time_rows], axis=0) if count == 0 else mine[-1]))
        kept.append((kept_own, kept_other))
        offset += patients

    packed = ((8, LANES), f32)
    payload = ((rank + 8, cells // 4), f32)
    summed = [((rank, cells), f32), square]
    few = dict(flops=2**20, moved=2**18)
    sofar, totals = (), []
    for count, patients in enumerate(SHARES):
        (total,) = call(add_piece, [((rank, patients), f32)], "add_piece", [VMEM] * 3, **few)(
            mine[count], theirs[count], *(sofar[1:] or [mine[-1]])
        )
        other = from_core(total)
        totals += [total, other]
        sofar = call(lambda *refs: weigh([0], *refs), summed, "weigh", [VMEM] * (2 + len(sofar)), **load(patients))(
            total, kept[count][0], *sofar
        )
        if count < len(SHARES) - 1:
            sofar = call(lambda *refs: weigh([0], *refs), summed, "weigh", [VMEM] * 4, **load(patients))(
                other, kept[count][1], *sofar
            )
    quarters = call(
        lambda *refs: weigh_last([0], *refs), [payload] * 4, "weigh_last", [VMEM] * 4,
        [pltpu.VMEM((rank, cells), f32), pltpu.VMEM((rank, rank), f32)], **load(patients)
    )(totals[-1], kept[-1][1], *sofar)
    inverse, time_gram = call(start_system, [square] * 2, "start_system", [VMEM] * 3, **few)(init, init_core, theirs[0])

    def over_ring(mine, third, second, first, shape, *after):
        (a,) = call(pair, [shape], "pair", [VMEM] * (2 + len(after)), **few)(mine, first, *after)
        (b,) = call(hold, [shape], "hold", [VMEM] * 2, **few)(second, a)
        return a, b, third

    a, b, c = over_ring(quarters[0], *[from_pat(quarters[i], i) for i in (1, 3, 2)], payload, inverse)
    part = a + (b + c)
    a, b, c = over_ring(part, *[from_pat(part, flip) for flip in (8, 24, 16)], payload)
    part, far_tail, tail = call(
        add_and_project, [payload, ((8, 2 * LANES), f32), packed], "add_and_project", [VMEM] * 5, **few
    )(a, b, c, init, inverse)
    far, high, tm = from_both(far_tail, 4), from_pat(part, 4), from_tm(tail)
    pat_gram, scaled, scale, solver = call(
        lambda *refs: feat_system(total_pat, *refs), [square, square, ((rank, LANES), f32), square], "feat_system", [VMEM] * 4, **few
    )(far_tail, far, inverse, time_gram)
    (weighted,) = call(scale_weighted, [((rank, cells // 4), f32)], "scale_weighted", [VMEM] * 4, **few)(
        part, high, scale, solver
    )
    double = ((rank, 2 * LANES), f32)
    (sums,) = call(solve_feat, [double], "solve_feat", [VMEM] * 6, **few)(far_tail, far, high, tm, weighted, solver)
    factor_pat, ran = call(scale_pat, [((rank, rows_dev), f32), packed], "scale_pat", [VMEM] * (1 + len(totals)), **few)(
        scaled, *totals
    )
    a, b, c = over_ring(sums, *[from_pat(sums, flip) for flip in (1, 3, 2)], double, ran)
    total = a + (b + c)
    sums, feat_raw = total[:, :LANES], total[:, LANES:]
    factor_feat, factor_time = call(
        lambda *refs: solve_time(total_pat, total_feat, *refs),
        [((rank, feat_dev), f32), ((time_dev, rank), f32)],
        "solve_time", [VMEM] * 4, **few,
    )(sums, from_core(sums), feat_raw, pat_gram)
    return (factor_pat, factor_feat, factor_time.T)


def solution(mesh):
    placed = (P("feat", "tm", "pat"), P(None, "feat"), P(None, "tm"))
    return jax.shard_map(
        per_device,
        mesh=mesh,
        in_specs=placed,
        out_specs=(P(None, "pat"), P(None, "feat"), P(None, "tm")),
        check_vma=False,
    )
```

time: 68.5 us -> 62.8 us (0.917)
  waiting for transfers between devices: 20.2 us -> 10.6 us
  Pallas kernels: 20 us -> 23.5 us
  local copies, waits for them, and re-layouts: 2.14 us -> 0.01 us
  starting transfers between devices: 25.3 us -> 26.9 us
  other arithmetic: 0.03 us -> 0.81 us
    ppermute x8 -> x10, waiting for transfers between devices: 13.9 us -> 6.72 us  [from_pat(): lax.ppermute(x, 'pat', [(i, i ^ flip) for i in range(lax.axis_size('pat'))])]
    ppermute x4 -> x3, waiting for transfers between devices: 5.79 us -> 0.01 us  [from_tm(): return lax.ppermute(x, 'tm', swap)]
    pallas_call x10 -> x22, Pallas kernels: 18.9 us -> 21.8 us  [the longest x4 11.2 us: bring(): call(body, [((rank, patients), f32), ((cells, patients), f32), *more], na...]
    ppermute x1, waiting for transfers between devices: 0.54 us -> 2.98 us  [from_both(): lax.ppermute(x, ('pat', 'tm'), [(i, i ^ 2 * flip + 1) for i in range(coun...]
    unnamed x4 -> x0, local copies, waits for them, and re-layouts: 2.14 us -> none
    ppermute x8 -> x10, starting transfers between devices: 12.3 us -> 14 us  [from_pat(): lax.ppermute(x, 'pat', [(i, i ^ flip) for i in range(lax.axis_size('pat'))])]
    ppermute x4 -> x6, waiting for transfers between devices: 0.01 us -> 0.85 us  [from_core(): return lax.ppermute(x, 'feat', swap)]
    concatenate x0 -> x2, other arithmetic: none -> 0.75 us  [the longest x1 0.74 us: per_device(): jnp.concatenate([feat_init, jnp.pad(time_init.T, ((0, 0), (0, feat_dev -...]
  transfers between devices with their start and end apart: 17 -> 20, of which waited for: 11 -> 8; matrix products, arithmetic and copies ran while one was open for 0% -> 0% of each run, Pallas kernels for 13% -> 26%
where the time goes in v2:
time: 62.8 us; the launch traced here: 62.6 us
  starting transfers between devices  26.9 us (43%)
  Pallas kernels  23.5 us (37%)
  waiting for transfers between devices  10.6 us (17%)
  other arithmetic  0.81 us (1%)
  between operations  0.8 us (1%)
    ppermute x10, starting transfers between devices, from_pat(): lax.ppermute(x, 'pat', [(i, i ^ flip) for i in range(lax.axis_size('pat'))])  14 us
    pallas_call x4, Pallas kernels, bring(): call(body, [((rank, patients), f32), ((cells, patients), f32), *more], na...  11.2 us
    ppermute x6, starting transfers between devices, from_core(): return lax.ppermute(x, 'feat', swap)  8.83 us
    ppermute x10, waiting for transfers between devices, from_pat(): lax.ppermute(x, 'pat', [(i, i ^ flip) for i in range(lax.axis_size('pat'))])  6.72 us
    ppermute x3, starting transfers between devices, from_tm(): return lax.ppermute(x, 'tm', swap)  3.58 us
    ppermute x1, waiting for transfers between devices, from_both(): lax.ppermute(x, ('pat', 'tm'), [(i, i ^ 2 * flip + 1) for i in range(coun...  2.98 us
    pallas_call x2, Pallas kernels, per_device(): call(lambda *refs: weigh([0], *refs), summed, 'weigh', [VMEM] * (2 + len(...  2.82 us
    pallas_call x1, Pallas kernels, per_device(): call(lambda *refs: solve_time(total_pat, total_feat, *refs), [((rank, fea...  1.72 us
  transfers between devices with their start and end apart: 20, of which 8 were waited for; matrix products, arithmetic and copies ran while one was open for 0% of the time, Pallas kernels for 26%

profile of v2, /device:TPU:1, one launch (start us, length us, event | category | flops | bytes accessed | tf_op | source)
XLA Modules:
  0.0 62.6 jit_solution(2723720629604136496)
XLA Ops:
  0.6 0.7 %select_maximum_fusion.refs_0_.init_ref = f32[40,128]{1,0:T(8,128)S(1)} fusion(f32[8,32]{1,0:T(8,128)} %bitcast.7, f32[32,128]{1,0:T(8,128)} %param.4), kind=kLoop, calls=%fused_computation.3 | loop fusion | flops 15360 | bytes 37888 | tf_op jit(solution)/shard_map/concatenate | solution.py:322
  1.4 3.2 %first_terms.1 = (f32[32,1280]{1,0:T(8,128)S(1)}, f32[1024,1280]{1,0:T(8,128)S(1)}, bf16[64,1024]{1,0:T(8,128)(2,1)S(1)}, f32[8,1280]{1,0:T(8,128)S(1)}) custom-call(f32[40,128]{1,0:T(8,128)S(1)} %select_maximum_fusion.refs_0_.init_ref, f32[1024,4096]{1,0:T(8,128)} %bitcast.3), custom_call_target="tpu_custom_call" | custom-call | flops 251658240 | bytes 5242880 | tf_op jit(solution)/shard_map/first_terms/pallas_call | solution.py:328
  4.6 1.5 %collective-permute-start.2 = (f32[32,1280]{1,0:T(8,128)S(1)}, f32[32,1280]{1,0:T(8,128)S(1)}, u32[]{:S(2)}, u32[]{:S(2)}) collective-permute-start(f32[32,1280]{1,0:T(8,128)S(1)} %get-tuple-element.39.refs_1_), channel_id=1, source_target_pairs={{0,2},{2,0},{1,3},{3,1},{4,6},{6,4},{5,7},{7,5},{8,10},{10,8},{9,1... | collective-permute-start | bytes 491528 | tf_op jit(solution)/shard_map/ppermute | solution.py:309
  6.1 0.1 collective-permute-start.3
  6.2 3.2 %terms_own.2 = (f32[32,1280]{1,0:T(8,128)S(1)}, f32[1024,1280]{1,0:T(8,128)S(1)}) custom-call(bf16[64,1024]{1,0:T(8,128)(2,1)S(1)} %get-tuple-element.38.refs_0_, f32[32,1280]{1,0:T(8,128)S(1)} %get-tuple-element.39.refs_1_, f32[1024,4096]{1,0:T(8,128)} %bitcast.4), custom_call_target="tpu_custom_call" | custom-call | flops 251658240 | bytes 5242880 | tf_op jit(solution)/shard_map/terms_own/pallas_call | solution.py:328
  9.4 0.0 collective-permute-done.3.core_ref
  9.4 0.0 collective-permute-done.2
  9.5 1.8 %collective-permute-start.4 = (f32[40,1280]{1,0:T(8,128)S(1)}, f32[40,1280]{1,0:T(8,128)S(1)}, u32[]{:S(2)}, u32[]{:S(2)}) collective-permute-start(f32[40,1280]{1,0:T(8,128)S(1)} %pad_maximum_fusion), channel_id=1, source_target_pairs={{0,1},{1,0},{2,3},{3,2},{4,5},{5,4},{6,7},{7,6},{8,9},{9,8},{10,11... | collective-permute-start | bytes 614408 | tf_op jit(solution)/shard_map/ppermute | solution.py:312
  11.3 2.4 %terms_for_core.1 = (f32[32,768]{1,0:T(8,128)S(1)}, f32[1024,768]{1,0:T(8,128)S(1)}) custom-call(bf16[64,1024]{1,0:T(8,128)(2,1)S(1)} %get-tuple-element.38.refs_0_, f32[32,1280]{1,0:T(8,128)S(1)} %get-tuple-element.40.refs_1_, f32[1024,4096]{1,0:T(8,128)} %bitcast.5), custom_call_target="tpu_custom_call" | custom-call | flops 150994944 | bytes 3145728 | tf_op jit(solution)/shard_map/terms_for_core/pallas_call | solution.py:328
  13.7 0.8 %collective-permute-start = (f32[32,768]{1,0:T(8,128)S(1)}, f32[32,768]{1,0:T(8,128)S(1)}, u32[]{:S(2)}, u32[]{:S(2)}) collective-permute-start(f32[32,768]{1,0:T(8,128)S(1)} %get-tuple-element.41.refs_1_), channel_id=1, source_target_pairs={{0,2},{2,0},{1,3},{3,1},{4,6},{6,4},{5,7},{7,5},{8,10},{10,8},{9,1... | collective-permute-start | bytes 294920 | tf_op jit(solution)/shard_map/ppermute | solution.py:309
  14.5 2.4 %terms_own.3 = (f32[32,768]{1,0:T(8,128)S(1)}, f32[1024,768]{1,0:T(8,128)S(1)}) custom-call(bf16[64,1024]{1,0:T(8,128)(2,1)S(1)} %get-tuple-element.38.refs_0_, f32[32,768]{1,0:T(8,128)S(1)} %get-tuple-element.41.refs_1_, f32[1024,4096]{1,0:T(8,128)} %bitcast.6), custom_call_target="tpu_custom_call" | custom-call | flops 150994944 | bytes 3145728 | tf_op jit(solution)/shard_map/terms_own/pallas_call | solution.py:328
  16.9 0.0 collective-permute-done
  16.9 0.0 collective-permute-done.4.theirs_ref.piece_ref
  16.9 0.5 collective-permute-start.5
  17.4 1.5 %collective-permute-start.1 = (f32[32,768]{1,0:T(8,128)S(1)}, f32[32,768]{1,0:T(8,128)S(1)}, u32[]{:S(2)}, u32[]{:S(2)}) collective-permute-start(f32[32,768]{1,0:T(8,128)S(1)} %add.20.refs_0_.mine_ref), channel_id=1, source_target_pairs={{0,1},{1,0},{2,3},{3,2},{4,5},{5,4},{6,7},{7,6},{8,9},{9,8},{10,11... | collective-permute-start | bytes 294920 | tf_op jit(solution)/shard_map/ppermute | solution.py:312
  18.9 1.7 %weigh.3 = (f32[32,1024]{1,0:T(8,128)S(1)}, f32[32,32]{1,0:T(8,128)S(1)}) custom-call(f32[32,1280]{1,0:T(8,128)S(1)} %add_piece.2.refs_0_, f32[1024,1280]{1,0:T(8,128)S(1)} %get-tuple-element.46.refs_1_), custom_call_target="tpu_custom_call" | custom-call | flops 251658240 | bytes 5242880 | tf_op jit(solution)/shard_map/weigh/pallas_call | solution.py:365
  20.6 0.0 collective-permute-done.5.refs_0_.refs_1_
  20.6 1.7 %weigh.4 = (f32[32,1024]{1,0:T(8,128)S(1)}, f32[32,32]{1,0:T(8,128)S(1)}) custom-call(f32[32,1280]{1,0:T(8,128)S(1)} %collective-permute-done.5.refs_0_.refs_1_, f32[1024,1280]{1,0:T(8,128)S(1)} %get-tuple-element.45.refs_1_, f32[32,1024]{1,0:T(8,128)S(1)} %get-tuple-element.47.refs_2_, f32[32,32]{1,0:T(8,128)S(1)} %get-tuple-element.48.refs_3_), custom_call_target="tpu_custom_call" | custom-call | flops 251658240 | bytes 5242880 | tf_op jit(solution)/shard_map/weigh/pallas_call | solution.py:369
  22.3 0.0 collective-permute-done.1.theirs_ref
  22.3 0.4 collective-permute-start.6
  22.8 1.1 %weigh.5 = (f32[32,1024]{1,0:T(8,128)S(1)}, f32[32,32]{1,0:T(8,128)S(1)}) custom-call(f32[32,768]{1,0:T(8,128)S(1)} %add_piece.3.refs_0_.refs_2_, f32[1024,768]{1,0:T(8,128)S(1)} %get-tuple-element.51.refs_1_, f32[32,1024]{1,0:T(8,128)S(1)} %get-tuple-element.52.refs_2_, f32[32,32]{1,0:T(8,128)S(1)} %get-tuple-element.49.refs_0_.refs_3_), custom_call_target="tpu_custom_call" | custom-call | flops 150994944 | bytes 3145728 | tf_op jit(solution)/shard_map/weigh/pallas_call | solution.py:365
  23.9 0.0 collective-permute-done.6.refs_0_.refs_3_
  23.9 1.2 %weigh_last.1 = (f32[40,256]{1,0:T(8,128)S(1)}, f32[40,256]{1,0:T(8,128)S(1)}, f32[40,256]{1,0:T(8,128)S(1)}, f32[40,256]{1,0:T(8,128)S(1)}) custom-call(f32[32,768]{1,0:T(8,128)S(1)} %collective-permute-done.6.refs_0_.refs_3_, f32[1024,768]{1,0:T(8,128)S(1)} %get-tuple-element.50.refs_1_, f32[32,1024]{1,0:T(8,128)S(1)} %get-tuple-element.53.refs_2_, ...), custom_call_target="tpu_custom_call" | custom-call | flops 150994944 | bytes 3145728 | tf_op jit(solution)/shard_map/weigh_last/pallas_call | solution.py:372
  25.1 3.0 %collective-permute-start.7 = (f32[40,256]{1,0:T(8,128)S(1)}, f32[40,256]{1,0:T(8,128)S(1)}, u32[]{:S(2)}, u32[]{:S(2)}) collective-permute-start(f32[40,256]{1,0:T(8,128)S(1)} %get-tuple-element.56), channel_id=1, source_target_pairs={{0,8},{4,12},{8,0},{12,4},{16,24},{20,28},{24,16},{28,20},{32,40},... | collective-permute-start | bytes 122888 | tf_op jit(solution)/shard_map/ppermute | solution.py:315
  28.1 0.9 %collective-permute-start.8 = (f32[40,256]{1,0:T(8,128)S(1)}, f32[40,256]{1,0:T(8,128)S(1)}, u32[]{:S(2)}, u32[]{:S(2)}) collective-permute-start(f32[40,256]{1,0:T(8,128)S(1)} %get-tuple-element.59), channel_id=1, source_target_pairs={{0,12},{4,8},{8,4},{12,0},{16,28},{20,24},{24,20},{28,16},{32,44},... | collective-permute-start | bytes 122888 | tf_op jit(solution)/shard_map/ppermute | solution.py:315
  29.0 0.0 collective-permute-start.9
  29.0 1.2 %start_system.1 = (f32[32,32]{1,0:T(8,128)S(1)}, f32[32,32]{1,0:T(8,128)S(1)}) custom-call(f32[40,128]{1,0:T(8,128)S(1)} %select_maximum_fusion.refs_0_.init_ref, f32[40,128]{1,0:T(8,128)S(1)} %collective-permute-done.3.core_ref, f32[40,1280]{1,0:T(8,128)S(1)} %collective-permute-done.4.theirs_ref.piece_ref), custom_call_target="tpu_custom_call" | custom-call | flops 1048576 | bytes 262144 | tf_op jit(solution)/shard_map/start_system/pallas_call | solution.py:376
  30.1 0.0 collective-permute-done.7.b_ref
  30.1 2.0 %collective-permute-done.8.a_ref = f32[40,256]{1,0:T(8,128)S(1)} collective-permute-done((f32[40,256]{1,0:T(8,128)S(1)}, f32[40,256]{1,0:T(8,128)S(1)}, u32[]{:S(2)}, u32[]{:S(2)}) %collective-permute-start.8) | collective-permute-done | bytes 40992 | tf_op jit(solution)/shard_map/ppermute | solution.py:315
  32.2 0.0 collective-permute-done.9
  32.2 3.0 %collective-permute-start.10 = (f32[40,256]{1,0:T(8,128)S(1)}, f32[40,256]{1,0:T(8,128)S(1)}, u32[]{:S(2)}, u32[]{:S(2)}) collective-permute-start(f32[40,256]{1,0:T(8,128)S(1)} %add_add_fusion.a_ref), channel_id=1, source_target_pairs={{0,64},{4,68},{8,72},{12,76},{16,80},{20,84},{24,88},{28,92},{32,9... | collective-permute-start | bytes 122888 | tf_op jit(solution)/shard_map/ppermute | solution.py:315
  35.2 0.8 %collective-permute-start.11 = (f32[40,256]{1,0:T(8,128)S(1)}, f32[40,256]{1,0:T(8,128)S(1)}, u32[]{:S(2)}, u32[]{:S(2)}) collective-permute-start(f32[40,256]{1,0:T(8,128)S(1)} %add_add_fusion.a_ref), channel_id=1, source_target_pairs={{0,96},{4,100},{8,104},{12,108},{16,112},{20,116},{24,120},{28,124... | collective-permute-start | bytes 122888 | tf_op jit(solution)/shard_map/ppermute | solution.py:315
  36.0 0.0 collective-permute-start.12
  36.0 0.7 %collective-permute-done.10.b_ref = f32[40,256]{1,0:T(8,128)S(1)} collective-permute-done((f32[40,256]{1,0:T(8,128)S(1)}, f32[40,256]{1,0:T(8,128)S(1)}, u32[]{:S(2)}, u32[]{:S(2)}) %collective-permute-start.10) | collective-permute-done | bytes 40992 | tf_op jit(solution)/shard_map/ppermute | solution.py:315
  36.6 2.6 %collective-permute-done.11.a_ref = f32[40,256]{1,0:T(8,128)S(1)} collective-permute-done((f32[40,256]{1,0:T(8,128)S(1)}, f32[40,256]{1,0:T(8,128)S(1)}, u32[]{:S(2)}, u32[]{:S(2)}) %collective-permute-start.11) | collective-permute-done | bytes 40992 | tf_op jit(solution)/shard_map/ppermute | solution.py:315
  39.2 0.0 collective-permute-done.12.c_ref
  39.2 0.6 add_and_project.1
  39.8 3.5 %collective-permute-start.14 = (f32[40,256]{1,0:T(8,128)S(1)}, f32[40,256]{1,0:T(8,128)S(1)}, u32[]{:S(2)}, u32[]{:S(2)}) collective-permute-start(f32[40,256]{1,0:T(8,128)S(1)} %get-tuple-element.65.own_ref), channel_id=1, source_target_pairs={{0,16},{4,20},{8,24},{12,28},{16,0},{20,4},{24,8},{28,12},{32,48},... | collective-permute-start | bytes 122888 | tf_op jit(solution)/shard_map/ppermute | solution.py:315
  43.3 0.4 collective-permute-start.13
  43.7 0.3 collective-permute-start.15
  44.0 3.0 %collective-permute-done.13.refs_1_.far_ref = f32[8,256]{1,0:T(8,128)S(1)} collective-permute-done((f32[8,256]{1,0:T(8,128)S(1)}, f32[8,256]{1,0:T(8,128)S(1)}, u32[]{:S(2)}, u32[]{:S(2)}) %collective-permute-start.13) | collective-permute-done | bytes 8224 | tf_op jit(solution)/shard_map/ppermute | solution.py:319
  47.0 1.1 %feat_system.1 = (f32[32,32]{1,0:T(8,128)S(1)}, f32[32,32]{1,0:T(8,128)S(1)}, f32[32,128]{1,0:T(8,128)S(1)}, f32[32,32]{1,0:T(8,128)S(1)}) custom-call(f32[8,256]{1,0:T(8,128)S(1)} %get-tuple-element.61.refs_0_.own_ref, f32[8,256]{1,0:T(8,128)S(1)} %collective-permute-done.13.refs_1_.far_ref, f32[32,32]{1,0:T(8,128)S(1)} %get-tuple-element.58.refs_0_.inverse_ref.refs_2_, ...), custom_call_target="tpu_custom_call" | custom-call | flops 1048576 | bytes 262144 | tf_op jit(solution)/shard_map/feat_system/pallas_call | solution.py:390
  48.1 0.0 collective-permute-done.14.high_ref
  48.1 0.1 scale_weighted.1.weighted_ref
  48.2 0.0 collective-permute-done.15.tm_ref
  48.2 0.6 %solve_feat.1.a_ref = f32[32,256]{1,0:T(8,128)S(1)} custom-call(f32[8,256]{1,0:T(8,128)S(1)} %get-tuple-element.61.refs_0_.own_ref, f32[8,256]{1,0:T(8,128)S(1)} %collective-permute-done.13.refs_1_.far_ref, f32[40,256]{1,0:T(8,128)S(1)} %collective-permute-done.14.high_ref, f32[8,128]{1,0:T(8,128)S(1)} %collective-permute-done.15.tm_ref, ...), custom_call_target="tpu_custom_call" | custom-call | flops 1048576 | bytes 262144 | tf_op jit(solution)/shard_map/solve_feat/pallas_call | solution.py:397
  48.8 1.5 %collective-permute-start.16 = (f32[32,256]{1,0:T(8,128)S(1)}, f32[32,256]{1,0:T(8,128)S(1)}, u32[]{:S(2)}, u32[]{:S(2)}) collective-permute-start(f32[32,256]{1,0:T(8,128)S(1)} %solve_feat.1.a_ref), channel_id=1, source_target_pairs={{0,8},{4,12},{8,0},{12,4},{16,24},{20,28},{24,16},{28,20},{32,40},... | collective-permute-start | bytes 98312 | tf_op jit(solution)/shard_map/ppermute | solution.py:315
  50.3 1.4 %collective-permute-start.17 = (f32[32,256]{1,0:T(8,128)S(1)}, f32[32,256]{1,0:T(8,128)S(1)}, u32[]{:S(2)}, u32[]{:S(2)}) collective-permute-start(f32[32,256]{1,0:T(8,128)S(1)} %solve_feat.1.a_ref), channel_id=1, source_target_pairs={{0,12},{4,8},{8,4},{12,0},{16,28},{20,24},{24,20},{28,16},{32,44},... | collective-permute-start | bytes 98312 | tf_op jit(solution)/shard_map/ppermute | solution.py:315
  51.7 0.0 collective-permute-start.18
  51.7 1.3 %scale_pat.1 = (f32[32,4096]{1,0:T(8,128)}, f32[8,128]{1,0:T(8,128)S(1)}) custom-call(f32[32,32]{1,0:T(8,128)S(1)} %get-tuple-element.63.scaled_ref, f32[32,1280]{1,0:T(8,128)S(1)} %add_piece.2.refs_0_, f32[32,1280]{1,0:T(8,128)S(1)} %collective-permute-done.5.refs_0_.refs_1_, f32[32,768]{1,0:T(8,128)S(1)} %add_piece.3.refs_0_.refs_2_, ...), custom_call_target="tpu_custom_call" | custom-call | flops 1048576 | bytes 262144 | tf_op jit(solution)/shard_map/scale_pat/pallas_call | solution.py:398
  53.1 0.1 collective-permute-done.16.b_ref
  53.1 1.1 %collective-permute-done.17.a_ref = f32[32,256]{1,0:T(8,128)S(1)} collective-permute-done((f32[32,256]{1,0:T(8,128)S(1)}, f32[32,256]{1,0:T(8,128)S(1)}, u32[]{:S(2)}, u32[]{:S(2)}) %collective-permute-start.17) | collective-permute-done | bytes 32800 | tf_op jit(solution)/shard_map/ppermute | solution.py:315
  54.3 0.2 collective-permute-done.18
  54.5 5.5 %collective-permute-start.19 = (f32[32,128]{1,0:T(8,128)S(1)}, f32[32,128]{1,0:T(8,128)S(1)}, u32[]{:S(2)}, u32[]{:S(2)}) collective-permute-start(f32[32,128]{1,0:T(8,128)S(1)} %get-tuple-element.74.refs_0_), channel_id=1, source_target_pairs={{0,2},{2,0},{1,3},{3,1},{4,6},{6,4},{5,7},{7,5},{8,10},{10,8},{9,1... | collective-permute-start | bytes 49160 | tf_op jit(solution)/shard_map/ppermute | solution.py:309
  60.0 0.8 %collective-permute-done.19.refs_1_ = f32[32,128]{1,0:T(8,128)S(1)} collective-permute-done((f32[32,128]{1,0:T(8,128)S(1)}, f32[32,128]{1,0:T(8,128)S(1)}, u32[]{:S(2)}, u32[]{:S(2)}) %collective-permute-start.19) | collective-permute-done | bytes 16416 | tf_op jit(solution)/shard_map/ppermute | solution.py:309
  60.9 1.7 %solve_time.1 = (f32[32,128]{1,0:T(8,128)}, f32[8,32]{1,0:T(8,128)}) custom-call(f32[32,128]{1,0:T(8,128)S(1)} %get-tuple-element.74.refs_0_, f32[32,128]{1,0:T(8,128)S(1)} %collective-permute-done.19.refs_1_, f32[32,128]{1,0:T(8,128)S(1)} %get-tuple-element.73.refs_2_, f32[32,32]{1,0:T(8,128)S(1)} %get-tuple-element.70.refs_3_), custom_call_target="tpu_custom_call" | custom-call | flops 1048576 | bytes 262144 | tf_op jit(solution)/shard_map/solve_time/pallas_call | solution.py:404
  (14 shorter events, 0.1 us)
Async XLA Ops:
  4.6 4.8 %collective-permute-start.2 = (f32[32,1280]{1,0:T(8,128)S(1)}, f32[32,1280]{1,0:T(8,128)S(1)}, u32[]{:S(2)}, u32[]{:S(2)}) collective-permute-start(f32[32,1280]{1,0:T(8,128)S(1)} %get-tuple-element.39.refs_1_), channel_id=1, source_target_pairs={{0,2},{2,0},{1,3},{3,1},{4,6},{6,4},{5,7},{7,5},{8,10},{10,8},{9,1... | collective-permute-start | bytes 491528 | tf_op jit(solution)/shard_map/ppermute | solution.py:309
  6.1 3.3 %collective-permute-start.3 = (f32[40,128]{1,0:T(8,128)S(1)}, f32[40,128]{1,0:T(8,128)S(1)}, u32[]{:S(2)}, u32[]{:S(2)}) collective-permute-start(f32[40,128]{1,0:T(8,128)S(1)} %select_maximum_fusion.refs_0_.init_ref), channel_id=1, source_target_pairs={{0,2},{2,0},{1,3},{3,1},{4,6},{6,4},{5,7},{7,5},{8,10},{10,8},{9,1... | collective-permute-start | bytes 61448 | tf_op jit(solution)/shard_map/ppermute | solution.py:309
  9.5 7.4 %collective-permute-start.4 = (f32[40,1280]{1,0:T(8,128)S(1)}, f32[40,1280]{1,0:T(8,128)S(1)}, u32[]{:S(2)}, u32[]{:S(2)}) collective-permute-start(f32[40,1280]{1,0:T(8,128)S(1)} %pad_maximum_fusion), channel_id=1, source_target_pairs={{0,1},{1,0},{2,3},{3,2},{4,5},{5,4},{6,7},{7,6},{8,9},{9,8},{10,11... | collective-permute-start | bytes 614408 | tf_op jit(solution)/shard_map/ppermute | solution.py:312
  13.7 3.2 %collective-permute-start = (f32[32,768]{1,0:T(8,128)S(1)}, f32[32,768]{1,0:T(8,128)S(1)}, u32[]{:S(2)}, u32[]{:S(2)}) collective-permute-start(f32[32,768]{1,0:T(8,128)S(1)} %get-tuple-element.41.refs_1_), channel_id=1, source_target_pairs={{0,2},{2,0},{1,3},{3,1},{4,6},{6,4},{5,7},{7,5},{8,10},{10,8},{9,1... | collective-permute-start | bytes 294920 | tf_op jit(solution)/shard_map/ppermute | solution.py:309
  16.9 3.7 %collective-permute-start.5 = (f32[32,1280]{1,0:T(8,128)S(1)}, f32[32,1280]{1,0:T(8,128)S(1)}, u32[]{:S(2)}, u32[]{:S(2)}) collective-permute-start(f32[32,1280]{1,0:T(8,128)S(1)} %add_piece.2.refs_0_), channel_id=1, source_target_pairs={{0,2},{2,0},{1,3},{3,1},{4,6},{6,4},{5,7},{7,5},{8,10},{10,8},{9,1... | collective-permute-start | bytes 491528 | tf_op jit(solution)/shard_map/ppermute | solution.py:309
  17.4 4.9 %collective-permute-start.1 = (f32[32,768]{1,0:T(8,128)S(1)}, f32[32,768]{1,0:T(8,128)S(1)}, u32[]{:S(2)}, u32[]{:S(2)}) collective-permute-start(f32[32,768]{1,0:T(8,128)S(1)} %add.20.refs_0_.mine_ref), channel_id=1, source_target_pairs={{0,1},{1,0},{2,3},{3,2},{4,5},{5,4},{6,7},{7,6},{8,9},{9,8},{10,11... | collective-permute-start | bytes 294920 | tf_op jit(solution)/shard_map/ppermute | solution.py:312
  22.3 1.6 %collective-permute-start.6 = (f32[32,768]{1,0:T(8,128)S(1)}, f32[32,768]{1,0:T(8,128)S(1)}, u32[]{:S(2)}, u32[]{:S(2)}) collective-permute-start(f32[32,768]{1,0:T(8,128)S(1)} %add_piece.3.refs_0_.refs_2_), channel_id=1, source_target_pairs={{0,2},{2,0},{1,3},{3,1},{4,6},{6,4},{5,7},{7,5},{8,10},{10,8},{9,1... | collective-permute-start | bytes 294920 | tf_op jit(solution)/shard_map/ppermute | solution.py:309
  25.1 5.0 %collective-permute-start.7 = (f32[40,256]{1,0:T(8,128)S(1)}, f32[40,256]{1,0:T(8,128)S(1)}, u32[]{:S(2)}, u32[]{:S(2)}) collective-permute-start(f32[40,256]{1,0:T(8,128)S(1)} %get-tuple-element.56), channel_id=1, source_target_pairs={{0,8},{4,12},{8,0},{12,4},{16,24},{20,28},{24,16},{28,20},{32,40},... | collective-permute-start | bytes 122888 | tf_op jit(solution)/shard_map/ppermute | solution.py:315
  28.1 4.1 %collective-permute-start.8 = (f32[40,256]{1,0:T(8,128)S(1)}, f32[40,256]{1,0:T(8,128)S(1)}, u32[]{:S(2)}, u32[]{:S(2)}) collective-permute-start(f32[40,256]{1,0:T(8,128)S(1)} %get-tuple-element.59), channel_id=1, source_target_pairs={{0,12},{4,8},{8,4},{12,0},{16,28},{20,24},{24,20},{28,16},{32,44},... | collective-permute-start | bytes 122888 | tf_op jit(solution)/shard_map/ppermute | solution.py:315
  29.0 3.2 %collective-permute-start.9 = (f32[40,256]{1,0:T(8,128)S(1)}, f32[40,256]{1,0:T(8,128)S(1)}, u32[]{:S(2)}, u32[]{:S(2)}) collective-permute-start(f32[40,256]{1,0:T(8,128)S(1)} %get-tuple-element.60), channel_id=1, source_target_pairs={{0,4},{4,0},{8,12},{12,8},{16,20},{20,16},{24,28},{28,24},{32,36},... | collective-permute-start | bytes 122888 | tf_op jit(solution)/shard_map/ppermute | solution.py:315
  32.2 4.4 %collective-permute-start.10 = (f32[40,256]{1,0:T(8,128)S(1)}, f32[40,256]{1,0:T(8,128)S(1)}, u32[]{:S(2)}, u32[]{:S(2)}) collective-permute-start(f32[40,256]{1,0:T(8,128)S(1)} %add_add_fusion.a_ref), channel_id=1, source_target_pairs={{0,64},{4,68},{8,72},{12,76},{16,80},{20,84},{24,88},{28,92},{32,9... | collective-permute-start | bytes 122888 | tf_op jit(solution)/shard_map/ppermute | solution.py:315
  35.2 4.1 %collective-permute-start.11 = (f32[40,256]{1,0:T(8,128)S(1)}, f32[40,256]{1,0:T(8,128)S(1)}, u32[]{:S(2)}, u32[]{:S(2)}) collective-permute-start(f32[40,256]{1,0:T(8,128)S(1)} %add_add_fusion.a_ref), channel_id=1, source_target_pairs={{0,96},{4,100},{8,104},{12,108},{16,112},{20,116},{24,120},{28,124... | collective-permute-start | bytes 122888 | tf_op jit(solution)/shard_map/ppermute | solution.py:315
  36.0 3.3 %collective-permute-start.12 = (f32[40,256]{1,0:T(8,128)S(1)}, f32[40,256]{1,0:T(8,128)S(1)}, u32[]{:S(2)}, u32[]{:S(2)}) collective-permute-start(f32[40,256]{1,0:T(8,128)S(1)} %add_add_fusion.a_ref), channel_id=1, source_target_pairs={{0,32},{4,36},{8,40},{12,44},{16,48},{20,52},{24,56},{28,60},{32,0... | collective-permute-start | bytes 122888 | tf_op jit(solution)/shard_map/ppermute | solution.py:315
  39.8 8.3 %collective-permute-start.14 = (f32[40,256]{1,0:T(8,128)S(1)}, f32[40,256]{1,0:T(8,128)S(1)}, u32[]{:S(2)}, u32[]{:S(2)}) collective-permute-start(f32[40,256]{1,0:T(8,128)S(1)} %get-tuple-element.65.own_ref), channel_id=1, source_target_pairs={{0,16},{4,20},{8,24},{12,28},{16,0},{20,4},{24,8},{28,12},{32,48},... | collective-permute-start | bytes 122888 | tf_op jit(solution)/shard_map/ppermute | solution.py:315
  43.3 3.7 %collective-permute-start.13 = (f32[8,256]{1,0:T(8,128)S(1)}, f32[8,256]{1,0:T(8,128)S(1)}, u32[]{:S(2)}, u32[]{:S(2)}) collective-permute-start(f32[8,256]{1,0:T(8,128)S(1)} %get-tuple-element.61.refs_0_.own_ref), channel_id=1, source_target_pairs={{0,17},{1,16},{4,21},{5,20},{8,25},{9,24},{12,29},{13,28},{16,1},{... | collective-permute-start | bytes 24584 | tf_op jit(solution)/shard_map/ppermute | solution.py:319
  43.7 4.4 %collective-permute-start.15 = (f32[8,128]{1,0:T(8,128)S(1)}, f32[8,128]{1,0:T(8,128)S(1)}, u32[]{:S(2)}, u32[]{:S(2)}) collective-permute-start(f32[8,128]{1,0:T(8,128)S(1)} %get-tuple-element.66), channel_id=1, source_target_pairs={{0,1},{1,0},{2,3},{3,2},{4,5},{5,4},{6,7},{7,6},{8,9},{9,8},{10,11... | collective-permute-start | bytes 12296 | tf_op jit(solution)/shard_map/ppermute | solution.py:312
  48.8 4.3 %collective-permute-start.16 = (f32[32,256]{1,0:T(8,128)S(1)}, f32[32,256]{1,0:T(8,128)S(1)}, u32[]{:S(2)}, u32[]{:S(2)}) collective-permute-start(f32[32,256]{1,0:T(8,128)S(1)} %solve_feat.1.a_ref), channel_id=1, source_target_pairs={{0,8},{4,12},{8,0},{12,4},{16,24},{20,28},{24,16},{28,20},{32,40},... | collective-permute-start | bytes 98312 | tf_op jit(solution)/shard_map/ppermute | solution.py:315
  50.3 4.0 %collective-permute-start.17 = (f32[32,256]{1,0:T(8,128)S(1)}, f32[32,256]{1,0:T(8,128)S(1)}, u32[]{:S(2)}, u32[]{:S(2)}) collective-permute-start(f32[32,256]{1,0:T(8,128)S(1)} %solve_feat.1.a_ref), channel_id=1, source_target_pairs={{0,12},{4,8},{8,4},{12,0},{16,28},{20,24},{24,20},{28,16},{32,44},... | collective-permute-start | bytes 98312 | tf_op jit(solution)/shard_map/ppermute | solution.py:315
  51.7 2.8 %collective-permute-start.18 = (f32[32,256]{1,0:T(8,128)S(1)}, f32[32,256]{1,0:T(8,128)S(1)}, u32[]{:S(2)}, u32[]{:S(2)}) collective-permute-start(f32[32,256]{1,0:T(8,128)S(1)} %solve_feat.1.a_ref), channel_id=1, source_target_pairs={{0,4},{4,0},{8,12},{12,8},{16,20},{20,16},{24,28},{28,24},{32,36},... | collective-permute-start | bytes 98312 | tf_op jit(solution)/shard_map/ppermute | solution.py:315
  54.5 6.4 %collective-permute-start.19 = (f32[32,128]{1,0:T(8,128)S(1)}, f32[32,128]{1,0:T(8,128)S(1)}, u32[]{:S(2)}, u32[]{:S(2)}) collective-permute-start(f32[32,128]{1,0:T(8,128)S(1)} %get-tuple-element.74.refs_0_), channel_id=1, source_target_pairs={{0,2},{2,0},{1,3},{3,1},{4,6},{6,4},{5,7},{7,5},{8,10},{10,8},{9,1... | collective-permute-start | bytes 49160 | tf_op jit(solution)/shard_map/ppermute | solution.py:309

commit v3 on v2

--- a/solution.py
+++ b/solution.py
@@ -93,68 +93,70 @@
 
 
 CHUNK = 256
-DEPTH = 256
-SHARES = (1280, 768)
-
-
-def terms_of(hl_ref, block_ref, kept_ref, terms_ref, sems, first, build=None):
-    rank = terms_ref.shape[0]
-    cells, patients = kept_ref.shape
+SHARES = (1024, 1024)
+LOADS = 8
+ROOM = 45
+
+
+def terms_of(mine, half, offset, hl_ref, block_ref, terms_ref, kept_ref, sems, build=None):
+    rank, patients = terms_ref.shape
+    cells = kept_ref.shape[0]
+    me = lax.axis_index("feat")
+    first = pl.multiple_of((me if mine else 1 - me) * half + offset, CHUNK)
+    step = cells // LOADS
     copies = []
-    for c in range(patients // CHUNK):
-        start = pl.multiple_of(first + c * CHUNK, CHUNK)
+    for i in range(LOADS):
+        rows = pl.ds(i * step, step)
         copies.append(
-            pltpu.make_async_copy(
-                block_ref.at[:, pl.ds(start, CHUNK)], kept_ref.at[:, pl.ds(c * CHUNK, CHUNK)], sems.at[c]
-            )
+            pltpu.make_async_copy(block_ref.at[rows, pl.ds(first, patients)], kept_ref.at[rows, :], sems.at[i])
         )
     for copy in copies:
         copy.start()
     if build is not None:
         build()
-    for c, copy in enumerate(copies):
+    for i, copy in enumerate(copies):
         copy.wait()
-        total = None
-        for d in range(0, cells, DEPTH):
-            hi, lo = split(kept_ref[d : d + DEPTH, c * CHUNK : (c + 1) * CHUNK])
-            both = quick(hl_ref[:, d : d + DEPTH], hi)
-            part = both[:rank] + both[rank:] + quick(hl_ref[:rank, d : d + DEPTH], lo)
-            total = part if total is None else total + part
-        terms_ref[:, c * CHUNK : (c + 1) * CHUNK] = total
-
-
-def factors(init):
-    rank = init.shape[0] - 8
-    return init[:rank, :], init[rank:, :rank]
-
-
-def first_terms(half, offset, init_ref, block_ref, terms_ref, kept_ref, hl_ref, time_ref, sems):
+        rows = slice(i * step, (i + 1) * step)
+        for c in range(0, patients, CHUNK):
+            hi, lo = split(kept_ref[rows, c : c + CHUNK])
+            both = quick(hl_ref[:, rows], hi)
+            part = both[:rank] + both[rank:] + quick(hl_ref[:rank, rows], lo)
+            if i > 0:
+                part = part + terms_ref[:, c : c + CHUNK]
+            terms_ref[:, c : c + CHUNK] = part
+
+
+def first_terms(half, init_ref, block_ref, terms_ref, kept_ref, hl_ref, time_out_ref, sems):
     def build():
-        feat, time = factors(init_ref[...])
+        rank = terms_ref.shape[0]
+        feat, time = init_ref[:rank, :], init_ref[rank:, :rank]
         count = (feat.shape[1], time.shape[0])
         product = exact(feat, one_hot_feat(*count)) * exact(time, one_hot_time(*count), TN)
-        hi, lo = split(product)
-        hl_ref[...] = jnp.concatenate([hi, lo], axis=0)
-        time_ref[...] = jnp.concatenate([init_ref[init_ref.shape[0] - 8 :, :]] * (time_ref.shape[1] // LANES), axis=1)
-
-    other = 1 - lax.axis_index("feat")
-    terms_of(hl_ref, block_ref, kept_ref, terms_ref, sems, other * half + offset, build)
+        hl_ref[...] = jnp.concatenate(split(product), axis=0)
+        time_out_ref[...] = jnp.concatenate([wide(time)] * (time_out_ref.shape[1] // LANES), axis=1)
+
+    terms_of(False, half, 0, hl_ref, block_ref, terms_ref, kept_ref, sems, build)
 
 
 def more_terms(mine, half, offset, hl_ref, before_ref, block_ref, terms_ref, kept_ref, sems):
-    me = lax.axis_index("feat")
-    terms_of(hl_ref, block_ref, kept_ref, terms_ref, sems, (me if mine else 1 - me) * half + offset)
+    terms_of(mine, half, offset, hl_ref, block_ref, terms_ref, kept_ref, sems)
 
 
 def start_system(init_ref, core_ref, piece_ref, inverse_ref, time_gram_ref):
     rank = inverse_ref.shape[0]
-    feat, time = factors(init_ref[...])
-    feat_other, _ = factors(core_ref[...])
-    time_other = piece_ref[rank:, :rank]
+    feat, feat_other = init_ref[:rank, :], core_ref[:rank, :]
+    time, time_other = init_ref[rank:, :rank], piece_ref[rank:, :rank]
     time_gram = exact(time, time, TN) + exact(time_other, time_other, TN)
     system = (exact(feat, feat, NT) + exact(feat_other, feat_other, NT)) * time_gram
     inverse_ref[...] = invert(system)
     time_gram_ref[...] = time_gram
+
+
+def solve_pat(inverse_ref, *refs):
+    count = len(refs) // 2
+    for terms_ref, out_ref in zip(refs[:count], refs[count:]):
+        out_ref[...] = exact(inverse_ref[...], terms_ref[...])
+    refs[-1][...] = jnp.zeros(refs[-1].shape, f32)
 
 
 def add_piece(mine_ref, theirs_ref, *refs):
@@ -178,10 +180,10 @@
         terms_ref, kept_ref = pairs[2 * i : 2 * i + 2]
         hi, lo = split(terms_ref[...])
         hl = jnp.concatenate([hi, lo], axis=0)
-        for c in range(0, terms_ref.shape[1], DEPTH):
-            kept_hi, kept_lo = split(kept_ref[:, first + c : first + c + DEPTH])
-            both = quick(kept_hi, hl[:, c : c + DEPTH], NT)
-            part = both[:, :rank] + both[:, rank:] + quick(kept_lo, hl[:rank, c : c + DEPTH], NT)
+        for c in range(0, terms_ref.shape[1], CHUNK):
+            kept_hi, kept_lo = split(kept_ref[:, first + c : first + c + CHUNK])
+            both = quick(kept_hi, hl[:, c : c + CHUNK], NT)
+            part = both[:, :rank] + both[:, rank:] + quick(kept_lo, hl[:rank, c : c + CHUNK], NT)
             total = part if total is None else total + part
         square = exact(terms_ref[...], terms_ref[...], NT)
         gram = square if gram is None else gram + square
@@ -212,21 +214,19 @@
     out_ref[...] = a_ref[...]
 
 
-def add_and_project(a_ref, b_ref, c_ref, init_ref, inverse_ref, out_ref, far_ref, tail_ref):
+def add_and_project(a_ref, b_ref, c_ref, time_ref, inverse_ref, out_ref, tail_ref):
     total = a_ref[...] + (b_ref[...] + c_ref[...])
     cells = total.shape[1]
-    rank, feat_count = init_ref.shape[0] - 8, 32
+    rank, feat_count = inverse_ref.shape[0], 32
     inverse = inverse_ref[...]
     weighted = exact(inverse, total[:rank, :])
     gram = pack(exact(exact(inverse, unpack(total[rank:, :LANES])), inverse, NT))
     time_count = cells // feat_count
-    _, time = factors(init_ref[...])
+    time = time_ref[:, :rank]
     spread = exact(time, one_hot_time(feat_count, time_count), TN)
     terms = pack(exact(weighted * spread, one_hot_feat(feat_count, time_count), NT))
-    tails = jnp.concatenate([gram, terms], axis=1)
     out_ref[:rank, :] = weighted
-    out_ref[rank:, :] = tails
-    far_ref[...] = tails
+    out_ref[rank:, :] = jnp.concatenate([gram, terms], axis=1)
     tail_ref[...] = terms
 
 
@@ -240,12 +240,12 @@
     return 1.0 / jnp.sqrt(column + epsilon), 1.0 / jnp.sqrt(row + epsilon)
 
 
-def feat_system(total_pat, own_ref, far_ref, inverse_ref, time_gram_ref, gram_ref, scaled_ref, scale_ref, solver_ref):
-    gram = unpack(own_ref[:, :LANES] + far_ref[:, :LANES]) / total_pat
+def feat_system(total_pat, own_ref, far_ref, time_gram_ref, gram_ref, scale_ref, solver_ref):
+    rank = gram_ref.shape[0]
+    gram = unpack(own_ref[rank:, :LANES] + far_ref[rank:, :LANES]) / total_pat
     column, row = norms(gram)
     pat_gram = gram * column * row
     gram_ref[...] = pat_gram
-    scaled_ref[...] = inverse_ref[...] * column
     scale_ref[...] = jnp.broadcast_to(column, scale_ref.shape)
     solver_ref[...] = invert(pat_gram * time_gram_ref[...]) * row
 
@@ -259,7 +259,7 @@
     rank, cells = weighted_ref.shape
     feat_count = 32
     time_count = cells // feat_count
-    terms = (own_ref[:, LANES:] + tm_ref[...]) + (high_ref[rank:, LANES:] + far_ref[:, LANES:])
+    terms = (own_ref[rank:, LANES:] + tm_ref[...]) + (high_ref[rank:, LANES:] + far_ref[rank:, LANES:])
     raw = exact(solver_ref[...], unpack(terms))
     spread = exact(raw, one_hot_feat(feat_count, time_count))
     time_terms = exact(weighted_ref[...] * spread, one_hot_time(feat_count, time_count), NT)
@@ -282,16 +282,16 @@
     time_ref[...] = factor * (1.0 / math.sqrt(total_pat * total_feat))
 
 
-def scale_pat(scaled_ref, *refs):
-    *terms, out_ref, ran_ref = refs
+def scale_pat(scale_ref, *refs):
+    *raws, out_ref, ran_ref = refs
     me = lax.axis_index("feat")
     half = out_ref.shape[1] // 2
     offset = 0
-    for i, terms_ref in enumerate(terms):
+    for i, raw_ref in enumerate(raws):
         who = me if i % 2 == 0 else 1 - me
-        patients = terms_ref.shape[1]
+        patients = raw_ref.shape[1]
         first = pl.multiple_of(who * half + offset, CHUNK)
-        out_ref[:, pl.ds(first, patients)] = exact(scaled_ref[...], terms_ref[...])
+        out_ref[:, pl.ds(first, patients)] = raw_ref[...] * scale_ref[:, :1]
         offset += patients * (i % 2)
     ran_ref[...] = jnp.zeros(ran_ref.shape, f32)
 
@@ -319,37 +319,32 @@
         return lax.ppermute(x, ("pat", "tm"), [(i, i ^ (2 * flip + 1)) for i in range(count)])
 
     square = ((rank, rank), f32)
-    init = jnp.concatenate([feat_init, jnp.pad(time_init.T, ((0, 0), (0, feat_dev - rank)))], axis=0)
 
     def load(patients):
-        return dict(flops=2 * 3 * rank * cells * patients, moved=4 * cells * patients)
+        return dict(flops=patients, moved=patients)
 
     def bring(body, patients, name, *operands, more=()):
         return call(
             body, [((rank, patients), f32), ((cells, patients), f32), *more], name,
-            [VMEM] * (len(operands) - 1) + [HBM], [pltpu.SemaphoreType.DMA((patients // CHUNK,))], 45, **load(patients),
+            [VMEM] * (len(operands) - 1) + [HBM], [pltpu.SemaphoreType.DMA((LOADS,))], ROOM, **load(patients),
         )(*operands)
 
-    offset, before, kept, mine, theirs = 0, None, [], [], []
-    for count, patients in enumerate(SHARES):
-        if count == 0:
-            away, kept_other, hl, time_rows = bring(
-                lambda *refs: first_terms(half, 0, *refs), patients, "first_terms", init, flat,
-                more=[((2 * rank, cells), bf16), ((8, patients), f32)],
-            )
-            arrived, init_core = lax.optimization_barrier((from_core(away), from_core(init)))
-        else:
-            away, kept_other = bring(
-                lambda *refs, offset=offset: more_terms(False, half, offset, *refs), patients, "terms_for_core", hl, before, flat
-            )
-            arrived = from_core(away)
-        before, kept_own = bring(
-            lambda *refs, offset=offset: more_terms(True, half, offset, *refs), patients, "terms_own", hl, away, flat
-        )
-        mine.append(before + arrived)
-        theirs.append(from_tm(jnp.concatenate([mine[0], time_rows], axis=0) if count == 0 else mine[-1]))
-        kept.append((kept_own, kept_other))
-        offset += patients
+    init = jnp.concatenate([feat_init, jnp.pad(time_init.T, ((0, 0), (0, feat_dev - rank)))], axis=0)
+    c0, c1 = SHARES
+    away_0, kept_o0, hl, time_rows = bring(
+        lambda *refs: first_terms(half, *refs), c0, "first_terms", init, flat,
+        more=[((2 * rank, cells), bf16), ((8, c0), f32)],
+    )
+    arrived_0, init_core = lax.optimization_barrier((from_core(away_0), from_core(init)))
+    own_0, kept_m0 = bring(lambda *refs: more_terms(True, half, 0, *refs), c0, "terms_own", hl, away_0, flat)
+    mine = [own_0 + arrived_0]
+    theirs = [from_tm(jnp.concatenate([mine[0], time_rows], axis=0))]
+    away_1, kept_o1 = bring(lambda *refs: more_terms(False, half, c0, *refs), c1, "terms_for_core", hl, own_0, flat)
+    arrived_1 = from_core(away_1)
+    own_1, kept_m1 = bring(lambda *refs: more_terms(True, half, c0, *refs), c1, "terms_own", hl, away_1, flat)
+    mine.append(own_1 + arrived_1)
+    theirs.append(from_tm(mine[1]))
+    kept = [(kept_m0, kept_o0), (kept_m1, kept_o1)]
 
     packed = ((8, LANES), f32)
     payload = ((rank + 8, cells // 4), f32)
@@ -362,18 +357,20 @@
         )
         other = from_core(total)
         totals += [total, other]
-        sofar = call(lambda *refs: weigh([0], *refs), summed, "weigh", [VMEM] * (2 + len(sofar)), **load(patients))(
+        sofar = call(lambda *refs: weigh([0], *refs), summed, "weigh", [VMEM] * (2 + len(sofar)), **dict(flops=10 * 6 * rank * cells * patients, moved=40 * cells * patients))(
             total, kept[count][0], *sofar
         )
         if count < len(SHARES) - 1:
-            sofar = call(lambda *refs: weigh([0], *refs), summed, "weigh", [VMEM] * 4, **load(patients))(
+            sofar = call(lambda *refs: weigh([0], *refs), summed, "weigh", [VMEM] * 4, **dict(flops=10 * 6 * rank * cells * patients, moved=40 * cells * patients))(
                 other, kept[count][1], *sofar
             )
     quarters = call(
         lambda *refs: weigh_last([0], *refs), [payload] * 4, "weigh_last", [VMEM] * 4,
-        [pltpu.VMEM((rank, cells), f32), pltpu.VMEM((rank, rank), f32)], **load(patients)
+        [pltpu.VMEM((rank, cells), f32), pltpu.VMEM((rank, rank), f32)], **dict(flops=10 * 6 * rank * cells * patients, moved=40 * cells * patients)
     )(totals[-1], kept[-1][1], *sofar)
-    inverse, time_gram = call(start_system, [square] * 2, "start_system", [VMEM] * 3, **few)(init, init_core, theirs[0])
+    inverse, time_gram = call(start_system, [square] * 2, "start_system", [VMEM] * 3, **few)(
+        init, init_core, theirs[0]
+    )
 
     def over_ring(mine, third, second, first, shape, *after):
         (a,) = call(pair, [shape], "pair", [VMEM] * (2 + len(after)), **few)(mine, first, *after)
@@ -382,21 +379,21 @@
 
     a, b, c = over_ring(quarters[0], *[from_pat(quarters[i], i) for i in (1, 3, 2)], payload, inverse)
     part = a + (b + c)
-    a, b, c = over_ring(part, *[from_pat(part, flip) for flip in (8, 24, 16)], payload)
-    part, far_tail, tail = call(
-        add_and_project, [payload, ((8, 2 * LANES), f32), packed], "add_and_project", [VMEM] * 5, **few
-    )(a, b, c, init, inverse)
-    far, high, tm = from_both(far_tail, 4), from_pat(part, 4), from_tm(tail)
-    pat_gram, scaled, scale, solver = call(
-        lambda *refs: feat_system(total_pat, *refs), [square, square, ((rank, LANES), f32), square], "feat_system", [VMEM] * 4, **few
-    )(far_tail, far, inverse, time_gram)
+    raws = [((rank, x.shape[1]), f32) for x in totals]
+    *raws, solved = call(solve_pat, raws + [packed], "solve_pat", [VMEM] * (1 + len(totals)), **few)(inverse, *totals)
+    a, b, c = over_ring(part, *[from_pat(part, flip) for flip in (8, 24, 16)], payload, solved)
+    part, tail = call(add_and_project, [payload, packed], "add_and_project", [VMEM] * 5, **few)(a, b, c, time_rows, inverse)
+    far, high, tm = from_both(part, 4), from_pat(part, 4), from_tm(tail)
+    pat_gram, scale, solver = call(
+        lambda *refs: feat_system(total_pat, *refs), [square, ((rank, LANES), f32), square], "feat_system", [VMEM] * 3, **few
+    )(part, far, time_gram)
     (weighted,) = call(scale_weighted, [((rank, cells // 4), f32)], "scale_weighted", [VMEM] * 4, **few)(
         part, high, scale, solver
     )
     double = ((rank, 2 * LANES), f32)
-    (sums,) = call(solve_feat, [double], "solve_feat", [VMEM] * 6, **few)(far_tail, far, high, tm, weighted, solver)
-    factor_pat, ran = call(scale_pat, [((rank, rows_dev), f32), packed], "scale_pat", [VMEM] * (1 + len(totals)), **few)(
-        scaled, *totals
+    (sums,) = call(solve_feat, [double], "solve_feat", [VMEM] * 6, **few)(part, far, high, tm, weighted, solver)
+    factor_pat, ran = call(scale_pat, [((rank, rows_dev), f32), packed], "scale_pat", [VMEM] * (1 + len(raws)), **few)(
+        scale, *raws
     )
     a, b, c = over_ring(sums, *[from_pat(sums, flip) for flip in (1, 3, 2)], double, ran)
     total = a + (b + c)

time: 62.8 us -> 60.5 us (0.963)
  starting transfers between devices: 26.9 us -> 24.7 us
  Pallas kernels: 23.5 us -> 22.5 us
  waiting for transfers between devices: 10.6 us -> 11.5 us
    ppermute x10, starting transfers between devices: 14 us -> 11.5 us  [from_pat(): lax.ppermute(x, 'pat', [(i, i ^ flip) for i in range(lax.axis_size('pat'))])]
    ppermute x1, waiting for transfers between devices: 2.98 us -> 0.74 us  [from_both(): lax.ppermute(x, ('pat', 'tm'), [(i, i ^ 2 * flip + 1) for i in range(coun...]
    ppermute x1, starting transfers between devices: 0.42 us -> 2.32 us  [from_both(): lax.ppermute(x, ('pat', 'tm'), [(i, i ^ 2 * flip + 1) for i in range(coun...]
    ppermute x3, waiting for transfers between devices: 0.01 us -> 1.87 us  [from_tm(): return lax.ppermute(x, 'tm', swap)]
    ppermute x3, starting transfers between devices: 3.58 us -> 1.89 us  [from_tm(): return lax.ppermute(x, 'tm', swap)]
    pallas_call x4, Pallas kernels: 11.2 us -> 9.75 us  [bring(): call(body, [((rank, patients), f32), ((cells, patients), f32), *more], na...]
    ppermute x10, waiting for transfers between devices: 6.72 us -> 8.01 us  [from_pat(): lax.ppermute(x, 'pat', [(i, i ^ flip) for i in range(lax.axis_size('pat'))])]
    pallas_call x3 -> x4, Pallas kernels: 3.33 us -> 3.68 us  [the longest x1 1.52 us: per_device(): call(lambda *refs: weigh([0], *refs), summed, 'weigh', [VMEM] * 4, **dict...]
  transfers between devices with their start and end apart: 20 -> 20, of which waited for: 8 -> 10; matrix products, arithmetic and copies ran while one was open for 0% -> 0% of each run, Pallas kernels for 26% -> 26%
where the time goes in v3:
time: 60.5 us; the launch traced here: 60.3 us
  starting transfers between devices  24.7 us (41%)
  Pallas kernels  22.5 us (37%)
  waiting for transfers between devices  11.5 us (19%)
  other arithmetic  0.81 us (1%)
  between operations  0.78 us (1%)
    ppermute x10, starting transfers between devices, from_pat(): lax.ppermute(x, 'pat', [(i, i ^ flip) for i in range(lax.axis_size('pat'))])  11.5 us
    pallas_call x4, Pallas kernels, bring(): call(body, [((rank, patients), f32), ((cells, patients), f32), *more], na...  9.75 us
    ppermute x6, starting transfers between devices, from_core(): return lax.ppermute(x, 'feat', swap)  9.05 us
    ppermute x10, waiting for transfers between devices, from_pat(): lax.ppermute(x, 'pat', [(i, i ^ flip) for i in range(lax.axis_size('pat'))])  8.01 us
    pallas_call x2, Pallas kernels, per_device(): call(lambda *refs: weigh([0], *refs), summed, 'weigh', [VMEM] * (2 + len(...  2.9 us
    ppermute x1, starting transfers between devices, from_both(): lax.ppermute(x, ('pat', 'tm'), [(i, i ^ 2 * flip + 1) for i in range(coun...  2.32 us
    ppermute x3, starting transfers between devices, from_tm(): return lax.ppermute(x, 'tm', swap)  1.89 us
    ppermute x3, waiting for transfers between devices, from_tm(): return lax.ppermute(x, 'tm', swap)  1.87 us
  transfers between devices with their start and end apart: 20, of which 10 were waited for; matrix products, arithmetic and copies ran while one was open for 0% of the time, Pallas kernels for 26%

profile of v3, /device:TPU:1, one launch (start us, length us, event | category | flops | bytes accessed | tf_op | source)
XLA Modules:
  0.0 60.3 jit_solution(12792367246618435683)
XLA Ops:
  0.6 0.7 %select_maximum_fusion.refs_0_.init_ref = f32[40,128]{1,0:T(8,128)S(1)} fusion(f32[8,32]{1,0:T(8,128)} %bitcast.7, f32[32,128]{1,0:T(8,128)} %param.4), kind=kLoop, calls=%fused_computation.3 | loop fusion | flops 15360 | bytes 37888 | tf_op jit(solution)/shard_map/concatenate | solution.py:332
  1.4 2.4 %first_terms.1 = (f32[32,1024]{1,0:T(8,128)S(1)}, f32[1024,1024]{1,0:T(8,128)S(1)}, bf16[64,1024]{1,0:T(8,128)(2,1)S(1)}, f32[8,1024]{1,0:T(8,128)S(1)}) custom-call(f32[40,128]{1,0:T(8,128)S(1)} %select_maximum_fusion.refs_0_.init_ref, f32[1024,4096]{1,0:T(8,128)} %bitcast.3), custom_call_target="tpu_custom_call" | custom-call | flops 1024 | bytes 1024 | tf_op jit(solution)/shard_map/first_terms/pallas_call | solution.py:327
  3.8 1.5 %collective-permute-start.2 = (f32[32,1024]{1,0:T(8,128)S(1)}, f32[32,1024]{1,0:T(8,128)S(1)}, u32[]{:S(2)}, u32[]{:S(2)}) collective-permute-start(f32[32,1024]{1,0:T(8,128)S(1)} %get-tuple-element.42.refs_1_), channel_id=1, source_target_pairs={{0,2},{2,0},{1,3},{3,1},{4,6},{6,4},{5,7},{7,5},{8,10},{10,8},{9,1... | collective-permute-start | bytes 393224 | tf_op jit(solution)/shard_map/ppermute | solution.py:309
  5.3 0.1 collective-permute-start.3
  5.4 2.4 %terms_own.2 = (f32[32,1024]{1,0:T(8,128)S(1)}, f32[1024,1024]{1,0:T(8,128)S(1)}) custom-call(bf16[64,1024]{1,0:T(8,128)(2,1)S(1)} %get-tuple-element.41.refs_0_, f32[32,1024]{1,0:T(8,128)S(1)} %get-tuple-element.42.refs_1_, f32[1024,4096]{1,0:T(8,128)} %bitcast.4), custom_call_target="tpu_custom_call" | custom-call | flops 1024 | bytes 1024 | tf_op jit(solution)/shard_map/terms_own/pallas_call | solution.py:327
  7.9 0.0 collective-permute-done.3.core_ref
  7.9 0.0 collective-permute-done.2
  7.9 1.8 %collective-permute-start.4 = (f32[40,1024]{1,0:T(8,128)S(1)}, f32[40,1024]{1,0:T(8,128)S(1)}, u32[]{:S(2)}, u32[]{:S(2)}) collective-permute-start(f32[40,1024]{1,0:T(8,128)S(1)} %pad_maximum_fusion), channel_id=1, source_target_pairs={{0,1},{1,0},{2,3},{3,2},{4,5},{5,4},{6,7},{7,6},{8,9},{9,8},{10,11... | collective-permute-start | bytes 491528 | tf_op jit(solution)/shard_map/ppermute | solution.py:312
  9.7 2.4 %terms_for_core.1 = (f32[32,1024]{1,0:T(8,128)S(1)}, f32[1024,1024]{1,0:T(8,128)S(1)}) custom-call(bf16[64,1024]{1,0:T(8,128)(2,1)S(1)} %get-tuple-element.41.refs_0_, f32[32,1024]{1,0:T(8,128)S(1)} %get-tuple-element.43.refs_1_, f32[1024,4096]{1,0:T(8,128)} %bitcast.5), custom_call_target="tpu_custom_call" | custom-call | flops 1024 | bytes 1024 | tf_op jit(solution)/shard_map/terms_for_core/pallas_call | solution.py:327
  12.2 0.8 %collective-permute-start = (f32[32,1024]{1,0:T(8,128)S(1)}, f32[32,1024]{1,0:T(8,128)S(1)}, u32[]{:S(2)}, u32[]{:S(2)}) collective-permute-start(f32[32,1024]{1,0:T(8,128)S(1)} %get-tuple-element.44.refs_1_), channel_id=1, source_target_pairs={{0,2},{2,0},{1,3},{3,1},{4,6},{6,4},{5,7},{7,5},{8,10},{10,8},{9,1... | collective-permute-start | bytes 393224 | tf_op jit(solution)/shard_map/ppermute | solution.py:309
  12.9 2.4 %terms_own.3 = (f32[32,1024]{1,0:T(8,128)S(1)}, f32[1024,1024]{1,0:T(8,128)S(1)}) custom-call(bf16[64,1024]{1,0:T(8,128)(2,1)S(1)} %get-tuple-element.41.refs_0_, f32[32,1024]{1,0:T(8,128)S(1)} %get-tuple-element.44.refs_1_, f32[1024,4096]{1,0:T(8,128)} %bitcast.6), custom_call_target="tpu_custom_call" | custom-call | flops 1024 | bytes 1024 | tf_op jit(solution)/shard_map/terms_own/pallas_call | solution.py:327
  15.4 0.0 collective-permute-done
  15.4 0.1 collective-permute-start.1
  15.5 0.0 collective-permute-done.4.theirs_ref.piece_ref
  15.6 0.2 collective-permute-start.5
  15.7 1.5 %weigh.3 = (f32[32,1024]{1,0:T(8,128)S(1)}, f32[32,32]{1,0:T(8,128)S(1)}) custom-call(f32[32,1024]{1,0:T(8,128)S(1)} %add_piece.2.refs_0_, f32[1024,1024]{1,0:T(8,128)S(1)} %get-tuple-element.49.refs_1_), custom_call_target="tpu_custom_call" | custom-call | flops 2013265920 | bytes 41943040 | tf_op jit(solution)/shard_map/weigh/pallas_call | solution.py:360
  17.2 0.0 collective-permute-done.5.refs_0_.refs_1_
  17.2 1.5 %weigh.4 = (f32[32,1024]{1,0:T(8,128)S(1)}, f32[32,32]{1,0:T(8,128)S(1)}) custom-call(f32[32,1024]{1,0:T(8,128)S(1)} %collective-permute-done.5.refs_0_.refs_1_, f32[1024,1024]{1,0:T(8,128)S(1)} %get-tuple-element.48.refs_1_, f32[32,1024]{1,0:T(8,128)S(1)} %get-tuple-element.50.refs_2_, f32[32,32]{1,0:T(8,128)S(1)} %get-tuple-element.51.refs_3_), custom_call_target="tpu_custom_call" | custom-call | flops 2013265920 | bytes 41943040 | tf_op jit(solution)/shard_map/weigh/pallas_call | solution.py:364
  18.7 1.9 %collective-permute-done.1.theirs_ref = f32[32,1024]{1,0:T(8,128)S(1)} collective-permute-done((f32[32,1024]{1,0:T(8,128)S(1)}, f32[32,1024]{1,0:T(8,128)S(1)}, u32[]{:S(2)}, u32[]{:S(2)}) %collective-permute-start.1) | collective-permute-done | bytes 131104 | tf_op jit(solution)/shard_map/ppermute | solution.py:312
  20.6 0.9 %collective-permute-start.6 = (f32[32,1024]{1,0:T(8,128)S(1)}, f32[32,1024]{1,0:T(8,128)S(1)}, u32[]{:S(2)}, u32[]{:S(2)}) collective-permute-start(f32[32,1024]{1,0:T(8,128)S(1)} %add_piece.3.refs_0_.refs_2_), channel_id=1, source_target_pairs={{0,2},{2,0},{1,3},{3,1},{4,6},{6,4},{5,7},{7,5},{8,10},{10,8},{9,1... | collective-permute-start | bytes 393224 | tf_op jit(solution)/shard_map/ppermute | solution.py:309
  21.5 1.4 %weigh.5 = (f32[32,1024]{1,0:T(8,128)S(1)}, f32[32,32]{1,0:T(8,128)S(1)}) custom-call(f32[32,1024]{1,0:T(8,128)S(1)} %add_piece.3.refs_0_.refs_2_, f32[1024,1024]{1,0:T(8,128)S(1)} %get-tuple-element.54.refs_1_, f32[32,1024]{1,0:T(8,128)S(1)} %get-tuple-element.55.refs_2_, f32[32,32]{1,0:T(8,128)S(1)} %get-tuple-element.52.refs_0_.refs_3_), custom_call_target="tpu_custom_call" | custom-call | flops 2013265920 | bytes 41943040 | tf_op jit(solution)/shard_map/weigh/pallas_call | solution.py:360
  22.9 0.0 collective-permute-done.6.refs_0_.refs_3_
  22.9 1.6 %weigh_last.1 = (f32[40,256]{1,0:T(8,128)S(1)}, f32[40,256]{1,0:T(8,128)S(1)}, f32[40,256]{1,0:T(8,128)S(1)}, f32[40,256]{1,0:T(8,128)S(1)}) custom-call(f32[32,1024]{1,0:T(8,128)S(1)} %collective-permute-done.6.refs_0_.refs_3_, f32[1024,1024]{1,0:T(8,128)S(1)} %get-tuple-element.53.refs_1_, f32[32,1024]{1,0:T(8,128)S(1)} %get-tuple-element.56.refs_2_, ...), custom_call_target="tpu_custom_call" | custom-call | flops 2013265920 | bytes 41943040 | tf_op jit(solution)/shard_map/weigh_last/pallas_call | solution.py:367
  24.5 2.8 %collective-permute-start.7 = (f32[40,256]{1,0:T(8,128)S(1)}, f32[40,256]{1,0:T(8,128)S(1)}, u32[]{:S(2)}, u32[]{:S(2)}) collective-permute-start(f32[40,256]{1,0:T(8,128)S(1)} %get-tuple-element.59), channel_id=1, source_target_pairs={{0,8},{4,12},{8,0},{12,4},{16,24},{20,28},{24,16},{28,20},{32,40},... | collective-permute-start | bytes 122888 | tf_op jit(solution)/shard_map/ppermute | solution.py:315
  27.3 0.9 %collective-permute-start.8 = (f32[40,256]{1,0:T(8,128)S(1)}, f32[40,256]{1,0:T(8,128)S(1)}, u32[]{:S(2)}, u32[]{:S(2)}) collective-permute-start(f32[40,256]{1,0:T(8,128)S(1)} %get-tuple-element.62), channel_id=1, source_target_pairs={{0,12},{4,8},{8,4},{12,0},{16,28},{20,24},{24,20},{28,16},{32,44},... | collective-permute-start | bytes 122888 | tf_op jit(solution)/shard_map/ppermute | solution.py:315
  28.2 0.0 collective-permute-start.9
  28.2 1.2 %start_system.1 = (f32[32,32]{1,0:T(8,128)S(1)}, f32[32,32]{1,0:T(8,128)S(1)}) custom-call(f32[40,128]{1,0:T(8,128)S(1)} %select_maximum_fusion.refs_0_.init_ref, f32[40,128]{1,0:T(8,128)S(1)} %collective-permute-done.3.core_ref, f32[40,1024]{1,0:T(8,128)S(1)} %collective-permute-done.4.theirs_ref.piece_ref), custom_call_target="tpu_custom_call" | custom-call | flops 1048576 | bytes 262144 | tf_op jit(solution)/shard_map/start_system/pallas_call | solution.py:371
  29.4 0.0 collective-permute-done.7.b_ref
  29.4 2.0 %collective-permute-done.8.a_ref = f32[40,256]{1,0:T(8,128)S(1)} collective-permute-done((f32[40,256]{1,0:T(8,128)S(1)}, f32[40,256]{1,0:T(8,128)S(1)}, u32[]{:S(2)}, u32[]{:S(2)}) %collective-permute-start.8) | collective-permute-done | bytes 40992 | tf_op jit(solution)/shard_map/ppermute | solution.py:315
  31.4 0.0 collective-permute-done.9
  31.4 3.2 %collective-permute-start.10 = (f32[40,256]{1,0:T(8,128)S(1)}, f32[40,256]{1,0:T(8,128)S(1)}, u32[]{:S(2)}, u32[]{:S(2)}) collective-permute-start(f32[40,256]{1,0:T(8,128)S(1)} %add_add_fusion.a_ref), channel_id=1, source_target_pairs={{0,64},{4,68},{8,72},{12,76},{16,80},{20,84},{24,88},{28,92},{32,9... | collective-permute-start | bytes 122888 | tf_op jit(solution)/shard_map/ppermute | solution.py:315
  34.6 0.8 %collective-permute-start.11 = (f32[40,256]{1,0:T(8,128)S(1)}, f32[40,256]{1,0:T(8,128)S(1)}, u32[]{:S(2)}, u32[]{:S(2)}) collective-permute-start(f32[40,256]{1,0:T(8,128)S(1)} %add_add_fusion.a_ref), channel_id=1, source_target_pairs={{0,96},{4,100},{8,104},{12,108},{16,112},{20,116},{24,120},{28,124... | collective-permute-start | bytes 122888 | tf_op jit(solution)/shard_map/ppermute | solution.py:315
  35.4 0.0 collective-permute-start.12
  35.4 0.5 solve_pat.1
  35.9 0.1 collective-permute-done.10.b_ref
  36.0 2.6 %collective-permute-done.11.a_ref = f32[40,256]{1,0:T(8,128)S(1)} collective-permute-done((f32[40,256]{1,0:T(8,128)S(1)}, f32[40,256]{1,0:T(8,128)S(1)}, u32[]{:S(2)}, u32[]{:S(2)}) %collective-permute-start.11) | collective-permute-done | bytes 40992 | tf_op jit(solution)/shard_map/ppermute | solution.py:315
  38.7 0.0 collective-permute-done.12.c_ref
  38.7 0.6 add_and_project.1
  39.2 2.3 %collective-permute-start.13 = (f32[40,256]{1,0:T(8,128)S(1)}, f32[40,256]{1,0:T(8,128)S(1)}, u32[]{:S(2)}, u32[]{:S(2)}) collective-permute-start(f32[40,256]{1,0:T(8,128)S(1)} %get-tuple-element.65.refs_0_.own_ref), channel_id=1, source_target_pairs={{0,17},{1,16},{4,21},{5,20},{8,25},{9,24},{12,29},{13,28},{16,1},{... | collective-permute-start | bytes 122888 | tf_op jit(solution)/shard_map/ppermute | solution.py:319
  41.6 1.1 %collective-permute-start.14 = (f32[40,256]{1,0:T(8,128)S(1)}, f32[40,256]{1,0:T(8,128)S(1)}, u32[]{:S(2)}, u32[]{:S(2)}) collective-permute-start(f32[40,256]{1,0:T(8,128)S(1)} %get-tuple-element.65.refs_0_.own_ref), channel_id=1, source_target_pairs={{0,16},{4,20},{8,24},{12,28},{16,0},{20,4},{24,8},{28,12},{32,48},... | collective-permute-start | bytes 122888 | tf_op jit(solution)/shard_map/ppermute | solution.py:315
  42.6 0.0 collective-permute-start.15
  42.6 0.7 %collective-permute-done.13.refs_1_.far_ref = f32[40,256]{1,0:T(8,128)S(1)} collective-permute-done((f32[40,256]{1,0:T(8,128)S(1)}, f32[40,256]{1,0:T(8,128)S(1)}, u32[]{:S(2)}, u32[]{:S(2)}) %collective-permute-start.13) | collective-permute-done | bytes 40992 | tf_op jit(solution)/shard_map/ppermute | solution.py:319
  43.4 1.1 %feat_system.1 = (f32[32,32]{1,0:T(8,128)S(1)}, f32[32,128]{1,0:T(8,128)S(1)}, f32[32,32]{1,0:T(8,128)S(1)}) custom-call(f32[40,256]{1,0:T(8,128)S(1)} %get-tuple-element.65.refs_0_.own_ref, f32[40,256]{1,0:T(8,128)S(1)} %collective-permute-done.13.refs_1_.far_ref, f32[32,32]{1,0:T(8,128)S(1)} %get-tuple-element.66.refs_2_), custom_call_target="tpu_custom_call" | custom-call | flops 1048576 | bytes 262144 | tf_op jit(solution)/shard_map/feat_system/pallas_call | solution.py:387
  44.4 1.5 %collective-permute-done.14.high_ref = f32[40,256]{1,0:T(8,128)S(1)} collective-permute-done((f32[40,256]{1,0:T(8,128)S(1)}, f32[40,256]{1,0:T(8,128)S(1)}, u32[]{:S(2)}, u32[]{:S(2)}) %collective-permute-start.14) | collective-permute-done | bytes 40992 | tf_op jit(solution)/shard_map/ppermute | solution.py:315
  45.9 0.1 scale_weighted.1.weighted_ref
  46.0 0.0 collective-permute-done.15.tm_ref
  46.0 0.6 %solve_feat.1.a_ref = f32[32,256]{1,0:T(8,128)S(1)} custom-call(f32[40,256]{1,0:T(8,128)S(1)} %get-tuple-element.65.refs_0_.own_ref, f32[40,256]{1,0:T(8,128)S(1)} %collective-permute-done.13.refs_1_.far_ref, f32[40,256]{1,0:T(8,128)S(1)} %collective-permute-done.14.high_ref, f32[8,128]{1,0:T(8,128)S(1)} %collective-permute-done.15.tm_ref, ...), custom_call_target="tpu_custom_call" | custom-call | flops 1048576 | bytes 262144 | tf_op jit(solution)/shard_map/solve_feat/pallas_call | solution.py:394
  46.6 1.3 %collective-permute-start.16 = (f32[32,256]{1,0:T(8,128)S(1)}, f32[32,256]{1,0:T(8,128)S(1)}, u32[]{:S(2)}, u32[]{:S(2)}) collective-permute-start(f32[32,256]{1,0:T(8,128)S(1)} %solve_feat.1.a_ref), channel_id=1, source_target_pairs={{0,8},{4,12},{8,0},{12,4},{16,24},{20,28},{24,16},{28,20},{32,40},... | collective-permute-start | bytes 98312 | tf_op jit(solution)/shard_map/ppermute | solution.py:315
  47.9 1.4 %collective-permute-start.17 = (f32[32,256]{1,0:T(8,128)S(1)}, f32[32,256]{1,0:T(8,128)S(1)}, u32[]{:S(2)}, u32[]{:S(2)}) collective-permute-start(f32[32,256]{1,0:T(8,128)S(1)} %solve_feat.1.a_ref), channel_id=1, source_target_pairs={{0,12},{4,8},{8,4},{12,0},{16,28},{20,24},{24,20},{28,16},{32,44},... | collective-permute-start | bytes 98312 | tf_op jit(solution)/shard_map/ppermute | solution.py:315
  49.3 0.1 collective-permute-start.18
  49.4 0.9 %scale_pat.1 = (f32[32,4096]{1,0:T(8,128)}, f32[8,128]{1,0:T(8,128)S(1)}) custom-call(f32[32,128]{1,0:T(8,128)S(1)} %get-tuple-element.67.scale_ref, f32[32,1024]{1,0:T(8,128)S(1)} %get-tuple-element.68.refs_0_, f32[32,1024]{1,0:T(8,128)S(1)} %get-tuple-element.69.refs_1_, f32[32,1024]{1,0:T(8,128)S(1)} %get-tuple-element.70.refs_2_, ...), custom_call_target="tpu_custom_call" | custom-call | flops 1048576 | bytes 262144 | tf_op jit(solution)/shard_map/scale_pat/pallas_call | solution.py:395
  50.3 0.7 %collective-permute-done.16.b_ref = f32[32,256]{1,0:T(8,128)S(1)} collective-permute-done((f32[32,256]{1,0:T(8,128)S(1)}, f32[32,256]{1,0:T(8,128)S(1)}, u32[]{:S(2)}, u32[]{:S(2)}) %collective-permute-start.16) | collective-permute-done | bytes 32800 | tf_op jit(solution)/shard_map/ppermute | solution.py:315
  51.0 0.9 %collective-permute-done.17.a_ref = f32[32,256]{1,0:T(8,128)S(1)} collective-permute-done((f32[32,256]{1,0:T(8,128)S(1)}, f32[32,256]{1,0:T(8,128)S(1)}, u32[]{:S(2)}, u32[]{:S(2)}) %collective-permute-start.17) | collective-permute-done | bytes 32800 | tf_op jit(solution)/shard_map/ppermute | solution.py:315
  51.9 0.2 collective-permute-done.18
  52.1 5.6 %collective-permute-start.19 = (f32[32,128]{1,0:T(8,128)S(1)}, f32[32,128]{1,0:T(8,128)S(1)}, u32[]{:S(2)}, u32[]{:S(2)}) collective-permute-start(f32[32,128]{1,0:T(8,128)S(1)} %get-tuple-element.80.refs_0_), channel_id=1, source_target_pairs={{0,2},{2,0},{1,3},{3,1},{4,6},{6,4},{5,7},{7,5},{8,10},{10,8},{9,1... | collective-permute-start | bytes 49160 | tf_op jit(solution)/shard_map/ppermute | solution.py:309
  57.7 0.8 %collective-permute-done.19.refs_1_ = f32[32,128]{1,0:T(8,128)S(1)} collective-permute-done((f32[32,128]{1,0:T(8,128)S(1)}, f32[32,128]{1,0:T(8,128)S(1)}, u32[]{:S(2)}, u32[]{:S(2)}) %collective-permute-start.19) | collective-permute-done | bytes 16416 | tf_op jit(solution)/shard_map/ppermute | solution.py:309
  58.5 1.7 %solve_time.1 = (f32[32,128]{1,0:T(8,128)}, f32[8,32]{1,0:T(8,128)}) custom-call(f32[32,128]{1,0:T(8,128)S(1)} %get-tuple-element.80.refs_0_, f32[32,128]{1,0:T(8,128)S(1)} %collective-permute-done.19.refs_1_, f32[32,128]{1,0:T(8,128)S(1)} %get-tuple-element.79.refs_2_, f32[32,32]{1,0:T(8,128)S(1)} %get-tuple-element.76.refs_3_), custom_call_target="tpu_custom_call" | custom-call | flops 1048576 | bytes 262144 | tf_op jit(solution)/shard_map/solve_time/pallas_call | solution.py:401
  (14 shorter events, 0.1 us)
Async XLA Ops:
  3.8 4.0 %collective-permute-start.2 = (f32[32,1024]{1,0:T(8,128)S(1)}, f32[32,1024]{1,0:T(8,128)S(1)}, u32[]{:S(2)}, u32[]{:S(2)}) collective-permute-start(f32[32,1024]{1,0:T(8,128)S(1)} %get-tuple-element.42.refs_1_), channel_id=1, source_target_pairs={{0,2},{2,0},{1,3},{3,1},{4,6},{6,4},{5,7},{7,5},{8,10},{10,8},{9,1... | collective-permute-start | bytes 393224 | tf_op jit(solution)/shard_map/ppermute | solution.py:309
  5.3 2.5 %collective-permute-start.3 = (f32[40,128]{1,0:T(8,128)S(1)}, f32[40,128]{1,0:T(8,128)S(1)}, u32[]{:S(2)}, u32[]{:S(2)}) collective-permute-start(f32[40,128]{1,0:T(8,128)S(1)} %select_maximum_fusion.refs_0_.init_ref), channel_id=1, source_target_pairs={{0,2},{2,0},{1,3},{3,1},{4,6},{6,4},{5,7},{7,5},{8,10},{10,8},{9,1... | collective-permute-start | bytes 61448 | tf_op jit(solution)/shard_map/ppermute | solution.py:309
  7.9 7.6 %collective-permute-start.4 = (f32[40,1024]{1,0:T(8,128)S(1)}, f32[40,1024]{1,0:T(8,128)S(1)}, u32[]{:S(2)}, u32[]{:S(2)}) collective-permute-start(f32[40,1024]{1,0:T(8,128)S(1)} %pad_maximum_fusion), channel_id=1, source_target_pairs={{0,1},{1,0},{2,3},{3,2},{4,5},{5,4},{6,7},{7,6},{8,9},{9,8},{10,11... | collective-permute-start | bytes 491528 | tf_op jit(solution)/shard_map/ppermute | solution.py:312
  12.2 3.2 %collective-permute-start = (f32[32,1024]{1,0:T(8,128)S(1)}, f32[32,1024]{1,0:T(8,128)S(1)}, u32[]{:S(2)}, u32[]{:S(2)}) collective-permute-start(f32[32,1024]{1,0:T(8,128)S(1)} %get-tuple-element.44.refs_1_), channel_id=1, source_target_pairs={{0,2},{2,0},{1,3},{3,1},{4,6},{6,4},{5,7},{7,5},{8,10},{10,8},{9,1... | collective-permute-start | bytes 393224 | tf_op jit(solution)/shard_map/ppermute | solution.py:309
  15.4 5.2 %collective-permute-start.1 = (f32[32,1024]{1,0:T(8,128)S(1)}, f32[32,1024]{1,0:T(8,128)S(1)}, u32[]{:S(2)}, u32[]{:S(2)}) collective-permute-start(f32[32,1024]{1,0:T(8,128)S(1)} %add.20.refs_0_.mine_ref), channel_id=1, source_target_pairs={{0,1},{1,0},{2,3},{3,2},{4,5},{5,4},{6,7},{7,6},{8,9},{9,8},{10,11... | collective-permute-start | bytes 393224 | tf_op jit(solution)/shard_map/ppermute | solution.py:312
  15.6 1.7 %collective-permute-start.5 = (f32[32,1024]{1,0:T(8,128)S(1)}, f32[32,1024]{1,0:T(8,128)S(1)}, u32[]{:S(2)}, u32[]{:S(2)}) collective-permute-start(f32[32,1024]{1,0:T(8,128)S(1)} %add_piece.2.refs_0_), channel_id=1, source_target_pairs={{0,2},{2,0},{1,3},{3,1},{4,6},{6,4},{5,7},{7,5},{8,10},{10,8},{9,1... | collective-permute-start | bytes 393224 | tf_op jit(solution)/shard_map/ppermute | solution.py:309
  20.6 2.3 %collective-permute-start.6 = (f32[32,1024]{1,0:T(8,128)S(1)}, f32[32,1024]{1,0:T(8,128)S(1)}, u32[]{:S(2)}, u32[]{:S(2)}) collective-permute-start(f32[32,1024]{1,0:T(8,128)S(1)} %add_piece.3.refs_0_.refs_2_), channel_id=1, source_target_pairs={{0,2},{2,0},{1,3},{3,1},{4,6},{6,4},{5,7},{7,5},{8,10},{10,8},{9,1... | collective-permute-start | bytes 393224 | tf_op jit(solution)/shard_map/ppermute | solution.py:309
  24.5 4.9 %collective-permute-start.7 = (f32[40,256]{1,0:T(8,128)S(1)}, f32[40,256]{1,0:T(8,128)S(1)}, u32[]{:S(2)}, u32[]{:S(2)}) collective-permute-start(f32[40,256]{1,0:T(8,128)S(1)} %get-tuple-element.59), channel_id=1, source_target_pairs={{0,8},{4,12},{8,0},{12,4},{16,24},{20,28},{24,16},{28,20},{32,40},... | collective-permute-start | bytes 122888 | tf_op jit(solution)/shard_map/ppermute | solution.py:315
  27.3 4.1 %collective-permute-start.8 = (f32[40,256]{1,0:T(8,128)S(1)}, f32[40,256]{1,0:T(8,128)S(1)}, u32[]{:S(2)}, u32[]{:S(2)}) collective-permute-start(f32[40,256]{1,0:T(8,128)S(1)} %get-tuple-element.62), channel_id=1, source_target_pairs={{0,12},{4,8},{8,4},{12,0},{16,28},{20,24},{24,20},{28,16},{32,44},... | collective-permute-start | bytes 122888 | tf_op jit(solution)/shard_map/ppermute | solution.py:315
  28.2 3.2 %collective-permute-start.9 = (f32[40,256]{1,0:T(8,128)S(1)}, f32[40,256]{1,0:T(8,128)S(1)}, u32[]{:S(2)}, u32[]{:S(2)}) collective-permute-start(f32[40,256]{1,0:T(8,128)S(1)} %get-tuple-element.63), channel_id=1, source_target_pairs={{0,4},{4,0},{8,12},{12,8},{16,20},{20,16},{24,28},{28,24},{32,36},... | collective-permute-start | bytes 122888 | tf_op jit(solution)/shard_map/ppermute | solution.py:315
  31.4 4.6 %collective-permute-start.10 = (f32[40,256]{1,0:T(8,128)S(1)}, f32[40,256]{1,0:T(8,128)S(1)}, u32[]{:S(2)}, u32[]{:S(2)}) collective-permute-start(f32[40,256]{1,0:T(8,128)S(1)} %add_add_fusion.a_ref), channel_id=1, source_target_pairs={{0,64},{4,68},{8,72},{12,76},{16,80},{20,84},{24,88},{28,92},{32,9... | collective-permute-start | bytes 122888 | tf_op jit(solution)/shard_map/ppermute | solution.py:315
  34.6 4.1 %collective-permute-start.11 = (f32[40,256]{1,0:T(8,128)S(1)}, f32[40,256]{1,0:T(8,128)S(1)}, u32[]{:S(2)}, u32[]{:S(2)}) collective-permute-start(f32[40,256]{1,0:T(8,128)S(1)} %add_add_fusion.a_ref), channel_id=1, source_target_pairs={{0,96},{4,100},{8,104},{12,108},{16,112},{20,116},{24,120},{28,124... | collective-permute-start | bytes 122888 | tf_op jit(solution)/shard_map/ppermute | solution.py:315
  35.4 3.3 %collective-permute-start.12 = (f32[40,256]{1,0:T(8,128)S(1)}, f32[40,256]{1,0:T(8,128)S(1)}, u32[]{:S(2)}, u32[]{:S(2)}) collective-permute-start(f32[40,256]{1,0:T(8,128)S(1)} %add_add_fusion.a_ref), channel_id=1, source_target_pairs={{0,32},{4,36},{8,40},{12,44},{16,48},{20,52},{24,56},{28,60},{32,0... | collective-permute-start | bytes 122888 | tf_op jit(solution)/shard_map/ppermute | solution.py:315
  39.2 4.1 %collective-permute-start.13 = (f32[40,256]{1,0:T(8,128)S(1)}, f32[40,256]{1,0:T(8,128)S(1)}, u32[]{:S(2)}, u32[]{:S(2)}) collective-permute-start(f32[40,256]{1,0:T(8,128)S(1)} %get-tuple-element.65.refs_0_.own_ref), channel_id=1, source_target_pairs={{0,17},{1,16},{4,21},{5,20},{8,25},{9,24},{12,29},{13,28},{16,1},{... | collective-permute-start | bytes 122888 | tf_op jit(solution)/shard_map/ppermute | solution.py:319
  41.6 4.4 %collective-permute-start.14 = (f32[40,256]{1,0:T(8,128)S(1)}, f32[40,256]{1,0:T(8,128)S(1)}, u32[]{:S(2)}, u32[]{:S(2)}) collective-permute-start(f32[40,256]{1,0:T(8,128)S(1)} %get-tuple-element.65.refs_0_.own_ref), channel_id=1, source_target_pairs={{0,16},{4,20},{8,24},{12,28},{16,0},{20,4},{24,8},{28,12},{32,48},... | collective-permute-start | bytes 122888 | tf_op jit(solution)/shard_map/ppermute | solution.py:315
  42.6 3.4 %collective-permute-start.15 = (f32[8,128]{1,0:T(8,128)S(1)}, f32[8,128]{1,0:T(8,128)S(1)}, u32[]{:S(2)}, u32[]{:S(2)}) collective-permute-start(f32[8,128]{1,0:T(8,128)S(1)} %get-tuple-element.73), channel_id=1, source_target_pairs={{0,1},{1,0},{2,3},{3,2},{4,5},{5,4},{6,7},{7,6},{8,9},{9,8},{10,11... | collective-permute-start | bytes 12296 | tf_op jit(solution)/shard_map/ppermute | solution.py:312
  46.6 4.3 %collective-permute-start.16 = (f32[32,256]{1,0:T(8,128)S(1)}, f32[32,256]{1,0:T(8,128)S(1)}, u32[]{:S(2)}, u32[]{:S(2)}) collective-permute-start(f32[32,256]{1,0:T(8,128)S(1)} %solve_feat.1.a_ref), channel_id=1, source_target_pairs={{0,8},{4,12},{8,0},{12,4},{16,24},{20,28},{24,16},{28,20},{32,40},... | collective-permute-start | bytes 98312 | tf_op jit(solution)/shard_map/ppermute | solution.py:315
  47.9 4.0 %collective-permute-start.17 = (f32[32,256]{1,0:T(8,128)S(1)}, f32[32,256]{1,0:T(8,128)S(1)}, u32[]{:S(2)}, u32[]{:S(2)}) collective-permute-start(f32[32,256]{1,0:T(8,128)S(1)} %solve_feat.1.a_ref), channel_id=1, source_target_pairs={{0,12},{4,8},{8,4},{12,0},{16,28},{20,24},{24,20},{28,16},{32,44},... | collective-permute-start | bytes 98312 | tf_op jit(solution)/shard_map/ppermute | solution.py:315
  49.3 2.8 %collective-permute-start.18 = (f32[32,256]{1,0:T(8,128)S(1)}, f32[32,256]{1,0:T(8,128)S(1)}, u32[]{:S(2)}, u32[]{:S(2)}) collective-permute-start(f32[32,256]{1,0:T(8,128)S(1)} %solve_feat.1.a_ref), channel_id=1, source_target_pairs={{0,4},{4,0},{8,12},{12,8},{16,20},{20,16},{24,28},{28,24},{32,36},... | collective-permute-start | bytes 98312 | tf_op jit(solution)/shard_map/ppermute | solution.py:315
  52.1 6.5 %collective-permute-start.19 = (f32[32,128]{1,0:T(8,128)S(1)}, f32[32,128]{1,0:T(8,128)S(1)}, u32[]{:S(2)}, u32[]{:S(2)}) collective-permute-start(f32[32,128]{1,0:T(8,128)S(1)} %get-tuple-element.80.refs_0_), channel_id=1, source_target_pairs={{0,2},{2,0},{1,3},{3,1},{4,6},{6,4},{5,7},{7,5},{8,10},{10,8},{9,1... | collective-permute-start | bytes 49160 | tf_op jit(solution)/shard_map/ppermute | solution.py:309

commit v4 on v3

--- a/solution.py
+++ b/solution.py
@@ -94,59 +94,75 @@
 
 CHUNK = 256
 SHARES = (1024, 1024)
-LOADS = 8
-ROOM = 45
-
-
-def terms_of(mine, half, offset, hl_ref, block_ref, terms_ref, kept_ref, sems, build=None):
-    rank, patients = terms_ref.shape
-    cells = kept_ref.shape[0]
-    me = lax.axis_index("feat")
-    first = pl.multiple_of((me if mine else 1 - me) * half + offset, CHUNK)
-    step = cells // LOADS
+LOADS = 4
+ROOM = 40
+
+
+def bring(half, mine, offset, *refs):
+    refs = list(refs)
+    sems = refs.pop() if mine is not None else None
     copies = []
-    for i in range(LOADS):
-        rows = pl.ds(i * step, step)
-        copies.append(
-            pltpu.make_async_copy(block_ref.at[rows, pl.ds(first, patients)], kept_ref.at[rows, :], sems.at[i])
-        )
+    if mine is not None:
+        build, there = {2: (False, False), 5: (False, True), 8: (True, True)}[len(refs)]
+    else:
+        build, there = False, True
+    source = refs[: 2 * build + (there and not build)]
+    refs = refs[len(source) :]
+    there_ref = refs.pop(0) if there else None
+    if mine is not None:
+        block_ref, refs = refs[0], refs[1:]
+        kept_ref = refs.pop(1 if there else 0)
+        me = lax.axis_index("feat")
+        first = pl.multiple_of((me if mine else 1 - me) * half + offset, CHUNK)
+        cells, patients = kept_ref.shape
+        step = cells // LOADS
+        for i in range(LOADS):
+            rows = pl.ds(i * step, step)
+            copies.append(
+                pltpu.make_async_copy(block_ref.at[rows, pl.ds(first, patients)], kept_ref.at[rows, :], sems.at[i])
+            )
+        for copy in copies:
+            copy.start()
+    if there:
+        terms_ref = refs[0]
+        rank, patients = terms_ref.shape
+        if build:
+            feat, time = source[0][...], source[1][...]
+            hl_ref, time_ref = refs[1:]
+            count = (feat.shape[1], time.shape[0])
+            product = exact(feat, one_hot_feat(*count)) * exact(time, one_hot_time(*count), TN)
+            hl_ref[...] = jnp.concatenate(split(product), axis=0)
+            below = jnp.zeros((rank - time.shape[0], LANES), f32)
+            time_ref[...] = jnp.concatenate([wide(time), below], axis=0)
+        else:
+            hl_ref = source[0]
+
+        def contract(columns):
+            total = None
+            for d in range(0, there_ref.shape[0], CHUNK):
+                hi, lo = split(there_ref[d : d + CHUNK, columns])
+                both = quick(hl_ref[:, d : d + CHUNK], hi)
+                part = both[:rank] + both[rank:] + quick(hl_ref[:rank, d : d + CHUNK], lo)
+                total = part if total is None else total + part
+            terms_ref[:, columns] = total
+
+        if copies:
+            @pl.loop(0, patients // CHUNK)
+            def _(c):
+                contract(pl.ds(pl.multiple_of(c * CHUNK, CHUNK), CHUNK))
+
+        else:
+            for c in range(0, patients, CHUNK):
+                contract(slice(c, c + CHUNK))
     for copy in copies:
-        copy.start()
-    if build is not None:
-        build()
-    for i, copy in enumerate(copies):
         copy.wait()
-        rows = slice(i * step, (i + 1) * step)
-        for c in range(0, patients, CHUNK):
-            hi, lo = split(kept_ref[rows, c : c + CHUNK])
-            both = quick(hl_ref[:, rows], hi)
-            part = both[:rank] + both[rank:] + quick(hl_ref[:rank, rows], lo)
-            if i > 0:
-                part = part + terms_ref[:, c : c + CHUNK]
-            terms_ref[:, c : c + CHUNK] = part
-
-
-def first_terms(half, init_ref, block_ref, terms_ref, kept_ref, hl_ref, time_out_ref, sems):
-    def build():
-        rank = terms_ref.shape[0]
-        feat, time = init_ref[:rank, :], init_ref[rank:, :rank]
-        count = (feat.shape[1], time.shape[0])
-        product = exact(feat, one_hot_feat(*count)) * exact(time, one_hot_time(*count), TN)
-        hl_ref[...] = jnp.concatenate(split(product), axis=0)
-        time_out_ref[...] = jnp.concatenate([wide(time)] * (time_out_ref.shape[1] // LANES), axis=1)
-
-    terms_of(False, half, 0, hl_ref, block_ref, terms_ref, kept_ref, sems, build)
-
-
-def more_terms(mine, half, offset, hl_ref, before_ref, block_ref, terms_ref, kept_ref, sems):
-    terms_of(mine, half, offset, hl_ref, block_ref, terms_ref, kept_ref, sems)
-
-
-def start_system(init_ref, core_ref, piece_ref, inverse_ref, time_gram_ref):
+
+
+def start_system(feat_ref, core_ref, time_ref, piece_ref, inverse_ref, time_gram_ref):
     rank = inverse_ref.shape[0]
-    feat, feat_other = init_ref[:rank, :], core_ref[:rank, :]
-    time, time_other = init_ref[rank:, :rank], piece_ref[rank:, :rank]
-    time_gram = exact(time, time, TN) + exact(time_other, time_other, TN)
+    feat, feat_other = feat_ref[...], core_ref[...]
+    time, time_other = time_ref[...], piece_ref[:, piece_ref.shape[1] - LANES :]
+    time_gram = (exact(time, time, TN) + exact(time_other, time_other, TN))[:rank, :rank]
     system = (exact(feat, feat, NT) + exact(feat_other, feat_other, NT)) * time_gram
     inverse_ref[...] = invert(system)
     time_gram_ref[...] = time_gram
@@ -161,7 +177,7 @@
 
 def add_piece(mine_ref, theirs_ref, *refs):
     out_ref = refs[-1]
-    out_ref[...] = mine_ref[...] + theirs_ref[: mine_ref.shape[0], :]
+    out_ref[...] = mine_ref[...] + theirs_ref[:, : mine_ref.shape[1]]
 
 
 def pack(square):
@@ -222,7 +238,7 @@
     weighted = exact(inverse, total[:rank, :])
     gram = pack(exact(exact(inverse, unpack(total[rank:, :LANES])), inverse, NT))
     time_count = cells // feat_count
-    time = time_ref[:, :rank]
+    time = time_ref[:time_count, :rank]
     spread = exact(time, one_hot_time(feat_count, time_count), TN)
     terms = pack(exact(weighted * spread, one_hot_feat(feat_count, time_count), NT))
     out_ref[:rank, :] = weighted
@@ -323,25 +339,28 @@
     def load(patients):
         return dict(flops=patients, moved=patients)
 
-    def bring(body, patients, name, *operands, more=()):
-        return call(
-            body, [((rank, patients), f32), ((cells, patients), f32), *more], name,
-            [VMEM] * (len(operands) - 1) + [HBM], [pltpu.SemaphoreType.DMA((LOADS,))], ROOM, **load(patients),
-        )(*operands)
-
-    init = jnp.concatenate([feat_init, jnp.pad(time_init.T, ((0, 0), (0, feat_dev - rank)))], axis=0)
+    def long(patients):
+        return dict(flops=10 * 6 * rank * cells * patients, moved=40 * cells * patients)
+
+    def step(mine, offset, after, *operands, before=0, more=()):
+        loads = [pltpu.SemaphoreType.DMA((LOADS,))] if after else []
+        outs = [((rank, before), f32)] * (before > 0) + [((cells, after), f32)] * (after > 0) + list(more)
+        specs = [VMEM] * (len(operands) - (after > 0)) + [HBM] * (after > 0)
+        return call(lambda *refs: bring(half, mine, offset, *refs), outs, "bring", specs, loads, ROOM, **load(before))(*operands)
+
+    time_rows = time_init.T
     c0, c1 = SHARES
-    away_0, kept_o0, hl, time_rows = bring(
-        lambda *refs: first_terms(half, *refs), c0, "first_terms", init, flat,
-        more=[((2 * rank, cells), bf16), ((8, c0), f32)],
-    )
-    arrived_0, init_core = lax.optimization_barrier((from_core(away_0), from_core(init)))
-    own_0, kept_m0 = bring(lambda *refs: more_terms(True, half, 0, *refs), c0, "terms_own", hl, away_0, flat)
+    (kept_o0,) = step(False, 0, c0, flat)
+    away_0, kept_m0, hl, time_rows = step(
+        True, 0, c0, feat_init, time_rows, kept_o0, flat, before=c0, more=[((2 * rank, cells), bf16), ((rank, LANES), f32)]
+    )
+    arrived_0, feat_core = lax.optimization_barrier((from_core(away_0), from_core(feat_init)))
+    own_0, kept_o1 = step(False, c0, c1, hl, kept_m0, flat, before=c0)
     mine = [own_0 + arrived_0]
-    theirs = [from_tm(jnp.concatenate([mine[0], time_rows], axis=0))]
-    away_1, kept_o1 = bring(lambda *refs: more_terms(False, half, c0, *refs), c1, "terms_for_core", hl, own_0, flat)
+    theirs = [from_tm(jnp.concatenate([mine[0], time_rows], axis=1))]
+    away_1, kept_m1 = step(True, c0, c1, hl, kept_o1, flat, before=c1)
     arrived_1 = from_core(away_1)
-    own_1, kept_m1 = bring(lambda *refs: more_terms(True, half, c0, *refs), c1, "terms_own", hl, away_1, flat)
+    (own_1,) = step(None, 0, 0, hl, kept_m1, before=c1)
     mine.append(own_1 + arrived_1)
     theirs.append(from_tm(mine[1]))
     kept = [(kept_m0, kept_o0), (kept_m1, kept_o1)]
@@ -357,19 +376,19 @@
         )
         other = from_core(total)
         totals += [total, other]
-        sofar = call(lambda *refs: weigh([0], *refs), summed, "weigh", [VMEM] * (2 + len(sofar)), **dict(flops=10 * 6 * rank * cells * patients, moved=40 * cells * patients))(
+        sofar = call(lambda *refs: weigh([0], *refs), summed, "weigh", [VMEM] * (2 + len(sofar)), **long(patients))(
             total, kept[count][0], *sofar
         )
         if count < len(SHARES) - 1:
-            sofar = call(lambda *refs: weigh([0], *refs), summed, "weigh", [VMEM] * 4, **dict(flops=10 * 6 * rank * cells * patients, moved=40 * cells * patients))(
+            sofar = call(lambda *refs: weigh([0], *refs), summed, "weigh", [VMEM] * 4, **long(patients))(
                 other, kept[count][1], *sofar
             )
     quarters = call(
         lambda *refs: weigh_last([0], *refs), [payload] * 4, "weigh_last", [VMEM] * 4,
-        [pltpu.VMEM((rank, cells), f32), pltpu.VMEM((rank, rank), f32)], **dict(flops=10 * 6 * rank * cells * patients, moved=40 * cells * patients)
+        [pltpu.VMEM((rank, cells), f32), pltpu.VMEM((rank, rank), f32)], **long(patients)
     )(totals[-1], kept[-1][1], *sofar)
-    inverse, time_gram = call(start_system, [square] * 2, "start_system", [VMEM] * 3, **few)(
-        init, init_core, theirs[0]
+    inverse, time_gram = call(start_system, [square] * 2, "start_system", [VMEM] * 4, **few)(
+        feat_init, feat_core, time_rows, theirs[0]
     )
 
     def over_ring(mine, third, second, first, shape, *after):

time: 60.5 us -> 59.7 us (0.987)
  waiting for transfers between devices: 11.5 us -> 10.5 us
  starting transfers between devices: 24.7 us -> 25.5 us
  other arithmetic: 0.81 us -> 0.06 us
    ppermute x6, starting transfers between devices: 9.05 us -> 10.1 us  [from_core(): return lax.ppermute(x, 'feat', swap)]
    ppermute x3, waiting for transfers between devices: 1.87 us -> 0.88 us  [from_tm(): return lax.ppermute(x, 'tm', swap)]
    concatenate x2 -> x1, other arithmetic: 0.75 us -> 0.01 us  [per_device(): theirs = [from_tm(jnp.concatenate([mine[0], time_rows], axis=1))]]
    pallas_call x6 -> x7, Pallas kernels: 12.4 us -> 12.6 us  [the longest x5 9.85 us: step(): call(lambda *refs: bring(half, mine, offset, *refs), outs, 'bring', specs...]
  transfers between devices with their start and end apart: 20 -> 20, of which waited for: 10 -> 11; matrix products, arithmetic and copies ran while one was open for 0% -> 0% of each run, Pallas kernels for 26% -> 23%
where the time goes in v4:
time: 59.7 us; the launch traced here: 59.6 us
  starting transfers between devices  25.5 us (43%)
  Pallas kernels  22.6 us (38%)
  waiting for transfers between devices  10.5 us (18%)
  between operations  0.81 us (1%)
    ppermute x10, starting transfers between devices, from_pat(): lax.ppermute(x, 'pat', [(i, i ^ flip) for i in range(lax.axis_size('pat'))])  11.3 us
    ppermute x6, starting transfers between devices, from_core(): return lax.ppermute(x, 'feat', swap)  10.1 us
    pallas_call x5, Pallas kernels, step(): call(lambda *refs: bring(half, mine, offset, *refs), outs, 'bring', specs...  9.85 us
    ppermute x10, waiting for transfers between devices, from_pat(): lax.ppermute(x, 'pat', [(i, i ^ flip) for i in range(lax.axis_size('pat'))])  7.96 us
    pallas_call x2, Pallas kernels, per_device(): call(lambda *refs: weigh([0], *refs), summed, 'weigh', [VMEM] * (2 + len(...  2.91 us
    ppermute x1, starting transfers between devices, from_both(): lax.ppermute(x, ('pat', 'tm'), [(i, i ^ 2 * flip + 1) for i in range(coun...  2.33 us
    ppermute x3, starting transfers between devices, from_tm(): return lax.ppermute(x, 'tm', swap)  1.89 us
    pallas_call x1, Pallas kernels, per_device(): call(lambda *refs: solve_time(total_pat, total_feat, *refs), [((rank, fea...  1.72 us
  transfers between devices with their start and end apart: 20, of which 11 were waited for; matrix products, arithmetic and copies ran while one was open for 0% of the time, Pallas kernels for 23%

profile of v4, /device:TPU:1, one launch (start us, length us, event | category | flops | bytes accessed | tf_op | source)
XLA Modules:
  0.0 59.6 jit_solution(1358488289267183756)
XLA Ops:
  0.6 0.0 copy-start
  0.6 0.0 copy-start.1
  0.7 2.2 %bring.5.refs_2_.refs_1_ = f32[1024,1024]{1,0:T(8,128)S(1)} custom-call(f32[1024,4096]{1,0:T(8,128)} %bitcast.4), custom_call_target="tpu_custom_call" | custom-call | tf_op jit(solution)/shard_map/bring/pallas_call | solution.py:349
  2.9 0.0 copy-done
  2.9 0.0 copy-done.1
  2.9 2.3 %bring.6 = (f32[32,1024]{1,0:T(8,128)S(1)}, f32[1024,1024]{1,0:T(8,128)S(1)}, bf16[64,1024]{1,0:T(8,128)(2,1)S(1)}, f32[32,128]{1,0:T(8,128)S(1)}) custom-call(f32[32,128]{1,0:T(8,128)S(1)} %copy-done, f32[8,32]{1,0:T(8,128)S(1)} %bitcast.3, f32[1024,1024]{1,0:T(8,128)S(1)} %bring.5.refs_2_.refs_1_, f32[1024,4096]{1,0:T(8,128)} %bitcast.5), custom_call_target="tpu_custom_call" | custom-call | flops 1024 | bytes 1024 | tf_op jit(solution)/shard_map/bring/pallas_call | solution.py:349
  5.2 1.5 %collective-permute-start.2 = (f32[32,1024]{1,0:T(8,128)S(1)}, f32[32,1024]{1,0:T(8,128)S(1)}, u32[]{:S(2)}, u32[]{:S(2)}) collective-permute-start(f32[32,1024]{1,0:T(8,128)S(1)} %get-tuple-element.45), channel_id=1, source_target_pairs={{0,2},{2,0},{1,3},{3,1},{4,6},{6,4},{5,7},{7,5},{8,10},{10,8},{9,1... | collective-permute-start | bytes 393224 | tf_op jit(solution)/shard_map/ppermute | solution.py:325
  6.7 0.1 collective-permute-start.3
  6.8 2.2 %bring.7 = (f32[32,1024]{1,0:T(8,128)S(1)}, f32[1024,1024]{1,0:T(8,128)S(1)}) custom-call(bf16[64,1024]{1,0:T(8,128)(2,1)S(1)} %get-tuple-element.39.refs_0_, f32[1024,1024]{1,0:T(8,128)S(1)} %get-tuple-element.40.refs_1_, f32[1024,4096]{1,0:T(8,128)} %bitcast.6), custom_call_target="tpu_custom_call" | custom-call | flops 1024 | bytes 1024 | tf_op jit(solution)/shard_map/bring/pallas_call | solution.py:349
  9.1 0.0 collective-permute-done.3.core_ref
  9.1 0.0 collective-permute-done.2
  9.1 1.8 %collective-permute-start.4 = (f32[32,1152]{1,0:T(8,128)S(1)}, f32[32,1152]{1,0:T(8,128)S(1)}, u32[]{:S(2)}, u32[]{:S(2)}) collective-permute-start(f32[32,1152]{1,0:T(8,128)S(1)} %pad_maximum_fusion), channel_id=1, source_target_pairs={{0,1},{1,0},{2,3},{3,2},{4,5},{5,4},{6,7},{7,6},{8,9},{9,8},{10,11... | collective-permute-start | bytes 442376 | tf_op jit(solution)/shard_map/ppermute | solution.py:328
  10.9 2.2 %bring.8 = (f32[32,1024]{1,0:T(8,128)S(1)}, f32[1024,1024]{1,0:T(8,128)S(1)}) custom-call(bf16[64,1024]{1,0:T(8,128)(2,1)S(1)} %get-tuple-element.39.refs_0_, f32[1024,1024]{1,0:T(8,128)S(1)} %get-tuple-element.41.refs_1_, f32[1024,4096]{1,0:T(8,128)} %bitcast.7), custom_call_target="tpu_custom_call" | custom-call | flops 1024 | bytes 1024 | tf_op jit(solution)/shard_map/bring/pallas_call | solution.py:349
  13.1 0.8 %collective-permute-start = (f32[32,1024]{1,0:T(8,128)S(1)}, f32[32,1024]{1,0:T(8,128)S(1)}, u32[]{:S(2)}, u32[]{:S(2)}) collective-permute-start(f32[32,1024]{1,0:T(8,128)S(1)} %get-tuple-element.43), channel_id=1, source_target_pairs={{0,2},{2,0},{1,3},{3,1},{4,6},{6,4},{5,7},{7,5},{8,10},{10,8},{9,1... | collective-permute-start | bytes 393224 | tf_op jit(solution)/shard_map/ppermute | solution.py:325
  13.9 0.9 %bring.9 = f32[32,1024]{1,0:T(8,128)S(1)} custom-call(bf16[64,1024]{1,0:T(8,128)(2,1)S(1)} %get-tuple-element.39.refs_0_, f32[1024,1024]{1,0:T(8,128)S(1)} %get-tuple-element.42.refs_1_), custom_call_target="tpu_custom_call" | custom-call | flops 1024 | bytes 1024 | tf_op jit(solution)/shard_map/bring/pallas_call | solution.py:349
  14.8 0.1 collective-permute-done
  14.9 0.1 collective-permute-start.1
  15.0 0.0 collective-permute-done.4.theirs_ref.piece_ref
  15.1 0.8 %collective-permute-start.5 = (f32[32,1024]{1,0:T(8,128)S(1)}, f32[32,1024]{1,0:T(8,128)S(1)}, u32[]{:S(2)}, u32[]{:S(2)}) collective-permute-start(f32[32,1024]{1,0:T(8,128)S(1)} %add_piece.2.refs_0_), channel_id=1, source_target_pairs={{0,2},{2,0},{1,3},{3,1},{4,6},{6,4},{5,7},{7,5},{8,10},{10,8},{9,1... | collective-permute-start | bytes 393224 | tf_op jit(solution)/shard_map/ppermute | solution.py:325
  15.8 1.5 %weigh.3 = (f32[32,1024]{1,0:T(8,128)S(1)}, f32[32,32]{1,0:T(8,128)S(1)}) custom-call(f32[32,1024]{1,0:T(8,128)S(1)} %add_piece.2.refs_0_, f32[1024,1024]{1,0:T(8,128)S(1)} %get-tuple-element.40.refs_1_), custom_call_target="tpu_custom_call" | custom-call | flops 2013265920 | bytes 41943040 | tf_op jit(solution)/shard_map/weigh/pallas_call | solution.py:379
  17.3 0.0 collective-permute-done.5.refs_0_.refs_1_
  17.3 1.5 %weigh.4 = (f32[32,1024]{1,0:T(8,128)S(1)}, f32[32,32]{1,0:T(8,128)S(1)}) custom-call(f32[32,1024]{1,0:T(8,128)S(1)} %collective-permute-done.5.refs_0_.refs_1_, f32[1024,1024]{1,0:T(8,128)S(1)} %bring.5.refs_2_.refs_1_, f32[32,1024]{1,0:T(8,128)S(1)} %get-tuple-element.48.refs_2_, f32[32,32]{1,0:T(8,128)S(1)} %get-tuple-element.49.refs_3_), custom_call_target="tpu_custom_call" | custom-call | flops 2013265920 | bytes 41943040 | tf_op jit(solution)/shard_map/weigh/pallas_call | solution.py:383
  18.9 0.9 %collective-permute-done.1.theirs_ref = f32[32,1024]{1,0:T(8,128)S(1)} collective-permute-done((f32[32,1024]{1,0:T(8,128)S(1)}, f32[32,1024]{1,0:T(8,128)S(1)}, u32[]{:S(2)}, u32[]{:S(2)}) %collective-permute-start.1) | collective-permute-done | bytes 131104 | tf_op jit(solution)/shard_map/ppermute | solution.py:328
  19.8 1.3 %collective-permute-start.6 = (f32[32,1024]{1,0:T(8,128)S(1)}, f32[32,1024]{1,0:T(8,128)S(1)}, u32[]{:S(2)}, u32[]{:S(2)}) collective-permute-start(f32[32,1024]{1,0:T(8,128)S(1)} %add_piece.3.refs_0_.refs_2_), channel_id=1, source_target_pairs={{0,2},{2,0},{1,3},{3,1},{4,6},{6,4},{5,7},{7,5},{8,10},{10,8},{9,1... | collective-permute-start | bytes 393224 | tf_op jit(solution)/shard_map/ppermute | solution.py:325
  21.0 1.4 %weigh.5 = (f32[32,1024]{1,0:T(8,128)S(1)}, f32[32,32]{1,0:T(8,128)S(1)}) custom-call(f32[32,1024]{1,0:T(8,128)S(1)} %add_piece.3.refs_0_.refs_2_, f32[1024,1024]{1,0:T(8,128)S(1)} %get-tuple-element.42.refs_1_, f32[32,1024]{1,0:T(8,128)S(1)} %get-tuple-element.51.refs_2_, f32[32,32]{1,0:T(8,128)S(1)} %get-tuple-element.50.refs_0_.refs_3_), custom_call_target="tpu_custom_call" | custom-call | flops 2013265920 | bytes 41943040 | tf_op jit(solution)/shard_map/weigh/pallas_call | solution.py:379
  22.4 0.0 collective-permute-done.6.refs_0_.refs_3_
  22.4 1.6 %weigh_last.1 = (f32[40,256]{1,0:T(8,128)S(1)}, f32[40,256]{1,0:T(8,128)S(1)}, f32[40,256]{1,0:T(8,128)S(1)}, f32[40,256]{1,0:T(8,128)S(1)}) custom-call(f32[32,1024]{1,0:T(8,128)S(1)} %collective-permute-done.6.refs_0_.refs_3_, f32[1024,1024]{1,0:T(8,128)S(1)} %get-tuple-element.41.refs_1_, f32[32,1024]{1,0:T(8,128)S(1)} %get-tuple-element.52.refs_2_, ...), custom_call_target="tpu_custom_call" | custom-call | flops 2013265920 | bytes 41943040 | tf_op jit(solution)/shard_map/weigh_last/pallas_call | solution.py:386
  24.0 2.8 %collective-permute-start.7 = (f32[40,256]{1,0:T(8,128)S(1)}, f32[40,256]{1,0:T(8,128)S(1)}, u32[]{:S(2)}, u32[]{:S(2)}) collective-permute-start(f32[40,256]{1,0:T(8,128)S(1)} %get-tuple-element.55), channel_id=1, source_target_pairs={{0,8},{4,12},{8,0},{12,4},{16,24},{20,28},{24,16},{28,20},{32,40},... | collective-permute-start | bytes 122888 | tf_op jit(solution)/shard_map/ppermute | solution.py:331
  26.8 0.9 %collective-permute-start.8 = (f32[40,256]{1,0:T(8,128)S(1)}, f32[40,256]{1,0:T(8,128)S(1)}, u32[]{:S(2)}, u32[]{:S(2)}) collective-permute-start(f32[40,256]{1,0:T(8,128)S(1)} %get-tuple-element.58), channel_id=1, source_target_pairs={{0,12},{4,8},{8,4},{12,0},{16,28},{20,24},{24,20},{28,16},{32,44},... | collective-permute-start | bytes 122888 | tf_op jit(solution)/shard_map/ppermute | solution.py:331
  27.7 0.0 collective-permute-start.9
  27.7 1.2 %start_system.1 = (f32[32,32]{1,0:T(8,128)S(1)}, f32[32,32]{1,0:T(8,128)S(1)}) custom-call(f32[32,128]{1,0:T(8,128)S(1)} %copy-done, f32[32,128]{1,0:T(8,128)S(1)} %collective-permute-done.3.core_ref, f32[32,128]{1,0:T(8,128)S(1)} %get-tuple-element.47.time_ref, f32[32,1152]{1,0:T(8,128)S(1)} %collective-permute-done.4.theirs_ref.piece_ref), custom_call_target="tpu_custom_call" | custom-call | flops 1048576 | bytes 262144 | tf_op jit(solution)/shard_map/start_system/pallas_call | solution.py:390
  28.9 0.0 collective-permute-done.7.b_ref
  28.9 2.0 %collective-permute-done.8.a_ref = f32[40,256]{1,0:T(8,128)S(1)} collective-permute-done((f32[40,256]{1,0:T(8,128)S(1)}, f32[40,256]{1,0:T(8,128)S(1)}, u32[]{:S(2)}, u32[]{:S(2)}) %collective-permute-start.8) | collective-permute-done | bytes 40992 | tf_op jit(solution)/shard_map/ppermute | solution.py:331
  30.9 0.0 collective-permute-done.9
  30.9 3.0 %collective-permute-start.10 = (f32[40,256]{1,0:T(8,128)S(1)}, f32[40,256]{1,0:T(8,128)S(1)}, u32[]{:S(2)}, u32[]{:S(2)}) collective-permute-start(f32[40,256]{1,0:T(8,128)S(1)} %add_add_fusion.a_ref), channel_id=1, source_target_pairs={{0,64},{4,68},{8,72},{12,76},{16,80},{20,84},{24,88},{28,92},{32,9... | collective-permute-start | bytes 122888 | tf_op jit(solution)/shard_map/ppermute | solution.py:331
  33.9 0.8 %collective-permute-start.11 = (f32[40,256]{1,0:T(8,128)S(1)}, f32[40,256]{1,0:T(8,128)S(1)}, u32[]{:S(2)}, u32[]{:S(2)}) collective-permute-start(f32[40,256]{1,0:T(8,128)S(1)} %add_add_fusion.a_ref), channel_id=1, source_target_pairs={{0,96},{4,100},{8,104},{12,108},{16,112},{20,116},{24,120},{28,124... | collective-permute-start | bytes 122888 | tf_op jit(solution)/shard_map/ppermute | solution.py:331
  34.7 0.0 collective-permute-start.12
  34.7 0.5 solve_pat.1
  35.2 0.1 collective-permute-done.10.b_ref
  35.4 2.6 %collective-permute-done.11.a_ref = f32[40,256]{1,0:T(8,128)S(1)} collective-permute-done((f32[40,256]{1,0:T(8,128)S(1)}, f32[40,256]{1,0:T(8,128)S(1)}, u32[]{:S(2)}, u32[]{:S(2)}) %collective-permute-start.11) | collective-permute-done | bytes 40992 | tf_op jit(solution)/shard_map/ppermute | solution.py:331
  38.0 0.0 collective-permute-done.12.c_ref
  38.0 0.6 add_and_project.1
  38.5 2.3 %collective-permute-start.13 = (f32[40,256]{1,0:T(8,128)S(1)}, f32[40,256]{1,0:T(8,128)S(1)}, u32[]{:S(2)}, u32[]{:S(2)}) collective-permute-start(f32[40,256]{1,0:T(8,128)S(1)} %get-tuple-element.61.refs_0_.own_ref), channel_id=1, source_target_pairs={{0,17},{1,16},{4,21},{5,20},{8,25},{9,24},{12,29},{13,28},{16,1},{... | collective-permute-start | bytes 122888 | tf_op jit(solution)/shard_map/ppermute | solution.py:335
  40.9 1.1 %collective-permute-start.14 = (f32[40,256]{1,0:T(8,128)S(1)}, f32[40,256]{1,0:T(8,128)S(1)}, u32[]{:S(2)}, u32[]{:S(2)}) collective-permute-start(f32[40,256]{1,0:T(8,128)S(1)} %get-tuple-element.61.refs_0_.own_ref), channel_id=1, source_target_pairs={{0,16},{4,20},{8,24},{12,28},{16,0},{20,4},{24,8},{28,12},{32,48},... | collective-permute-start | bytes 122888 | tf_op jit(solution)/shard_map/ppermute | solution.py:331
  42.0 0.0 collective-permute-start.15
  42.0 0.7 %collective-permute-done.13.refs_1_.far_ref = f32[40,256]{1,0:T(8,128)S(1)} collective-permute-done((f32[40,256]{1,0:T(8,128)S(1)}, f32[40,256]{1,0:T(8,128)S(1)}, u32[]{:S(2)}, u32[]{:S(2)}) %collective-permute-start.13) | collective-permute-done | bytes 40992 | tf_op jit(solution)/shard_map/ppermute | solution.py:335
  42.7 1.1 %feat_system.1 = (f32[32,32]{1,0:T(8,128)S(1)}, f32[32,128]{1,0:T(8,128)S(1)}, f32[32,32]{1,0:T(8,128)S(1)}) custom-call(f32[40,256]{1,0:T(8,128)S(1)} %get-tuple-element.61.refs_0_.own_ref, f32[40,256]{1,0:T(8,128)S(1)} %collective-permute-done.13.refs_1_.far_ref, f32[32,32]{1,0:T(8,128)S(1)} %get-tuple-element.62.refs_2_), custom_call_target="tpu_custom_call" | custom-call | flops 1048576 | bytes 262144 | tf_op jit(solution)/shard_map/feat_system/pallas_call | solution.py:406
  43.7 1.5 %collective-permute-done.14.high_ref = f32[40,256]{1,0:T(8,128)S(1)} collective-permute-done((f32[40,256]{1,0:T(8,128)S(1)}, f32[40,256]{1,0:T(8,128)S(1)}, u32[]{:S(2)}, u32[]{:S(2)}) %collective-permute-start.14) | collective-permute-done | bytes 40992 | tf_op jit(solution)/shard_map/ppermute | solution.py:331
  45.2 0.1 scale_weighted.1.weighted_ref
  45.3 0.0 collective-permute-done.15.tm_ref
  45.3 0.6 %solve_feat.1.a_ref = f32[32,256]{1,0:T(8,128)S(1)} custom-call(f32[40,256]{1,0:T(8,128)S(1)} %get-tuple-element.61.refs_0_.own_ref, f32[40,256]{1,0:T(8,128)S(1)} %collective-permute-done.13.refs_1_.far_ref, f32[40,256]{1,0:T(8,128)S(1)} %collective-permute-done.14.high_ref, f32[8,128]{1,0:T(8,128)S(1)} %collective-permute-done.15.tm_ref, ...), custom_call_target="tpu_custom_call" | custom-call | flops 1048576 | bytes 262144 | tf_op jit(solution)/shard_map/solve_feat/pallas_call | solution.py:413
  45.9 1.3 %collective-permute-start.16 = (f32[32,256]{1,0:T(8,128)S(1)}, f32[32,256]{1,0:T(8,128)S(1)}, u32[]{:S(2)}, u32[]{:S(2)}) collective-permute-start(f32[32,256]{1,0:T(8,128)S(1)} %solve_feat.1.a_ref), channel_id=1, source_target_pairs={{0,8},{4,12},{8,0},{12,4},{16,24},{20,28},{24,16},{28,20},{32,40},... | collective-permute-start | bytes 98312 | tf_op jit(solution)/shard_map/ppermute | solution.py:331
  47.2 1.4 %collective-permute-start.17 = (f32[32,256]{1,0:T(8,128)S(1)}, f32[32,256]{1,0:T(8,128)S(1)}, u32[]{:S(2)}, u32[]{:S(2)}) collective-permute-start(f32[32,256]{1,0:T(8,128)S(1)} %solve_feat.1.a_ref), channel_id=1, source_target_pairs={{0,12},{4,8},{8,4},{12,0},{16,28},{20,24},{24,20},{28,16},{32,44},... | collective-permute-start | bytes 98312 | tf_op jit(solution)/shard_map/ppermute | solution.py:331
  48.6 0.1 collective-permute-start.18
  48.7 0.9 %scale_pat.1 = (f32[32,4096]{1,0:T(8,128)}, f32[8,128]{1,0:T(8,128)S(1)}) custom-call(f32[32,128]{1,0:T(8,128)S(1)} %get-tuple-element.63.scale_ref, f32[32,1024]{1,0:T(8,128)S(1)} %get-tuple-element.64.refs_0_, f32[32,1024]{1,0:T(8,128)S(1)} %get-tuple-element.65.refs_1_, f32[32,1024]{1,0:T(8,128)S(1)} %get-tuple-element.66.refs_2_, ...), custom_call_target="tpu_custom_call" | custom-call | flops 1048576 | bytes 262144 | tf_op jit(solution)/shard_map/scale_pat/pallas_call | solution.py:414
  49.6 0.7 %collective-permute-done.16.b_ref = f32[32,256]{1,0:T(8,128)S(1)} collective-permute-done((f32[32,256]{1,0:T(8,128)S(1)}, f32[32,256]{1,0:T(8,128)S(1)}, u32[]{:S(2)}, u32[]{:S(2)}) %collective-permute-start.16) | collective-permute-done | bytes 32800 | tf_op jit(solution)/shard_map/ppermute | solution.py:331
  50.3 0.9 %collective-permute-done.17.a_ref = f32[32,256]{1,0:T(8,128)S(1)} collective-permute-done((f32[32,256]{1,0:T(8,128)S(1)}, f32[32,256]{1,0:T(8,128)S(1)}, u32[]{:S(2)}, u32[]{:S(2)}) %collective-permute-start.17) | collective-permute-done | bytes 32800 | tf_op jit(solution)/shard_map/ppermute | solution.py:331
  51.2 0.1 collective-permute-done.18
  51.3 5.7 %collective-permute-start.19 = (f32[32,128]{1,0:T(8,128)S(1)}, f32[32,128]{1,0:T(8,128)S(1)}, u32[]{:S(2)}, u32[]{:S(2)}) collective-permute-start(f32[32,128]{1,0:T(8,128)S(1)} %get-tuple-element.76.refs_0_), channel_id=1, source_target_pairs={{0,2},{2,0},{1,3},{3,1},{4,6},{6,4},{5,7},{7,5},{8,10},{10,8},{9,1... | collective-permute-start | bytes 49160 | tf_op jit(solution)/shard_map/ppermute | solution.py:325
  57.0 0.8 %collective-permute-done.19.refs_1_ = f32[32,128]{1,0:T(8,128)S(1)} collective-permute-done((f32[32,128]{1,0:T(8,128)S(1)}, f32[32,128]{1,0:T(8,128)S(1)}, u32[]{:S(2)}, u32[]{:S(2)}) %collective-permute-start.19) | collective-permute-done | bytes 16416 | tf_op jit(solution)/shard_map/ppermute | solution.py:325
  57.8 1.7 %solve_time.1 = (f32[32,128]{1,0:T(8,128)}, f32[8,32]{1,0:T(8,128)}) custom-call(f32[32,128]{1,0:T(8,128)S(1)} %get-tuple-element.76.refs_0_, f32[32,128]{1,0:T(8,128)S(1)} %collective-permute-done.19.refs_1_, f32[32,128]{1,0:T(8,128)S(1)} %get-tuple-element.75.refs_2_, f32[32,32]{1,0:T(8,128)S(1)} %get-tuple-element.72.refs_3_), custom_call_target="tpu_custom_call" | custom-call | flops 1048576 | bytes 262144 | tf_op jit(solution)/shard_map/solve_time/pallas_call | solution.py:420
  (14 shorter events, 0.1 us)
Async XLA Ops:
  0.6 2.3 %copy-start = (f32[32,128]{1,0:T(8,128)S(1)}, f32[32,128]{1,0:T(8,128)}, u32[]{:S(2)}) copy-start(f32[32,128]{1,0:T(8,128)} %feat_ref.1) | copy-start | bytes 49156
  0.6 2.3 %copy-start.1 = (f32[32,8]{0,1:T(8,128)S(1)}, f32[32,8]{0,1:T(8,128)}, u32[]{:S(2)}) copy-start(f32[32,8]{0,1:T(8,128)} %param.5) | copy-start | bytes 3076
  5.2 3.8 %collective-permute-start.2 = (f32[32,1024]{1,0:T(8,128)S(1)}, f32[32,1024]{1,0:T(8,128)S(1)}, u32[]{:S(2)}, u32[]{:S(2)}) collective-permute-start(f32[32,1024]{1,0:T(8,128)S(1)} %get-tuple-element.45), channel_id=1, source_target_pairs={{0,2},{2,0},{1,3},{3,1},{4,6},{6,4},{5,7},{7,5},{8,10},{10,8},{9,1... | collective-permute-start | bytes 393224 | tf_op jit(solution)/shard_map/ppermute | solution.py:325
  6.7 2.3 %collective-permute-start.3 = (f32[32,128]{1,0:T(8,128)S(1)}, f32[32,128]{1,0:T(8,128)S(1)}, u32[]{:S(2)}, u32[]{:S(2)}) collective-permute-start(f32[32,128]{1,0:T(8,128)S(1)} %copy-done), channel_id=1, source_target_pairs={{0,2},{2,0},{1,3},{3,1},{4,6},{6,4},{5,7},{7,5},{8,10},{10,8},{9,1... | collective-permute-start | bytes 49160 | tf_op jit(solution)/shard_map/ppermute | solution.py:325
  9.1 5.9 %collective-permute-start.4 = (f32[32,1152]{1,0:T(8,128)S(1)}, f32[32,1152]{1,0:T(8,128)S(1)}, u32[]{:S(2)}, u32[]{:S(2)}) collective-permute-start(f32[32,1152]{1,0:T(8,128)S(1)} %pad_maximum_fusion), channel_id=1, source_target_pairs={{0,1},{1,0},{2,3},{3,2},{4,5},{5,4},{6,7},{7,6},{8,9},{9,8},{10,11... | collective-permute-start | bytes 442376 | tf_op jit(solution)/shard_map/ppermute | solution.py:328
  13.1 1.8 %collective-permute-start = (f32[32,1024]{1,0:T(8,128)S(1)}, f32[32,1024]{1,0:T(8,128)S(1)}, u32[]{:S(2)}, u32[]{:S(2)}) collective-permute-start(f32[32,1024]{1,0:T(8,128)S(1)} %get-tuple-element.43), channel_id=1, source_target_pairs={{0,2},{2,0},{1,3},{3,1},{4,6},{6,4},{5,7},{7,5},{8,10},{10,8},{9,1... | collective-permute-start | bytes 393224 | tf_op jit(solution)/shard_map/ppermute | solution.py:325
  14.9 4.8 %collective-permute-start.1 = (f32[32,1024]{1,0:T(8,128)S(1)}, f32[32,1024]{1,0:T(8,128)S(1)}, u32[]{:S(2)}, u32[]{:S(2)}) collective-permute-start(f32[32,1024]{1,0:T(8,128)S(1)} %add.18.refs_0_.mine_ref), channel_id=1, source_target_pairs={{0,1},{1,0},{2,3},{3,2},{4,5},{5,4},{6,7},{7,6},{8,9},{9,8},{10,11... | collective-permute-start | bytes 393224 | tf_op jit(solution)/shard_map/ppermute | solution.py:328
  15.1 2.3 %collective-permute-start.5 = (f32[32,1024]{1,0:T(8,128)S(1)}, f32[32,1024]{1,0:T(8,128)S(1)}, u32[]{:S(2)}, u32[]{:S(2)}) collective-permute-start(f32[32,1024]{1,0:T(8,128)S(1)} %add_piece.2.refs_0_), channel_id=1, source_target_pairs={{0,2},{2,0},{1,3},{3,1},{4,6},{6,4},{5,7},{7,5},{8,10},{10,8},{9,1... | collective-permute-start | bytes 393224 | tf_op jit(solution)/shard_map/ppermute | solution.py:325
  19.8 2.7 %collective-permute-start.6 = (f32[32,1024]{1,0:T(8,128)S(1)}, f32[32,1024]{1,0:T(8,128)S(1)}, u32[]{:S(2)}, u32[]{:S(2)}) collective-permute-start(f32[32,1024]{1,0:T(8,128)S(1)} %add_piece.3.refs_0_.refs_2_), channel_id=1, source_target_pairs={{0,2},{2,0},{1,3},{3,1},{4,6},{6,4},{5,7},{7,5},{8,10},{10,8},{9,1... | collective-permute-start | bytes 393224 | tf_op jit(solution)/shard_map/ppermute | solution.py:325
  24.0 4.9 %collective-permute-start.7 = (f32[40,256]{1,0:T(8,128)S(1)}, f32[40,256]{1,0:T(8,128)S(1)}, u32[]{:S(2)}, u32[]{:S(2)}) collective-permute-start(f32[40,256]{1,0:T(8,128)S(1)} %get-tuple-element.55), channel_id=1, source_target_pairs={{0,8},{4,12},{8,0},{12,4},{16,24},{20,28},{24,16},{28,20},{32,40},... | collective-permute-start | bytes 122888 | tf_op jit(solution)/shard_map/ppermute | solution.py:331
  26.8 4.1 %collective-permute-start.8 = (f32[40,256]{1,0:T(8,128)S(1)}, f32[40,256]{1,0:T(8,128)S(1)}, u32[]{:S(2)}, u32[]{:S(2)}) collective-permute-start(f32[40,256]{1,0:T(8,128)S(1)} %get-tuple-element.58), channel_id=1, source_target_pairs={{0,12},{4,8},{8,4},{12,0},{16,28},{20,24},{24,20},{28,16},{32,44},... | collective-permute-start | bytes 122888 | tf_op jit(solution)/shard_map/ppermute | solution.py:331
  27.7 3.2 %collective-permute-start.9 = (f32[40,256]{1,0:T(8,128)S(1)}, f32[40,256]{1,0:T(8,128)S(1)}, u32[]{:S(2)}, u32[]{:S(2)}) collective-permute-start(f32[40,256]{1,0:T(8,128)S(1)} %get-tuple-element.59), channel_id=1, source_target_pairs={{0,4},{4,0},{8,12},{12,8},{16,20},{20,16},{24,28},{28,24},{32,36},... | collective-permute-start | bytes 122888 | tf_op jit(solution)/shard_map/ppermute | solution.py:331
  30.9 4.4 %collective-permute-start.10 = (f32[40,256]{1,0:T(8,128)S(1)}, f32[40,256]{1,0:T(8,128)S(1)}, u32[]{:S(2)}, u32[]{:S(2)}) collective-permute-start(f32[40,256]{1,0:T(8,128)S(1)} %add_add_fusion.a_ref), channel_id=1, source_target_pairs={{0,64},{4,68},{8,72},{12,76},{16,80},{20,84},{24,88},{28,92},{32,9... | collective-permute-start | bytes 122888 | tf_op jit(solution)/shard_map/ppermute | solution.py:331
  33.9 4.1 %collective-permute-start.11 = (f32[40,256]{1,0:T(8,128)S(1)}, f32[40,256]{1,0:T(8,128)S(1)}, u32[]{:S(2)}, u32[]{:S(2)}) collective-permute-start(f32[40,256]{1,0:T(8,128)S(1)} %add_add_fusion.a_ref), channel_id=1, source_target_pairs={{0,96},{4,100},{8,104},{12,108},{16,112},{20,116},{24,120},{28,124... | collective-permute-start | bytes 122888 | tf_op jit(solution)/shard_map/ppermute | solution.py:331
  34.7 3.3 %collective-permute-start.12 = (f32[40,256]{1,0:T(8,128)S(1)}, f32[40,256]{1,0:T(8,128)S(1)}, u32[]{:S(2)}, u32[]{:S(2)}) collective-permute-start(f32[40,256]{1,0:T(8,128)S(1)} %add_add_fusion.a_ref), channel_id=1, source_target_pairs={{0,32},{4,36},{8,40},{12,44},{16,48},{20,52},{24,56},{28,60},{32,0... | collective-permute-start | bytes 122888 | tf_op jit(solution)/shard_map/ppermute | solution.py:331
  38.5 4.1 %collective-permute-start.13 = (f32[40,256]{1,0:T(8,128)S(1)}, f32[40,256]{1,0:T(8,128)S(1)}, u32[]{:S(2)}, u32[]{:S(2)}) collective-permute-start(f32[40,256]{1,0:T(8,128)S(1)} %get-tuple-element.61.refs_0_.own_ref), channel_id=1, source_target_pairs={{0,17},{1,16},{4,21},{5,20},{8,25},{9,24},{12,29},{13,28},{16,1},{... | collective-permute-start | bytes 122888 | tf_op jit(solution)/shard_map/ppermute | solution.py:335
  40.9 4.4 %collective-permute-start.14 = (f32[40,256]{1,0:T(8,128)S(1)}, f32[40,256]{1,0:T(8,128)S(1)}, u32[]{:S(2)}, u32[]{:S(2)}) collective-permute-start(f32[40,256]{1,0:T(8,128)S(1)} %get-tuple-element.61.refs_0_.own_ref), channel_id=1, source_target_pairs={{0,16},{4,20},{8,24},{12,28},{16,0},{20,4},{24,8},{28,12},{32,48},... | collective-permute-start | bytes 122888 | tf_op jit(solution)/shard_map/ppermute | solution.py:331
  42.0 3.4 %collective-permute-start.15 = (f32[8,128]{1,0:T(8,128)S(1)}, f32[8,128]{1,0:T(8,128)S(1)}, u32[]{:S(2)}, u32[]{:S(2)}) collective-permute-start(f32[8,128]{1,0:T(8,128)S(1)} %get-tuple-element.69), channel_id=1, source_target_pairs={{0,1},{1,0},{2,3},{3,2},{4,5},{5,4},{6,7},{7,6},{8,9},{9,8},{10,11... | collective-permute-start | bytes 12296 | tf_op jit(solution)/shard_map/ppermute | solution.py:328
  45.9 4.3 %collective-permute-start.16 = (f32[32,256]{1,0:T(8,128)S(1)}, f32[32,256]{1,0:T(8,128)S(1)}, u32[]{:S(2)}, u32[]{:S(2)}) collective-permute-start(f32[32,256]{1,0:T(8,128)S(1)} %solve_feat.1.a_ref), channel_id=1, source_target_pairs={{0,8},{4,12},{8,0},{12,4},{16,24},{20,28},{24,16},{28,20},{32,40},... | collective-permute-start | bytes 98312 | tf_op jit(solution)/shard_map/ppermute | solution.py:331
  47.2 4.0 %collective-permute-start.17 = (f32[32,256]{1,0:T(8,128)S(1)}, f32[32,256]{1,0:T(8,128)S(1)}, u32[]{:S(2)}, u32[]{:S(2)}) collective-permute-start(f32[32,256]{1,0:T(8,128)S(1)} %solve_feat.1.a_ref), channel_id=1, source_target_pairs={{0,12},{4,8},{8,4},{12,0},{16,28},{20,24},{24,20},{28,16},{32,44},... | collective-permute-start | bytes 98312 | tf_op jit(solution)/shard_map/ppermute | solution.py:331
  48.6 2.8 %collective-permute-start.18 = (f32[32,256]{1,0:T(8,128)S(1)}, f32[32,256]{1,0:T(8,128)S(1)}, u32[]{:S(2)}, u32[]{:S(2)}) collective-permute-start(f32[32,256]{1,0:T(8,128)S(1)} %solve_feat.1.a_ref), channel_id=1, source_target_pairs={{0,4},{4,0},{8,12},{12,8},{16,20},{20,16},{24,28},{28,24},{32,36},... | collective-permute-start | bytes 98312 | tf_op jit(solution)/shard_map/ppermute | solution.py:331
  51.3 6.5 %collective-permute-start.19 = (f32[32,128]{1,0:T(8,128)S(1)}, f32[32,128]{1,0:T(8,128)S(1)}, u32[]{:S(2)}, u32[]{:S(2)}) collective-permute-start(f32[32,128]{1,0:T(8,128)S(1)} %get-tuple-element.76.refs_0_), channel_id=1, source_target_pairs={{0,2},{2,0},{1,3},{3,1},{4,6},{6,4},{5,7},{7,5},{8,10},{10,8},{9,1... | collective-permute-start | bytes 49160 | tf_op jit(solution)/shard_map/ppermute | solution.py:325

commit v5 on v4

--- a/solution.py
+++ b/solution.py
@@ -45,7 +45,7 @@
     return jnp.where(lax.rem(iota(shape, 1), time) == iota(shape, 0), 1.0, 0.0).astype(f32)
 
 
-def eliminate(tiles, group=8):
+def eliminate(tiles, group=16):
     rank = tiles[0].shape[0]
     rows = iota((rank, LANES), 0)
     for start in range(0, rank, group):
@@ -158,6 +158,37 @@
         copy.wait()
 
 
+def bring_both(half, offset, hl_ref, before_ref, block_ref, terms_ref, other_ref, mine_ref, sems):
+    me = lax.axis_index("feat")
+    rank = terms_ref.shape[0]
+    cells, patients = other_ref.shape
+    step = cells // LOADS
+    copies = []
+    for part, (who, kept_ref) in enumerate(((1 - me, other_ref), (me, mine_ref))):
+        first = pl.multiple_of(who * half + offset, CHUNK)
+        for i in range(LOADS):
+            rows = pl.ds(i * step, step)
+            copies.append(
+                pltpu.make_async_copy(
+                    block_ref.at[rows, pl.ds(first, patients)], kept_ref.at[rows, :], sems.at[part * LOADS + i]
+                )
+            )
+    for copy in copies:
+        copy.start()
+    for i in range(LOADS):
+        copies[i].wait()
+        rows = slice(i * step, (i + 1) * step)
+        for c in range(0, patients, CHUNK):
+            hi, lo = split(other_ref[rows, c : c + CHUNK])
+            both = quick(hl_ref[:, rows], hi)
+            part = both[:rank] + both[rank:] + quick(hl_ref[:rank, rows], lo)
+            if i > 0:
+                part = part + terms_ref[:, c : c + CHUNK]
+            terms_ref[:, c : c + CHUNK] = part
+    for copy in copies[LOADS:]:
+        copy.wait()
+
+
 def start_system(feat_ref, core_ref, time_ref, piece_ref, inverse_ref, time_gram_ref):
     rank = inverse_ref.shape[0]
     feat, feat_other = feat_ref[...], core_ref[...]
@@ -355,10 +386,13 @@
         True, 0, c0, feat_init, time_rows, kept_o0, flat, before=c0, more=[((2 * rank, cells), bf16), ((rank, LANES), f32)]
     )
     arrived_0, feat_core = lax.optimization_barrier((from_core(away_0), from_core(feat_init)))
-    own_0, kept_o1 = step(False, c0, c1, hl, kept_m0, flat, before=c0)
+    (own_0,) = step(None, 0, 0, hl, kept_m0, before=c0)
     mine = [own_0 + arrived_0]
     theirs = [from_tm(jnp.concatenate([mine[0], time_rows], axis=1))]
-    away_1, kept_m1 = step(True, c0, c1, hl, kept_o1, flat, before=c1)
+    away_1, kept_o1, kept_m1 = call(
+        lambda *refs: bring_both(half, c0, *refs), [((rank, c1), f32), ((cells, c1), f32), ((cells, c1), f32)],
+        "bring_both", [VMEM, VMEM, HBM], [pltpu.SemaphoreType.DMA((2 * LOADS,))], ROOM, **load(c1),
+    )(hl, own_0, flat)
     arrived_1 = from_core(away_1)
     (own_1,) = step(None, 0, 0, hl, kept_m1, before=c1)
     mine.append(own_1 + arrived_1)

time: 59.7 us -> 59.6 us (level)
  waiting for transfers between devices: 10.5 us -> 11.6 us
  Pallas kernels: 22.6 us -> 21.8 us
    pallas_call x5 -> x4, Pallas kernels: 9.85 us -> 6.29 us  [step(): call(lambda *refs: bring(half, mine, offset, *refs), outs, 'bring', specs...]
    pallas_call x0 -> x1, Pallas kernels: none -> 3.49 us  [per_device(): call(lambda *refs: bring_both(half, c0, *refs), [((rank, c1), f32), ((cel...]
  transfers between devices with their start and end apart: 20 -> 20, of which waited for: 11 -> 12; matrix products, arithmetic and copies ran while one was open for 0% -> 0% of each run, Pallas kernels for 23% -> 22%
where the time goes in v5:
time: 59.6 us; the launch traced here: 59.4 us
  starting transfers between devices  25.2 us (42%)
  Pallas kernels  21.8 us (37%)
  waiting for transfers between devices  11.6 us (19%)
  between operations  0.79 us (1%)
    ppermute x10, starting transfers between devices, from_pat(): lax.ppermute(x, 'pat', [(i, i ^ flip) for i in range(lax.axis_size('pat'))])  11.5 us
    ppermute x6, starting transfers between devices, from_core(): return lax.ppermute(x, 'feat', swap)  9.54 us
    ppermute x10, waiting for transfers between devices, from_pat(): lax.ppermute(x, 'pat', [(i, i ^ flip) for i in range(lax.axis_size('pat'))])  8.22 us
    pallas_call x4, Pallas kernels, step(): call(lambda *refs: bring(half, mine, offset, *refs), outs, 'bring', specs...  6.29 us
    pallas_call x1, Pallas kernels, per_device(): call(lambda *refs: bring_both(half, c0, *refs), [((rank, c1), f32), ((cel...  3.49 us
    pallas_call x2, Pallas kernels, per_device(): call(lambda *refs: weigh([0], *refs), summed, 'weigh', [VMEM] * (2 + len(...  2.8 us
    ppermute x1, starting transfers between devices, from_both(): lax.ppermute(x, ('pat', 'tm'), [(i, i ^ 2 * flip + 1) for i in range(coun...  2.31 us
    ppermute x3, starting transfers between devices, from_tm(): return lax.ppermute(x, 'tm', swap)  1.89 us
  transfers between devices with their start and end apart: 20, of which 12 were waited for; matrix products, arithmetic and copies ran while one was open for 0% of the time, Pallas kernels for 22%

profile of v5, /device:TPU:1, one launch (start us, length us, event | category | flops | bytes accessed | tf_op | source)
XLA Modules:
  0.0 59.4 jit_solution(15606393245452491112)
XLA Ops:
  0.6 0.0 copy-start
  0.6 0.0 copy-start.1
  0.7 2.2 %bring.4.refs_2_.refs_1_ = f32[1024,1024]{1,0:T(8,128)S(1)} custom-call(f32[1024,4096]{1,0:T(8,128)} %bitcast.4), custom_call_target="tpu_custom_call" | custom-call | tf_op jit(solution)/shard_map/bring/pallas_call | solution.py:380
  2.9 0.0 copy-done
  2.9 0.0 copy-done.1
  2.9 2.3 %bring.5 = (f32[32,1024]{1,0:T(8,128)S(1)}, f32[1024,1024]{1,0:T(8,128)S(1)}, bf16[64,1024]{1,0:T(8,128)(2,1)S(1)}, f32[32,128]{1,0:T(8,128)S(1)}) custom-call(f32[32,128]{1,0:T(8,128)S(1)} %copy-done, f32[8,32]{1,0:T(8,128)S(1)} %bitcast.3, f32[1024,1024]{1,0:T(8,128)S(1)} %bring.4.refs_2_.refs_1_, f32[1024,4096]{1,0:T(8,128)} %bitcast.5), custom_call_target="tpu_custom_call" | custom-call | flops 1024 | bytes 1024 | tf_op jit(solution)/shard_map/bring/pallas_call | solution.py:380
  5.2 1.5 %collective-permute-start.2 = (f32[32,1024]{1,0:T(8,128)S(1)}, f32[32,1024]{1,0:T(8,128)S(1)}, u32[]{:S(2)}, u32[]{:S(2)}) collective-permute-start(f32[32,1024]{1,0:T(8,128)S(1)} %get-tuple-element.42), channel_id=1, source_target_pairs={{0,2},{2,0},{1,3},{3,1},{4,6},{6,4},{5,7},{7,5},{8,10},{10,8},{9,1... | collective-permute-start | bytes 393224 | tf_op jit(solution)/shard_map/ppermute | solution.py:356
  6.7 0.1 collective-permute-start.3
  6.8 0.9 %bring.6.refs_1_ = f32[32,1024]{1,0:T(8,128)S(1)} custom-call(bf16[64,1024]{1,0:T(8,128)(2,1)S(1)} %get-tuple-element.38.refs_0_, f32[1024,1024]{1,0:T(8,128)S(1)} %get-tuple-element.39.refs_1_), custom_call_target="tpu_custom_call" | custom-call | flops 1024 | bytes 1024 | tf_op jit(solution)/shard_map/bring/pallas_call | solution.py:380
  7.7 0.2 collective-permute-done.3.core_ref
  7.9 0.0 collective-permute-done.2
  8.0 1.8 %collective-permute-start.4 = (f32[32,1152]{1,0:T(8,128)S(1)}, f32[32,1152]{1,0:T(8,128)S(1)}, u32[]{:S(2)}, u32[]{:S(2)}) collective-permute-start(f32[32,1152]{1,0:T(8,128)S(1)} %pad_maximum_fusion), channel_id=1, source_target_pairs={{0,1},{1,0},{2,3},{3,2},{4,5},{5,4},{6,7},{7,6},{8,9},{9,8},{10,11... | collective-permute-start | bytes 442376 | tf_op jit(solution)/shard_map/ppermute | solution.py:359
  9.8 3.5 %bring_both.1 = (f32[32,1024]{1,0:T(8,128)S(1)}, f32[1024,1024]{1,0:T(8,128)S(1)}, f32[1024,1024]{1,0:T(8,128)S(1)}) custom-call(bf16[64,1024]{1,0:T(8,128)(2,1)S(1)} %get-tuple-element.38.refs_0_, f32[32,1024]{1,0:T(8,128)S(1)} %bring.6.refs_1_, f32[1024,4096]{1,0:T(8,128)} %bitcast.6), custom_call_target="tpu_custom_call" | custom-call | flops 1024 | bytes 1024 | tf_op jit(solution)/shard_map/bring_both/pallas_call | solution.py:392
  13.3 0.6 collective-permute-start
  13.8 0.9 %bring.7 = f32[32,1024]{1,0:T(8,128)S(1)} custom-call(bf16[64,1024]{1,0:T(8,128)(2,1)S(1)} %get-tuple-element.38.refs_0_, f32[1024,1024]{1,0:T(8,128)S(1)} %get-tuple-element.40.refs_1_), custom_call_target="tpu_custom_call" | custom-call | flops 1024 | bytes 1024 | tf_op jit(solution)/shard_map/bring/pallas_call | solution.py:380
  14.7 0.1 collective-permute-done
  14.8 0.1 collective-permute-start.1
  14.9 0.0 collective-permute-done.4.theirs_ref.piece_ref
  15.0 0.4 collective-permute-start.5
  15.4 1.4 %weigh.3 = (f32[32,1024]{1,0:T(8,128)S(1)}, f32[32,32]{1,0:T(8,128)S(1)}) custom-call(f32[32,1024]{1,0:T(8,128)S(1)} %add_piece.2.refs_0_, f32[1024,1024]{1,0:T(8,128)S(1)} %get-tuple-element.39.refs_1_), custom_call_target="tpu_custom_call" | custom-call | flops 2013265920 | bytes 41943040 | tf_op jit(solution)/shard_map/weigh/pallas_call | solution.py:413
  16.8 0.0 collective-permute-done.5.refs_0_.refs_1_
  16.8 1.4 %weigh.4 = (f32[32,1024]{1,0:T(8,128)S(1)}, f32[32,32]{1,0:T(8,128)S(1)}) custom-call(f32[32,1024]{1,0:T(8,128)S(1)} %collective-permute-done.5.refs_0_.refs_1_, f32[1024,1024]{1,0:T(8,128)S(1)} %bring.4.refs_2_.refs_1_, f32[32,1024]{1,0:T(8,128)S(1)} %get-tuple-element.45.refs_2_, f32[32,32]{1,0:T(8,128)S(1)} %get-tuple-element.46.refs_3_), custom_call_target="tpu_custom_call" | custom-call | flops 2013265920 | bytes 41943040 | tf_op jit(solution)/shard_map/weigh/pallas_call | solution.py:417
  18.2 1.4 %collective-permute-done.1.theirs_ref = f32[32,1024]{1,0:T(8,128)S(1)} collective-permute-done((f32[32,1024]{1,0:T(8,128)S(1)}, f32[32,1024]{1,0:T(8,128)S(1)}, u32[]{:S(2)}, u32[]{:S(2)}) %collective-permute-start.1) | collective-permute-done | bytes 131104 | tf_op jit(solution)/shard_map/ppermute | solution.py:359
  19.7 1.3 %collective-permute-start.6 = (f32[32,1024]{1,0:T(8,128)S(1)}, f32[32,1024]{1,0:T(8,128)S(1)}, u32[]{:S(2)}, u32[]{:S(2)}) collective-permute-start(f32[32,1024]{1,0:T(8,128)S(1)} %add_piece.3.refs_0_.refs_2_), channel_id=1, source_target_pairs={{0,2},{2,0},{1,3},{3,1},{4,6},{6,4},{5,7},{7,5},{8,10},{10,8},{9,1... | collective-permute-start | bytes 393224 | tf_op jit(solution)/shard_map/ppermute | solution.py:356
  20.9 1.4 %weigh.5 = (f32[32,1024]{1,0:T(8,128)S(1)}, f32[32,32]{1,0:T(8,128)S(1)}) custom-call(f32[32,1024]{1,0:T(8,128)S(1)} %add_piece.3.refs_0_.refs_2_, f32[1024,1024]{1,0:T(8,128)S(1)} %get-tuple-element.40.refs_1_, f32[32,1024]{1,0:T(8,128)S(1)} %get-tuple-element.49.refs_2_, f32[32,32]{1,0:T(8,128)S(1)} %get-tuple-element.47.refs_0_.refs_3_), custom_call_target="tpu_custom_call" | custom-call | flops 2013265920 | bytes 41943040 | tf_op jit(solution)/shard_map/weigh/pallas_call | solution.py:413
  22.3 0.0 collective-permute-done.6.refs_0_.refs_3_
  22.3 1.5 %weigh_last.1 = (f32[40,256]{1,0:T(8,128)S(1)}, f32[40,256]{1,0:T(8,128)S(1)}, f32[40,256]{1,0:T(8,128)S(1)}, f32[40,256]{1,0:T(8,128)S(1)}) custom-call(f32[32,1024]{1,0:T(8,128)S(1)} %collective-permute-done.6.refs_0_.refs_3_, f32[1024,1024]{1,0:T(8,128)S(1)} %get-tuple-element.48.refs_1_, f32[32,1024]{1,0:T(8,128)S(1)} %get-tuple-element.50.refs_2_, ...), custom_call_target="tpu_custom_call" | custom-call | flops 2013265920 | bytes 41943040 | tf_op jit(solution)/shard_map/weigh_last/pallas_call | solution.py:420
  23.8 2.8 %collective-permute-start.7 = (f32[40,256]{1,0:T(8,128)S(1)}, f32[40,256]{1,0:T(8,128)S(1)}, u32[]{:S(2)}, u32[]{:S(2)}) collective-permute-start(f32[40,256]{1,0:T(8,128)S(1)} %get-tuple-element.53), channel_id=1, source_target_pairs={{0,8},{4,12},{8,0},{12,4},{16,24},{20,28},{24,16},{28,20},{32,40},... | collective-permute-start | bytes 122888 | tf_op jit(solution)/shard_map/ppermute | solution.py:362
  26.7 0.9 %collective-permute-start.8 = (f32[40,256]{1,0:T(8,128)S(1)}, f32[40,256]{1,0:T(8,128)S(1)}, u32[]{:S(2)}, u32[]{:S(2)}) collective-permute-start(f32[40,256]{1,0:T(8,128)S(1)} %get-tuple-element.56), channel_id=1, source_target_pairs={{0,12},{4,8},{8,4},{12,0},{16,28},{20,24},{24,20},{28,16},{32,44},... | collective-permute-start | bytes 122888 | tf_op jit(solution)/shard_map/ppermute | solution.py:362
  27.5 0.0 collective-permute-start.9
  27.5 1.1 %start_system.1 = (f32[32,32]{1,0:T(8,128)S(1)}, f32[32,32]{1,0:T(8,128)S(1)}) custom-call(f32[32,128]{1,0:T(8,128)S(1)} %copy-done, f32[32,128]{1,0:T(8,128)S(1)} %collective-permute-done.3.core_ref, f32[32,128]{1,0:T(8,128)S(1)} %get-tuple-element.44.time_ref, f32[32,1152]{1,0:T(8,128)S(1)} %collective-permute-done.4.theirs_ref.piece_ref), custom_call_target="tpu_custom_call" | custom-call | flops 1048576 | bytes 262144 | tf_op jit(solution)/shard_map/start_system/pallas_call | solution.py:424
  28.6 0.0 collective-permute-done.7.b_ref
  28.6 2.1 %collective-permute-done.8.a_ref = f32[40,256]{1,0:T(8,128)S(1)} collective-permute-done((f32[40,256]{1,0:T(8,128)S(1)}, f32[40,256]{1,0:T(8,128)S(1)}, u32[]{:S(2)}, u32[]{:S(2)}) %collective-permute-start.8) | collective-permute-done | bytes 40992 | tf_op jit(solution)/shard_map/ppermute | solution.py:362
  30.7 0.0 collective-permute-done.9
  30.8 3.2 %collective-permute-start.10 = (f32[40,256]{1,0:T(8,128)S(1)}, f32[40,256]{1,0:T(8,128)S(1)}, u32[]{:S(2)}, u32[]{:S(2)}) collective-permute-start(f32[40,256]{1,0:T(8,128)S(1)} %add_add_fusion.a_ref), channel_id=1, source_target_pairs={{0,64},{4,68},{8,72},{12,76},{16,80},{20,84},{24,88},{28,92},{32,9... | collective-permute-start | bytes 122888 | tf_op jit(solution)/shard_map/ppermute | solution.py:362
  33.9 0.8 %collective-permute-start.11 = (f32[40,256]{1,0:T(8,128)S(1)}, f32[40,256]{1,0:T(8,128)S(1)}, u32[]{:S(2)}, u32[]{:S(2)}) collective-permute-start(f32[40,256]{1,0:T(8,128)S(1)} %add_add_fusion.a_ref), channel_id=1, source_target_pairs={{0,96},{4,100},{8,104},{12,108},{16,112},{20,116},{24,120},{28,124... | collective-permute-start | bytes 122888 | tf_op jit(solution)/shard_map/ppermute | solution.py:362
  34.7 0.0 collective-permute-start.12
  34.7 0.5 solve_pat.1
  35.3 0.1 collective-permute-done.10.b_ref
  35.4 2.6 %collective-permute-done.11.a_ref = f32[40,256]{1,0:T(8,128)S(1)} collective-permute-done((f32[40,256]{1,0:T(8,128)S(1)}, f32[40,256]{1,0:T(8,128)S(1)}, u32[]{:S(2)}, u32[]{:S(2)}) %collective-permute-start.11) | collective-permute-done | bytes 40992 | tf_op jit(solution)/shard_map/ppermute | solution.py:362
  38.0 0.0 collective-permute-done.12.c_ref
  38.0 0.6 add_and_project.1
  38.6 2.3 %collective-permute-start.13 = (f32[40,256]{1,0:T(8,128)S(1)}, f32[40,256]{1,0:T(8,128)S(1)}, u32[]{:S(2)}, u32[]{:S(2)}) collective-permute-start(f32[40,256]{1,0:T(8,128)S(1)} %get-tuple-element.59.refs_0_.own_ref), channel_id=1, source_target_pairs={{0,17},{1,16},{4,21},{5,20},{8,25},{9,24},{12,29},{13,28},{16,1},{... | collective-permute-start | bytes 122888 | tf_op jit(solution)/shard_map/ppermute | solution.py:366
  40.9 1.1 %collective-permute-start.14 = (f32[40,256]{1,0:T(8,128)S(1)}, f32[40,256]{1,0:T(8,128)S(1)}, u32[]{:S(2)}, u32[]{:S(2)}) collective-permute-start(f32[40,256]{1,0:T(8,128)S(1)} %get-tuple-element.59.refs_0_.own_ref), channel_id=1, source_target_pairs={{0,16},{4,20},{8,24},{12,28},{16,0},{20,4},{24,8},{28,12},{32,48},... | collective-permute-start | bytes 122888 | tf_op jit(solution)/shard_map/ppermute | solution.py:362
  42.0 0.0 collective-permute-start.15
  42.0 0.7 %collective-permute-done.13.refs_1_.far_ref = f32[40,256]{1,0:T(8,128)S(1)} collective-permute-done((f32[40,256]{1,0:T(8,128)S(1)}, f32[40,256]{1,0:T(8,128)S(1)}, u32[]{:S(2)}, u32[]{:S(2)}) %collective-permute-start.13) | collective-permute-done | bytes 40992 | tf_op jit(solution)/shard_map/ppermute | solution.py:366
  42.7 0.9 %feat_system.1 = (f32[32,32]{1,0:T(8,128)S(1)}, f32[32,128]{1,0:T(8,128)S(1)}, f32[32,32]{1,0:T(8,128)S(1)}) custom-call(f32[40,256]{1,0:T(8,128)S(1)} %get-tuple-element.59.refs_0_.own_ref, f32[40,256]{1,0:T(8,128)S(1)} %collective-permute-done.13.refs_1_.far_ref, f32[32,32]{1,0:T(8,128)S(1)} %get-tuple-element.60.refs_2_), custom_call_target="tpu_custom_call" | custom-call | flops 1048576 | bytes 262144 | tf_op jit(solution)/shard_map/feat_system/pallas_call | solution.py:440
  43.6 1.6 %collective-permute-done.14.high_ref = f32[40,256]{1,0:T(8,128)S(1)} collective-permute-done((f32[40,256]{1,0:T(8,128)S(1)}, f32[40,256]{1,0:T(8,128)S(1)}, u32[]{:S(2)}, u32[]{:S(2)}) %collective-permute-start.14) | collective-permute-done | bytes 40992 | tf_op jit(solution)/shard_map/ppermute | solution.py:362
  45.2 0.1 scale_weighted.1.weighted_ref
  45.3 0.0 collective-permute-done.15.tm_ref
  45.3 0.6 %solve_feat.1.a_ref = f32[32,256]{1,0:T(8,128)S(1)} custom-call(f32[40,256]{1,0:T(8,128)S(1)} %get-tuple-element.59.refs_0_.own_ref, f32[40,256]{1,0:T(8,128)S(1)} %collective-permute-done.13.refs_1_.far_ref, f32[40,256]{1,0:T(8,128)S(1)} %collective-permute-done.14.high_ref, f32[8,128]{1,0:T(8,128)S(1)} %collective-permute-done.15.tm_ref, ...), custom_call_target="tpu_custom_call" | custom-call | flops 1048576 | bytes 262144 | tf_op jit(solution)/shard_map/solve_feat/pallas_call | solution.py:447
  45.9 1.3 %collective-permute-start.16 = (f32[32,256]{1,0:T(8,128)S(1)}, f32[32,256]{1,0:T(8,128)S(1)}, u32[]{:S(2)}, u32[]{:S(2)}) collective-permute-start(f32[32,256]{1,0:T(8,128)S(1)} %solve_feat.1.a_ref), channel_id=1, source_target_pairs={{0,8},{4,12},{8,0},{12,4},{16,24},{20,28},{24,16},{28,20},{32,40},... | collective-permute-start | bytes 98312 | tf_op jit(solution)/shard_map/ppermute | solution.py:362
  47.2 1.4 %collective-permute-start.17 = (f32[32,256]{1,0:T(8,128)S(1)}, f32[32,256]{1,0:T(8,128)S(1)}, u32[]{:S(2)}, u32[]{:S(2)}) collective-permute-start(f32[32,256]{1,0:T(8,128)S(1)} %solve_feat.1.a_ref), channel_id=1, source_target_pairs={{0,12},{4,8},{8,4},{12,0},{16,28},{20,24},{24,20},{28,16},{32,44},... | collective-permute-start | bytes 98312 | tf_op jit(solution)/shard_map/ppermute | solution.py:362
  48.6 0.1 collective-permute-start.18
  48.7 0.9 %scale_pat.1 = (f32[32,4096]{1,0:T(8,128)}, f32[8,128]{1,0:T(8,128)S(1)}) custom-call(f32[32,128]{1,0:T(8,128)S(1)} %get-tuple-element.61.scale_ref, f32[32,1024]{1,0:T(8,128)S(1)} %get-tuple-element.62.refs_0_, f32[32,1024]{1,0:T(8,128)S(1)} %get-tuple-element.63.refs_1_, f32[32,1024]{1,0:T(8,128)S(1)} %get-tuple-element.64.refs_2_, ...), custom_call_target="tpu_custom_call" | custom-call | flops 1048576 | bytes 262144 | tf_op jit(solution)/shard_map/scale_pat/pallas_call | solution.py:448
  49.6 0.7 %collective-permute-done.16.b_ref = f32[32,256]{1,0:T(8,128)S(1)} collective-permute-done((f32[32,256]{1,0:T(8,128)S(1)}, f32[32,256]{1,0:T(8,128)S(1)}, u32[]{:S(2)}, u32[]{:S(2)}) %collective-permute-start.16) | collective-permute-done | bytes 32800 | tf_op jit(solution)/shard_map/ppermute | solution.py:362
  50.3 0.9 %collective-permute-done.17.a_ref = f32[32,256]{1,0:T(8,128)S(1)} collective-permute-done((f32[32,256]{1,0:T(8,128)S(1)}, f32[32,256]{1,0:T(8,128)S(1)}, u32[]{:S(2)}, u32[]{:S(2)}) %collective-permute-start.17) | collective-permute-done | bytes 32800 | tf_op jit(solution)/shard_map/ppermute | solution.py:362
  51.2 0.1 collective-permute-done.18
  51.4 5.7 %collective-permute-start.19 = (f32[32,128]{1,0:T(8,128)S(1)}, f32[32,128]{1,0:T(8,128)S(1)}, u32[]{:S(2)}, u32[]{:S(2)}) collective-permute-start(f32[32,128]{1,0:T(8,128)S(1)} %get-tuple-element.74.refs_0_), channel_id=1, source_target_pairs={{0,2},{2,0},{1,3},{3,1},{4,6},{6,4},{5,7},{7,5},{8,10},{10,8},{9,1... | collective-permute-start | bytes 49160 | tf_op jit(solution)/shard_map/ppermute | solution.py:356
  57.0 0.8 %collective-permute-done.19.refs_1_ = f32[32,128]{1,0:T(8,128)S(1)} collective-permute-done((f32[32,128]{1,0:T(8,128)S(1)}, f32[32,128]{1,0:T(8,128)S(1)}, u32[]{:S(2)}, u32[]{:S(2)}) %collective-permute-start.19) | collective-permute-done | bytes 16416 | tf_op jit(solution)/shard_map/ppermute | solution.py:356
  57.9 1.6 %solve_time.1 = (f32[32,128]{1,0:T(8,128)}, f32[8,32]{1,0:T(8,128)}) custom-call(f32[32,128]{1,0:T(8,128)S(1)} %get-tuple-element.74.refs_0_, f32[32,128]{1,0:T(8,128)S(1)} %collective-permute-done.19.refs_1_, f32[32,128]{1,0:T(8,128)S(1)} %get-tuple-element.73.refs_2_, f32[32,32]{1,0:T(8,128)S(1)} %get-tuple-element.70.refs_3_), custom_call_target="tpu_custom_call" | custom-call | flops 1048576 | bytes 262144 | tf_op jit(solution)/shard_map/solve_time/pallas_call | solution.py:454
  (14 shorter events, 0.1 us)
Async XLA Ops:
  0.6 2.3 %copy-start = (f32[32,128]{1,0:T(8,128)S(1)}, f32[32,128]{1,0:T(8,128)}, u32[]{:S(2)}) copy-start(f32[32,128]{1,0:T(8,128)} %feat_ref.1) | copy-start | bytes 49156
  0.6 2.3 %copy-start.1 = (f32[32,8]{0,1:T(8,128)S(1)}, f32[32,8]{0,1:T(8,128)}, u32[]{:S(2)}) copy-start(f32[32,8]{0,1:T(8,128)} %param.5) | copy-start | bytes 3076
  5.2 2.7 %collective-permute-start.2 = (f32[32,1024]{1,0:T(8,128)S(1)}, f32[32,1024]{1,0:T(8,128)S(1)}, u32[]{:S(2)}, u32[]{:S(2)}) collective-permute-start(f32[32,1024]{1,0:T(8,128)S(1)} %get-tuple-element.42), channel_id=1, source_target_pairs={{0,2},{2,0},{1,3},{3,1},{4,6},{6,4},{5,7},{7,5},{8,10},{10,8},{9,1... | collective-permute-start | bytes 393224 | tf_op jit(solution)/shard_map/ppermute | solution.py:356
  6.7 1.2 %collective-permute-start.3 = (f32[32,128]{1,0:T(8,128)S(1)}, f32[32,128]{1,0:T(8,128)S(1)}, u32[]{:S(2)}, u32[]{:S(2)}) collective-permute-start(f32[32,128]{1,0:T(8,128)S(1)} %copy-done), channel_id=1, source_target_pairs={{0,2},{2,0},{1,3},{3,1},{4,6},{6,4},{5,7},{7,5},{8,10},{10,8},{9,1... | collective-permute-start | bytes 49160 | tf_op jit(solution)/shard_map/ppermute | solution.py:356
  8.0 7.0 %collective-permute-start.4 = (f32[32,1152]{1,0:T(8,128)S(1)}, f32[32,1152]{1,0:T(8,128)S(1)}, u32[]{:S(2)}, u32[]{:S(2)}) collective-permute-start(f32[32,1152]{1,0:T(8,128)S(1)} %pad_maximum_fusion), channel_id=1, source_target_pairs={{0,1},{1,0},{2,3},{3,2},{4,5},{5,4},{6,7},{7,6},{8,9},{9,8},{10,11... | collective-permute-start | bytes 442376 | tf_op jit(solution)/shard_map/ppermute | solution.py:359
  13.3 1.6 %collective-permute-start = (f32[32,1024]{1,0:T(8,128)S(1)}, f32[32,1024]{1,0:T(8,128)S(1)}, u32[]{:S(2)}, u32[]{:S(2)}) collective-permute-start(f32[32,1024]{1,0:T(8,128)S(1)} %get-tuple-element.41), channel_id=1, source_target_pairs={{0,2},{2,0},{1,3},{3,1},{4,6},{6,4},{5,7},{7,5},{8,10},{10,8},{9,1... | collective-permute-start | bytes 393224 | tf_op jit(solution)/shard_map/ppermute | solution.py:356
  14.8 4.8 %collective-permute-start.1 = (f32[32,1024]{1,0:T(8,128)S(1)}, f32[32,1024]{1,0:T(8,128)S(1)}, u32[]{:S(2)}, u32[]{:S(2)}) collective-permute-start(f32[32,1024]{1,0:T(8,128)S(1)} %add.18.refs_0_.mine_ref), channel_id=1, source_target_pairs={{0,1},{1,0},{2,3},{3,2},{4,5},{5,4},{6,7},{7,6},{8,9},{9,8},{10,11... | collective-permute-start | bytes 393224 | tf_op jit(solution)/shard_map/ppermute | solution.py:359
  15.0 1.9 %collective-permute-start.5 = (f32[32,1024]{1,0:T(8,128)S(1)}, f32[32,1024]{1,0:T(8,128)S(1)}, u32[]{:S(2)}, u32[]{:S(2)}) collective-permute-start(f32[32,1024]{1,0:T(8,128)S(1)} %add_piece.2.refs_0_), channel_id=1, source_target_pairs={{0,2},{2,0},{1,3},{3,1},{4,6},{6,4},{5,7},{7,5},{8,10},{10,8},{9,1... | collective-permute-start | bytes 393224 | tf_op jit(solution)/shard_map/ppermute | solution.py:356
  19.7 2.7 %collective-permute-start.6 = (f32[32,1024]{1,0:T(8,128)S(1)}, f32[32,1024]{1,0:T(8,128)S(1)}, u32[]{:S(2)}, u32[]{:S(2)}) collective-permute-start(f32[32,1024]{1,0:T(8,128)S(1)} %add_piece.3.refs_0_.refs_2_), channel_id=1, source_target_pairs={{0,2},{2,0},{1,3},{3,1},{4,6},{6,4},{5,7},{7,5},{8,10},{10,8},{9,1... | collective-permute-start | bytes 393224 | tf_op jit(solution)/shard_map/ppermute | solution.py:356
  23.8 4.8 %collective-permute-start.7 = (f32[40,256]{1,0:T(8,128)S(1)}, f32[40,256]{1,0:T(8,128)S(1)}, u32[]{:S(2)}, u32[]{:S(2)}) collective-permute-start(f32[40,256]{1,0:T(8,128)S(1)} %get-tuple-element.53), channel_id=1, source_target_pairs={{0,8},{4,12},{8,0},{12,4},{16,24},{20,28},{24,16},{28,20},{32,40},... | collective-permute-start | bytes 122888 | tf_op jit(solution)/shard_map/ppermute | solution.py:362
  26.7 4.1 %collective-permute-start.8 = (f32[40,256]{1,0:T(8,128)S(1)}, f32[40,256]{1,0:T(8,128)S(1)}, u32[]{:S(2)}, u32[]{:S(2)}) collective-permute-start(f32[40,256]{1,0:T(8,128)S(1)} %get-tuple-element.56), channel_id=1, source_target_pairs={{0,12},{4,8},{8,4},{12,0},{16,28},{20,24},{24,20},{28,16},{32,44},... | collective-permute-start | bytes 122888 | tf_op jit(solution)/shard_map/ppermute | solution.py:362
  27.5 3.2 %collective-permute-start.9 = (f32[40,256]{1,0:T(8,128)S(1)}, f32[40,256]{1,0:T(8,128)S(1)}, u32[]{:S(2)}, u32[]{:S(2)}) collective-permute-start(f32[40,256]{1,0:T(8,128)S(1)} %get-tuple-element.57), channel_id=1, source_target_pairs={{0,4},{4,0},{8,12},{12,8},{16,20},{20,16},{24,28},{28,24},{32,36},... | collective-permute-start | bytes 122888 | tf_op jit(solution)/shard_map/ppermute | solution.py:362
  30.8 4.6 %collective-permute-start.10 = (f32[40,256]{1,0:T(8,128)S(1)}, f32[40,256]{1,0:T(8,128)S(1)}, u32[]{:S(2)}, u32[]{:S(2)}) collective-permute-start(f32[40,256]{1,0:T(8,128)S(1)} %add_add_fusion.a_ref), channel_id=1, source_target_pairs={{0,64},{4,68},{8,72},{12,76},{16,80},{20,84},{24,88},{28,92},{32,9... | collective-permute-start | bytes 122888 | tf_op jit(solution)/shard_map/ppermute | solution.py:362
  33.9 4.1 %collective-permute-start.11 = (f32[40,256]{1,0:T(8,128)S(1)}, f32[40,256]{1,0:T(8,128)S(1)}, u32[]{:S(2)}, u32[]{:S(2)}) collective-permute-start(f32[40,256]{1,0:T(8,128)S(1)} %add_add_fusion.a_ref), channel_id=1, source_target_pairs={{0,96},{4,100},{8,104},{12,108},{16,112},{20,116},{24,120},{28,124... | collective-permute-start | bytes 122888 | tf_op jit(solution)/shard_map/ppermute | solution.py:362
  34.7 3.3 %collective-permute-start.12 = (f32[40,256]{1,0:T(8,128)S(1)}, f32[40,256]{1,0:T(8,128)S(1)}, u32[]{:S(2)}, u32[]{:S(2)}) collective-permute-start(f32[40,256]{1,0:T(8,128)S(1)} %add_add_fusion.a_ref), channel_id=1, source_target_pairs={{0,32},{4,36},{8,40},{12,44},{16,48},{20,52},{24,56},{28,60},{32,0... | collective-permute-start | bytes 122888 | tf_op jit(solution)/shard_map/ppermute | solution.py:362
  38.6 4.1 %collective-permute-start.13 = (f32[40,256]{1,0:T(8,128)S(1)}, f32[40,256]{1,0:T(8,128)S(1)}, u32[]{:S(2)}, u32[]{:S(2)}) collective-permute-start(f32[40,256]{1,0:T(8,128)S(1)} %get-tuple-element.59.refs_0_.own_ref), channel_id=1, source_target_pairs={{0,17},{1,16},{4,21},{5,20},{8,25},{9,24},{12,29},{13,28},{16,1},{... | collective-permute-start | bytes 122888 | tf_op jit(solution)/shard_map/ppermute | solution.py:366
  40.9 4.4 %collective-permute-start.14 = (f32[40,256]{1,0:T(8,128)S(1)}, f32[40,256]{1,0:T(8,128)S(1)}, u32[]{:S(2)}, u32[]{:S(2)}) collective-permute-start(f32[40,256]{1,0:T(8,128)S(1)} %get-tuple-element.59.refs_0_.own_ref), channel_id=1, source_target_pairs={{0,16},{4,20},{8,24},{12,28},{16,0},{20,4},{24,8},{28,12},{32,48},... | collective-permute-start | bytes 122888 | tf_op jit(solution)/shard_map/ppermute | solution.py:362
  42.0 3.4 %collective-permute-start.15 = (f32[8,128]{1,0:T(8,128)S(1)}, f32[8,128]{1,0:T(8,128)S(1)}, u32[]{:S(2)}, u32[]{:S(2)}) collective-permute-start(f32[8,128]{1,0:T(8,128)S(1)} %get-tuple-element.67), channel_id=1, source_target_pairs={{0,1},{1,0},{2,3},{3,2},{4,5},{5,4},{6,7},{7,6},{8,9},{9,8},{10,11... | collective-permute-start | bytes 12296 | tf_op jit(solution)/shard_map/ppermute | solution.py:359
  45.9 4.3 %collective-permute-start.16 = (f32[32,256]{1,0:T(8,128)S(1)}, f32[32,256]{1,0:T(8,128)S(1)}, u32[]{:S(2)}, u32[]{:S(2)}) collective-permute-start(f32[32,256]{1,0:T(8,128)S(1)} %solve_feat.1.a_ref), channel_id=1, source_target_pairs={{0,8},{4,12},{8,0},{12,4},{16,24},{20,28},{24,16},{28,20},{32,40},... | collective-permute-start | bytes 98312 | tf_op jit(solution)/shard_map/ppermute | solution.py:362
  47.2 4.0 %collective-permute-start.17 = (f32[32,256]{1,0:T(8,128)S(1)}, f32[32,256]{1,0:T(8,128)S(1)}, u32[]{:S(2)}, u32[]{:S(2)}) collective-permute-start(f32[32,256]{1,0:T(8,128)S(1)} %solve_feat.1.a_ref), channel_id=1, source_target_pairs={{0,12},{4,8},{8,4},{12,0},{16,28},{20,24},{24,20},{28,16},{32,44},... | collective-permute-start | bytes 98312 | tf_op jit(solution)/shard_map/ppermute | solution.py:362
  48.6 2.8 %collective-permute-start.18 = (f32[32,256]{1,0:T(8,128)S(1)}, f32[32,256]{1,0:T(8,128)S(1)}, u32[]{:S(2)}, u32[]{:S(2)}) collective-permute-start(f32[32,256]{1,0:T(8,128)S(1)} %solve_feat.1.a_ref), channel_id=1, source_target_pairs={{0,4},{4,0},{8,12},{12,8},{16,20},{20,16},{24,28},{28,24},{32,36},... | collective-permute-start | bytes 98312 | tf_op jit(solution)/shard_map/ppermute | solution.py:362
  51.4 6.5 %collective-permute-start.19 = (f32[32,128]{1,0:T(8,128)S(1)}, f32[32,128]{1,0:T(8,128)S(1)}, u32[]{:S(2)}, u32[]{:S(2)}) collective-permute-start(f32[32,128]{1,0:T(8,128)S(1)} %get-tuple-element.74.refs_0_), channel_id=1, source_target_pairs={{0,2},{2,0},{1,3},{3,1},{4,6},{6,4},{5,7},{7,5},{8,10},{10,8},{9,1... | collective-permute-start | bytes 49160 | tf_op jit(solution)/shard_map/ppermute | solution.py:356

commit v6 on v3

--- a/solution.py
+++ b/solution.py
@@ -45,7 +45,7 @@
     return jnp.where(lax.rem(iota(shape, 1), time) == iota(shape, 0), 1.0, 0.0).astype(f32)
 
 
-def eliminate(tiles, group=8):
+def eliminate(tiles, group=16):
     rank = tiles[0].shape[0]
     rows = iota((rank, LANES), 0)
     for start in range(0, rank, group):
@@ -94,59 +94,73 @@
 
 CHUNK = 256
 SHARES = (1024, 1024)
-LOADS = 8
-ROOM = 45
-
-
-def terms_of(mine, half, offset, hl_ref, block_ref, terms_ref, kept_ref, sems, build=None):
+LOADS = 4
+ROOM = 40
+
+
+def contract(hl_ref, there_ref, terms_ref):
     rank, patients = terms_ref.shape
-    cells = kept_ref.shape[0]
+    for c in range(0, patients, CHUNK):
+        total = None
+        for d in range(0, there_ref.shape[0], CHUNK):
+            hi, lo = split(there_ref[d : d + CHUNK, c : c + CHUNK])
+            both = quick(hl_ref[:, d : d + CHUNK], hi)
+            part = both[:rank] + both[rank:] + quick(hl_ref[:rank, d : d + CHUNK], lo)
+            total = part if total is None else total + part
+        terms_ref[:, c : c + CHUNK] = total
+
+
+def bring_both(half, offset, hl_ref, before_ref, block_ref, terms_ref, other_ref, mine_ref, sems, build=None):
     me = lax.axis_index("feat")
-    first = pl.multiple_of((me if mine else 1 - me) * half + offset, CHUNK)
+    rank = terms_ref.shape[0]
+    cells, patients = other_ref.shape
     step = cells // LOADS
     copies = []
-    for i in range(LOADS):
-        rows = pl.ds(i * step, step)
-        copies.append(
-            pltpu.make_async_copy(block_ref.at[rows, pl.ds(first, patients)], kept_ref.at[rows, :], sems.at[i])
-        )
+    for part, (who, kept_ref) in enumerate(((1 - me, other_ref), (me, mine_ref))):
+        first = pl.multiple_of(who * half + offset, CHUNK)
+        for i in range(LOADS):
+            rows = pl.ds(i * step, step)
+            copies.append(
+                pltpu.make_async_copy(
+                    block_ref.at[rows, pl.ds(first, patients)], kept_ref.at[rows, :], sems.at[part * LOADS + i]
+                )
+            )
     for copy in copies:
         copy.start()
     if build is not None:
         build()
-    for i, copy in enumerate(copies):
-        copy.wait()
+    for i in range(LOADS):
+        copies[i].wait()
         rows = slice(i * step, (i + 1) * step)
         for c in range(0, patients, CHUNK):
-            hi, lo = split(kept_ref[rows, c : c + CHUNK])
+            hi, lo = split(other_ref[rows, c : c + CHUNK])
             both = quick(hl_ref[:, rows], hi)
             part = both[:rank] + both[rank:] + quick(hl_ref[:rank, rows], lo)
             if i > 0:
                 part = part + terms_ref[:, c : c + CHUNK]
             terms_ref[:, c : c + CHUNK] = part
-
-
-def first_terms(half, init_ref, block_ref, terms_ref, kept_ref, hl_ref, time_out_ref, sems):
+    for copy in copies[LOADS:]:
+        copy.wait()
+
+
+def bring_first(half, init_ref, block_ref, terms_ref, other_ref, mine_ref, hl_ref, time_ref, sems):
     def build():
         rank = terms_ref.shape[0]
         feat, time = init_ref[:rank, :], init_ref[rank:, :rank]
         count = (feat.shape[1], time.shape[0])
         product = exact(feat, one_hot_feat(*count)) * exact(time, one_hot_time(*count), TN)
         hl_ref[...] = jnp.concatenate(split(product), axis=0)
-        time_out_ref[...] = jnp.concatenate([wide(time)] * (time_out_ref.shape[1] // LANES), axis=1)
-
-    terms_of(False, half, 0, hl_ref, block_ref, terms_ref, kept_ref, sems, build)
-
-
-def more_terms(mine, half, offset, hl_ref, before_ref, block_ref, terms_ref, kept_ref, sems):
-    terms_of(mine, half, offset, hl_ref, block_ref, terms_ref, kept_ref, sems)
-
-
-def start_system(init_ref, core_ref, piece_ref, inverse_ref, time_gram_ref):
+        below = jnp.zeros((rank - time.shape[0], LANES), f32)
+        time_ref[...] = jnp.concatenate([wide(time), below], axis=0)
+
+    bring_both(half, 0, hl_ref, None, block_ref, terms_ref, other_ref, mine_ref, sems, build)
+
+
+def start_system(feat_ref, core_ref, time_ref, piece_ref, inverse_ref, time_gram_ref):
     rank = inverse_ref.shape[0]
-    feat, feat_other = init_ref[:rank, :], core_ref[:rank, :]
-    time, time_other = init_ref[rank:, :rank], piece_ref[rank:, :rank]
-    time_gram = exact(time, time, TN) + exact(time_other, time_other, TN)
+    feat, feat_other = feat_ref[:rank, :], core_ref[:rank, :]
+    time, time_other = time_ref[...], piece_ref[:, piece_ref.shape[1] - LANES :]
+    time_gram = (exact(time, time, TN) + exact(time_other, time_other, TN))[:rank, :rank]
     system = (exact(feat, feat, NT) + exact(feat_other, feat_other, NT)) * time_gram
     inverse_ref[...] = invert(system)
     time_gram_ref[...] = time_gram
@@ -161,7 +175,7 @@
 
 def add_piece(mine_ref, theirs_ref, *refs):
     out_ref = refs[-1]
-    out_ref[...] = mine_ref[...] + theirs_ref[: mine_ref.shape[0], :]
+    out_ref[...] = mine_ref[...] + theirs_ref[:, : mine_ref.shape[1]]
 
 
 def pack(square):
@@ -222,7 +236,7 @@
     weighted = exact(inverse, total[:rank, :])
     gram = pack(exact(exact(inverse, unpack(total[rank:, :LANES])), inverse, NT))
     time_count = cells // feat_count
-    time = time_ref[:, :rank]
+    time = time_ref[:time_count, :rank]
     spread = exact(time, one_hot_time(feat_count, time_count), TN)
     terms = pack(exact(weighted * spread, one_hot_feat(feat_count, time_count), NT))
     out_ref[:rank, :] = weighted
@@ -323,25 +337,31 @@
     def load(patients):
         return dict(flops=patients, moved=patients)
 
-    def bring(body, patients, name, *operands, more=()):
-        return call(
-            body, [((rank, patients), f32), ((cells, patients), f32), *more], name,
-            [VMEM] * (len(operands) - 1) + [HBM], [pltpu.SemaphoreType.DMA((LOADS,))], ROOM, **load(patients),
-        )(*operands)
-
+    def long(patients):
+        return dict(flops=10 * 6 * rank * cells * patients, moved=40 * cells * patients)
+
+    def contracted(hl, there):
+        patients = there.shape[1]
+        return call(contract, [((rank, patients), f32)], "contract", [VMEM] * 2, **load(patients))(hl, there)[0]
+
+    c0, c1 = SHARES
+    both = [pltpu.SemaphoreType.DMA((2 * LOADS,))]
     init = jnp.concatenate([feat_init, jnp.pad(time_init.T, ((0, 0), (0, feat_dev - rank)))], axis=0)
-    c0, c1 = SHARES
-    away_0, kept_o0, hl, time_rows = bring(
-        lambda *refs: first_terms(half, *refs), c0, "first_terms", init, flat,
-        more=[((2 * rank, cells), bf16), ((8, c0), f32)],
-    )
+    away_0, kept_o0, kept_m0, hl, time_rows = call(
+        lambda *refs: bring_first(half, *refs),
+        [((rank, c0), f32), ((cells, c0), f32), ((cells, c0), f32), ((2 * rank, cells), bf16), ((rank, LANES), f32)],
+        "bring_first", [VMEM, HBM], both, ROOM, **load(c0),
+    )(init, flat)
     arrived_0, init_core = lax.optimization_barrier((from_core(away_0), from_core(init)))
-    own_0, kept_m0 = bring(lambda *refs: more_terms(True, half, 0, *refs), c0, "terms_own", hl, away_0, flat)
+    own_0 = contracted(hl, kept_m0)
     mine = [own_0 + arrived_0]
-    theirs = [from_tm(jnp.concatenate([mine[0], time_rows], axis=0))]
-    away_1, kept_o1 = bring(lambda *refs: more_terms(False, half, c0, *refs), c1, "terms_for_core", hl, own_0, flat)
+    theirs = [from_tm(jnp.concatenate([mine[0], time_rows], axis=1))]
+    away_1, kept_o1, kept_m1 = call(
+        lambda *refs: bring_both(half, c0, *refs), [((rank, c1), f32), ((cells, c1), f32), ((cells, c1), f32)],
+        "bring_both", [VMEM, VMEM, HBM], both, ROOM, **load(c1),
+    )(hl, own_0, flat)
     arrived_1 = from_core(away_1)
-    own_1, kept_m1 = bring(lambda *refs: more_terms(True, half, c0, *refs), c1, "terms_own", hl, away_1, flat)
+    own_1 = contracted(hl, kept_m1)
     mine.append(own_1 + arrived_1)
     theirs.append(from_tm(mine[1]))
     kept = [(kept_m0, kept_o0), (kept_m1, kept_o1)]
@@ -357,19 +377,19 @@
         )
         other = from_core(total)
         totals += [total, other]
-        sofar = call(lambda *refs: weigh([0], *refs), summed, "weigh", [VMEM] * (2 + len(sofar)), **dict(flops=10 * 6 * rank * cells * patients, moved=40 * cells * patients))(
+        sofar = call(lambda *refs: weigh([0], *refs), summed, "weigh", [VMEM] * (2 + len(sofar)), **long(patients))(
             total, kept[count][0], *sofar
         )
         if count < len(SHARES) - 1:
-            sofar = call(lambda *refs: weigh([0], *refs), summed, "weigh", [VMEM] * 4, **dict(flops=10 * 6 * rank * cells * patients, moved=40 * cells * patients))(
+            sofar = call(lambda *refs: weigh([0], *refs), summed, "weigh", [VMEM] * 4, **long(patients))(
                 other, kept[count][1], *sofar
             )
     quarters = call(
         lambda *refs: weigh_last([0], *refs), [payload] * 4, "weigh_last", [VMEM] * 4,
-        [pltpu.VMEM((rank, cells), f32), pltpu.VMEM((rank, rank), f32)], **dict(flops=10 * 6 * rank * cells * patients, moved=40 * cells * patients)
+        [pltpu.VMEM((rank, cells), f32), pltpu.VMEM((rank, rank), f32)], **long(patients)
     )(totals[-1], kept[-1][1], *sofar)
-    inverse, time_gram = call(start_system, [square] * 2, "start_system", [VMEM] * 3, **few)(
-        init, init_core, theirs[0]
+    inverse, time_gram = call(start_system, [square] * 2, "start_system", [VMEM] * 4, **few)(
+        init, init_core, time_rows, theirs[0]
     )
 
     def over_ring(mine, third, second, first, shape, *after):

time: 60.5 us -> 59.3 us (0.980)
  Pallas kernels: 22.5 us -> 21.1 us
    pallas_call x6, Pallas kernels: 12.4 us -> 11.4 us  [the longest x1 3.61 us: per_device(): call(lambda *refs: bring_first(half, *refs), [((rank, c0), f32), ((cells,...]
  transfers between devices with their start and end apart: 20 -> 20, of which waited for: 10 -> 12; matrix products, arithmetic and copies ran while one was open for 0% -> 0% of each run, Pallas kernels for 26% -> 22%
where the time goes in v6:
time: 59.3 us; the launch traced here: 59.1 us
  starting transfers between devices  25 us (42%)
  Pallas kernels  21.1 us (36%)
  waiting for transfers between devices  11.5 us (19%)
  other arithmetic  0.8 us (1%)
  between operations  0.75 us (1%)
    ppermute x10, starting transfers between devices, from_pat(): lax.ppermute(x, 'pat', [(i, i ^ flip) for i in range(lax.axis_size('pat'))])  11.3 us
    ppermute x6, starting transfers between devices, from_core(): return lax.ppermute(x, 'feat', swap)  9.53 us
    ppermute x10, waiting for transfers between devices, from_pat(): lax.ppermute(x, 'pat', [(i, i ^ flip) for i in range(lax.axis_size('pat'))])  8.22 us
    pallas_call x1, Pallas kernels, per_device(): call(lambda *refs: bring_first(half, *refs), [((rank, c0), f32), ((cells,...  3.61 us
    pallas_call x1, Pallas kernels, per_device(): call(lambda *refs: bring_both(half, c0, *refs), [((rank, c1), f32), ((cel...  3.49 us
    pallas_call x2, Pallas kernels, per_device(): call(lambda *refs: weigh([0], *refs), summed, 'weigh', [VMEM] * (2 + len(...  2.8 us
    ppermute x1, starting transfers between devices, from_both(): lax.ppermute(x, ('pat', 'tm'), [(i, i ^ 2 * flip + 1) for i in range(coun...  2.32 us
    ppermute x3, starting transfers between devices, from_tm(): return lax.ppermute(x, 'tm', swap)  1.89 us
  transfers between devices with their start and end apart: 20, of which 12 were waited for; matrix products, arithmetic and copies ran while one was open for 0% of the time, Pallas kernels for 22%

profile of v6, /device:TPU:1, one launch (start us, length us, event | category | flops | bytes accessed | tf_op | source)
XLA Modules:
  0.0 59.1 jit_solution(10442679456119892560)
XLA Ops:
  0.6 0.7 %select_maximum_fusion.refs_0_.feat_ref = f32[40,128]{1,0:T(8,128)S(1)} fusion(f32[8,32]{1,0:T(8,128)} %bitcast.5, f32[32,128]{1,0:T(8,128)} %param.4), kind=kLoop, calls=%fused_computation.3 | loop fusion | flops 15360 | bytes 37888 | tf_op jit(solution)/shard_map/concatenate | solution.py:349
  1.4 3.6 %bring_first.1 = (f32[32,1024]{1,0:T(8,128)S(1)}, f32[1024,1024]{1,0:T(8,128)S(1)}, f32[1024,1024]{1,0:T(8,128)S(1)}, bf16[64,1024]{1,0:T(8,128)(2,1)S(1)}, f32[32,128]{1,0:T(8,128)S(1)}) custom-call(f32[40,128]{1,0:T(8,128)S(1)} %select_maximum_fusion.refs_0_.feat_ref, f32[1024,4096]{1,0:T(8,128)} %bitcast.3), custom_call_target="tpu_custom_call" | custom-call | flops 1024 | bytes 1024 | tf_op jit(solution)/shard_map/bring_first/pallas_call | solution.py:350
  5.0 1.5 %collective-permute-start.2 = (f32[32,1024]{1,0:T(8,128)S(1)}, f32[32,1024]{1,0:T(8,128)S(1)}, u32[]{:S(2)}, u32[]{:S(2)}) collective-permute-start(f32[32,1024]{1,0:T(8,128)S(1)} %get-tuple-element.43), channel_id=1, source_target_pairs={{0,2},{2,0},{1,3},{3,1},{4,6},{6,4},{5,7},{7,5},{8,10},{10,8},{9,1... | collective-permute-start | bytes 393224 | tf_op jit(solution)/shard_map/ppermute | solution.py:323
  6.5 0.1 collective-permute-start.3
  6.6 0.9 %contract.2.refs_1_ = f32[32,1024]{1,0:T(8,128)S(1)} custom-call(bf16[64,1024]{1,0:T(8,128)(2,1)S(1)} %get-tuple-element.39.hl_ref.refs_0_, f32[1024,1024]{1,0:T(8,128)S(1)} %get-tuple-element.40.there_ref.refs_1_), custom_call_target="tpu_custom_call" | custom-call | flops 1024 | bytes 1024 | tf_op jit(solution)/shard_map/contract/pallas_call | solution.py:345
  7.4 0.2 collective-permute-done.3.core_ref
  7.7 0.0 collective-permute-done.2
  7.7 1.8 %collective-permute-start.4 = (f32[32,1152]{1,0:T(8,128)S(1)}, f32[32,1152]{1,0:T(8,128)S(1)}, u32[]{:S(2)}, u32[]{:S(2)}) collective-permute-start(f32[32,1152]{1,0:T(8,128)S(1)} %pad_maximum_fusion), channel_id=1, source_target_pairs={{0,1},{1,0},{2,3},{3,2},{4,5},{5,4},{6,7},{7,6},{8,9},{9,8},{10,11... | collective-permute-start | bytes 442376 | tf_op jit(solution)/shard_map/ppermute | solution.py:326
  9.5 3.5 %bring_both.1 = (f32[32,1024]{1,0:T(8,128)S(1)}, f32[1024,1024]{1,0:T(8,128)S(1)}, f32[1024,1024]{1,0:T(8,128)S(1)}) custom-call(bf16[64,1024]{1,0:T(8,128)(2,1)S(1)} %get-tuple-element.39.hl_ref.refs_0_, f32[32,1024]{1,0:T(8,128)S(1)} %contract.2.refs_1_, f32[1024,4096]{1,0:T(8,128)} %bitcast.4), custom_call_target="tpu_custom_call" | custom-call | flops 1024 | bytes 1024 | tf_op jit(solution)/shard_map/bring_both/pallas_call | solution.py:359
  13.0 0.6 collective-permute-start
  13.6 0.9 %contract.3 = f32[32,1024]{1,0:T(8,128)S(1)} custom-call(bf16[64,1024]{1,0:T(8,128)(2,1)S(1)} %get-tuple-element.39.hl_ref.refs_0_, f32[1024,1024]{1,0:T(8,128)S(1)} %get-tuple-element.41.there_ref.refs_1_), custom_call_target="tpu_custom_call" | custom-call | flops 1024 | bytes 1024 | tf_op jit(solution)/shard_map/contract/pallas_call | solution.py:345
  14.4 0.1 collective-permute-done
  14.6 0.1 collective-permute-start.1
  14.7 0.0 collective-permute-done.4.theirs_ref.piece_ref
  14.7 0.4 collective-permute-start.5
  15.2 1.4 %weigh.3 = (f32[32,1024]{1,0:T(8,128)S(1)}, f32[32,32]{1,0:T(8,128)S(1)}) custom-call(f32[32,1024]{1,0:T(8,128)S(1)} %add_piece.2.refs_0_, f32[1024,1024]{1,0:T(8,128)S(1)} %get-tuple-element.40.there_ref.refs_1_), custom_call_target="tpu_custom_call" | custom-call | flops 2013265920 | bytes 41943040 | tf_op jit(solution)/shard_map/weigh/pallas_call | solution.py:380
  16.6 0.0 collective-permute-done.5.refs_0_.refs_1_
  16.6 1.5 %weigh.4 = (f32[32,1024]{1,0:T(8,128)S(1)}, f32[32,32]{1,0:T(8,128)S(1)}) custom-call(f32[32,1024]{1,0:T(8,128)S(1)} %collective-permute-done.5.refs_0_.refs_1_, f32[1024,1024]{1,0:T(8,128)S(1)} %get-tuple-element.46.refs_1_, f32[32,1024]{1,0:T(8,128)S(1)} %get-tuple-element.47.refs_2_, f32[32,32]{1,0:T(8,128)S(1)} %get-tuple-element.48.refs_3_), custom_call_target="tpu_custom_call" | custom-call | flops 2013265920 | bytes 41943040 | tf_op jit(solution)/shard_map/weigh/pallas_call | solution.py:384
  18.1 1.3 %collective-permute-done.1.theirs_ref = f32[32,1024]{1,0:T(8,128)S(1)} collective-permute-done((f32[32,1024]{1,0:T(8,128)S(1)}, f32[32,1024]{1,0:T(8,128)S(1)}, u32[]{:S(2)}, u32[]{:S(2)}) %collective-permute-start.1) | collective-permute-done | bytes 131104 | tf_op jit(solution)/shard_map/ppermute | solution.py:326
  19.4 1.3 %collective-permute-start.6 = (f32[32,1024]{1,0:T(8,128)S(1)}, f32[32,1024]{1,0:T(8,128)S(1)}, u32[]{:S(2)}, u32[]{:S(2)}) collective-permute-start(f32[32,1024]{1,0:T(8,128)S(1)} %add_piece.3.refs_0_.refs_2_), channel_id=1, source_target_pairs={{0,2},{2,0},{1,3},{3,1},{4,6},{6,4},{5,7},{7,5},{8,10},{10,8},{9,1... | collective-permute-start | bytes 393224 | tf_op jit(solution)/shard_map/ppermute | solution.py:323
  20.7 1.4 %weigh.5 = (f32[32,1024]{1,0:T(8,128)S(1)}, f32[32,32]{1,0:T(8,128)S(1)}) custom-call(f32[32,1024]{1,0:T(8,128)S(1)} %add_piece.3.refs_0_.refs_2_, f32[1024,1024]{1,0:T(8,128)S(1)} %get-tuple-element.41.there_ref.refs_1_, f32[32,1024]{1,0:T(8,128)S(1)} %get-tuple-element.51.refs_2_, f32[32,32]{1,0:T(8,128)S(1)} %get-tuple-element.49.refs_0_.refs_3_), custom_call_target="tpu_custom_call" | custom-call | flops 2013265920 | bytes 41943040 | tf_op jit(solution)/shard_map/weigh/pallas_call | solution.py:380
  22.1 0.0 collective-permute-done.6.refs_0_.refs_3_
  22.1 1.6 %weigh_last.1 = (f32[40,256]{1,0:T(8,128)S(1)}, f32[40,256]{1,0:T(8,128)S(1)}, f32[40,256]{1,0:T(8,128)S(1)}, f32[40,256]{1,0:T(8,128)S(1)}) custom-call(f32[32,1024]{1,0:T(8,128)S(1)} %collective-permute-done.6.refs_0_.refs_3_, f32[1024,1024]{1,0:T(8,128)S(1)} %get-tuple-element.50.refs_1_, f32[32,1024]{1,0:T(8,128)S(1)} %get-tuple-element.52.refs_2_, ...), custom_call_target="tpu_custom_call" | custom-call | flops 2013265920 | bytes 41943040 | tf_op jit(solution)/shard_map/weigh_last/pallas_call | solution.py:387
  23.7 2.8 %collective-permute-start.7 = (f32[40,256]{1,0:T(8,128)S(1)}, f32[40,256]{1,0:T(8,128)S(1)}, u32[]{:S(2)}, u32[]{:S(2)}) collective-permute-start(f32[40,256]{1,0:T(8,128)S(1)} %get-tuple-element.55), channel_id=1, source_target_pairs={{0,8},{4,12},{8,0},{12,4},{16,24},{20,28},{24,16},{28,20},{32,40},... | collective-permute-start | bytes 122888 | tf_op jit(solution)/shard_map/ppermute | solution.py:329
  26.5 0.9 %collective-permute-start.8 = (f32[40,256]{1,0:T(8,128)S(1)}, f32[40,256]{1,0:T(8,128)S(1)}, u32[]{:S(2)}, u32[]{:S(2)}) collective-permute-start(f32[40,256]{1,0:T(8,128)S(1)} %get-tuple-element.58), channel_id=1, source_target_pairs={{0,12},{4,8},{8,4},{12,0},{16,28},{20,24},{24,20},{28,16},{32,44},... | collective-permute-start | bytes 122888 | tf_op jit(solution)/shard_map/ppermute | solution.py:329
  27.4 0.0 collective-permute-start.9
  27.4 1.1 %start_system.1 = (f32[32,32]{1,0:T(8,128)S(1)}, f32[32,32]{1,0:T(8,128)S(1)}) custom-call(f32[40,128]{1,0:T(8,128)S(1)} %select_maximum_fusion.refs_0_.feat_ref, f32[40,128]{1,0:T(8,128)S(1)} %collective-permute-done.3.core_ref, f32[32,128]{1,0:T(8,128)S(1)} %get-tuple-element.45.time_ref, f32[32,1152]{1,0:T(8,128)S(1)} %collective-permute-done.4.theirs_ref.piece_ref), custom_call_target="tpu_custom_call" | custom-call | flops 1048576 | bytes 262144 | tf_op jit(solution)/shard_map/start_system/pallas_call | solution.py:391
  28.4 0.0 collective-permute-done.7.b_ref
  28.5 2.1 %collective-permute-done.8.a_ref = f32[40,256]{1,0:T(8,128)S(1)} collective-permute-done((f32[40,256]{1,0:T(8,128)S(1)}, f32[40,256]{1,0:T(8,128)S(1)}, u32[]{:S(2)}, u32[]{:S(2)}) %collective-permute-start.8) | collective-permute-done | bytes 40992 | tf_op jit(solution)/shard_map/ppermute | solution.py:329
  30.6 0.0 collective-permute-done.9
  30.6 3.0 %collective-permute-start.10 = (f32[40,256]{1,0:T(8,128)S(1)}, f32[40,256]{1,0:T(8,128)S(1)}, u32[]{:S(2)}, u32[]{:S(2)}) collective-permute-start(f32[40,256]{1,0:T(8,128)S(1)} %add_add_fusion.a_ref), channel_id=1, source_target_pairs={{0,64},{4,68},{8,72},{12,76},{16,80},{20,84},{24,88},{28,92},{32,9... | collective-permute-start | bytes 122888 | tf_op jit(solution)/shard_map/ppermute | solution.py:329
  33.6 0.8 %collective-permute-start.11 = (f32[40,256]{1,0:T(8,128)S(1)}, f32[40,256]{1,0:T(8,128)S(1)}, u32[]{:S(2)}, u32[]{:S(2)}) collective-permute-start(f32[40,256]{1,0:T(8,128)S(1)} %add_add_fusion.a_ref), channel_id=1, source_target_pairs={{0,96},{4,100},{8,104},{12,108},{16,112},{20,116},{24,120},{28,124... | collective-permute-start | bytes 122888 | tf_op jit(solution)/shard_map/ppermute | solution.py:329
  34.4 0.0 collective-permute-start.12
  34.4 0.5 solve_pat.1
  34.9 0.1 collective-permute-done.10.b_ref
  35.0 2.6 %collective-permute-done.11.a_ref = f32[40,256]{1,0:T(8,128)S(1)} collective-permute-done((f32[40,256]{1,0:T(8,128)S(1)}, f32[40,256]{1,0:T(8,128)S(1)}, u32[]{:S(2)}, u32[]{:S(2)}) %collective-permute-start.11) | collective-permute-done | bytes 40992 | tf_op jit(solution)/shard_map/ppermute | solution.py:329
  37.6 0.0 collective-permute-done.12.c_ref
  37.7 0.6 add_and_project.1
  38.2 2.3 %collective-permute-start.13 = (f32[40,256]{1,0:T(8,128)S(1)}, f32[40,256]{1,0:T(8,128)S(1)}, u32[]{:S(2)}, u32[]{:S(2)}) collective-permute-start(f32[40,256]{1,0:T(8,128)S(1)} %get-tuple-element.61.refs_0_.own_ref), channel_id=1, source_target_pairs={{0,17},{1,16},{4,21},{5,20},{8,25},{9,24},{12,29},{13,28},{16,1},{... | collective-permute-start | bytes 122888 | tf_op jit(solution)/shard_map/ppermute | solution.py:333
  40.5 1.1 %collective-permute-start.14 = (f32[40,256]{1,0:T(8,128)S(1)}, f32[40,256]{1,0:T(8,128)S(1)}, u32[]{:S(2)}, u32[]{:S(2)}) collective-permute-start(f32[40,256]{1,0:T(8,128)S(1)} %get-tuple-element.61.refs_0_.own_ref), channel_id=1, source_target_pairs={{0,16},{4,20},{8,24},{12,28},{16,0},{20,4},{24,8},{28,12},{32,48},... | collective-permute-start | bytes 122888 | tf_op jit(solution)/shard_map/ppermute | solution.py:329
  41.6 0.0 collective-permute-start.15
  41.6 0.7 %collective-permute-done.13.refs_1_.far_ref = f32[40,256]{1,0:T(8,128)S(1)} collective-permute-done((f32[40,256]{1,0:T(8,128)S(1)}, f32[40,256]{1,0:T(8,128)S(1)}, u32[]{:S(2)}, u32[]{:S(2)}) %collective-permute-start.13) | collective-permute-done | bytes 40992 | tf_op jit(solution)/shard_map/ppermute | solution.py:333
  42.4 0.9 %feat_system.1 = (f32[32,32]{1,0:T(8,128)S(1)}, f32[32,128]{1,0:T(8,128)S(1)}, f32[32,32]{1,0:T(8,128)S(1)}) custom-call(f32[40,256]{1,0:T(8,128)S(1)} %get-tuple-element.61.refs_0_.own_ref, f32[40,256]{1,0:T(8,128)S(1)} %collective-permute-done.13.refs_1_.far_ref, f32[32,32]{1,0:T(8,128)S(1)} %get-tuple-element.62.refs_2_), custom_call_target="tpu_custom_call" | custom-call | flops 1048576 | bytes 262144 | tf_op jit(solution)/shard_map/feat_system/pallas_call | solution.py:407
  43.3 1.6 %collective-permute-done.14.high_ref = f32[40,256]{1,0:T(8,128)S(1)} collective-permute-done((f32[40,256]{1,0:T(8,128)S(1)}, f32[40,256]{1,0:T(8,128)S(1)}, u32[]{:S(2)}, u32[]{:S(2)}) %collective-permute-start.14) | collective-permute-done | bytes 40992 | tf_op jit(solution)/shard_map/ppermute | solution.py:329
  44.9 0.1 scale_weighted.1.weighted_ref
  45.0 0.0 collective-permute-done.15.tm_ref
  45.0 0.6 %solve_feat.1.a_ref = f32[32,256]{1,0:T(8,128)S(1)} custom-call(f32[40,256]{1,0:T(8,128)S(1)} %get-tuple-element.61.refs_0_.own_ref, f32[40,256]{1,0:T(8,128)S(1)} %collective-permute-done.13.refs_1_.far_ref, f32[40,256]{1,0:T(8,128)S(1)} %collective-permute-done.14.high_ref, f32[8,128]{1,0:T(8,128)S(1)} %collective-permute-done.15.tm_ref, ...), custom_call_target="tpu_custom_call" | custom-call | flops 1048576 | bytes 262144 | tf_op jit(solution)/shard_map/solve_feat/pallas_call | solution.py:414
  45.6 1.3 %collective-permute-start.16 = (f32[32,256]{1,0:T(8,128)S(1)}, f32[32,256]{1,0:T(8,128)S(1)}, u32[]{:S(2)}, u32[]{:S(2)}) collective-permute-start(f32[32,256]{1,0:T(8,128)S(1)} %solve_feat.1.a_ref), channel_id=1, source_target_pairs={{0,8},{4,12},{8,0},{12,4},{16,24},{20,28},{24,16},{28,20},{32,40},... | collective-permute-start | bytes 98312 | tf_op jit(solution)/shard_map/ppermute | solution.py:329
  46.9 1.4 %collective-permute-start.17 = (f32[32,256]{1,0:T(8,128)S(1)}, f32[32,256]{1,0:T(8,128)S(1)}, u32[]{:S(2)}, u32[]{:S(2)}) collective-permute-start(f32[32,256]{1,0:T(8,128)S(1)} %solve_feat.1.a_ref), channel_id=1, source_target_pairs={{0,12},{4,8},{8,4},{12,0},{16,28},{20,24},{24,20},{28,16},{32,44},... | collective-permute-start | bytes 98312 | tf_op jit(solution)/shard_map/ppermute | solution.py:329
  48.2 0.1 collective-permute-start.18
  48.3 0.9 %scale_pat.1 = (f32[32,4096]{1,0:T(8,128)}, f32[8,128]{1,0:T(8,128)S(1)}) custom-call(f32[32,128]{1,0:T(8,128)S(1)} %get-tuple-element.63.scale_ref, f32[32,1024]{1,0:T(8,128)S(1)} %get-tuple-element.64.refs_0_, f32[32,1024]{1,0:T(8,128)S(1)} %get-tuple-element.65.refs_1_, f32[32,1024]{1,0:T(8,128)S(1)} %get-tuple-element.66.refs_2_, ...), custom_call_target="tpu_custom_call" | custom-call | flops 1048576 | bytes 262144 | tf_op jit(solution)/shard_map/scale_pat/pallas_call | solution.py:415
  49.2 0.7 %collective-permute-done.16.b_ref = f32[32,256]{1,0:T(8,128)S(1)} collective-permute-done((f32[32,256]{1,0:T(8,128)S(1)}, f32[32,256]{1,0:T(8,128)S(1)}, u32[]{:S(2)}, u32[]{:S(2)}) %collective-permute-start.16) | collective-permute-done | bytes 32800 | tf_op jit(solution)/shard_map/ppermute | solution.py:329
  50.0 0.9 %collective-permute-done.17.a_ref = f32[32,256]{1,0:T(8,128)S(1)} collective-permute-done((f32[32,256]{1,0:T(8,128)S(1)}, f32[32,256]{1,0:T(8,128)S(1)}, u32[]{:S(2)}, u32[]{:S(2)}) %collective-permute-start.17) | collective-permute-done | bytes 32800 | tf_op jit(solution)/shard_map/ppermute | solution.py:329
  50.9 0.1 collective-permute-done.18
  51.0 5.7 %collective-permute-start.19 = (f32[32,128]{1,0:T(8,128)S(1)}, f32[32,128]{1,0:T(8,128)S(1)}, u32[]{:S(2)}, u32[]{:S(2)}) collective-permute-start(f32[32,128]{1,0:T(8,128)S(1)} %get-tuple-element.76.refs_0_), channel_id=1, source_target_pairs={{0,2},{2,0},{1,3},{3,1},{4,6},{6,4},{5,7},{7,5},{8,10},{10,8},{9,1... | collective-permute-start | bytes 49160 | tf_op jit(solution)/shard_map/ppermute | solution.py:323
  56.7 0.8 %collective-permute-done.19.refs_1_ = f32[32,128]{1,0:T(8,128)S(1)} collective-permute-done((f32[32,128]{1,0:T(8,128)S(1)}, f32[32,128]{1,0:T(8,128)S(1)}, u32[]{:S(2)}, u32[]{:S(2)}) %collective-permute-start.19) | collective-permute-done | bytes 16416 | tf_op jit(solution)/shard_map/ppermute | solution.py:323
  57.5 1.6 %solve_time.1 = (f32[32,128]{1,0:T(8,128)}, f32[8,32]{1,0:T(8,128)}) custom-call(f32[32,128]{1,0:T(8,128)S(1)} %get-tuple-element.76.refs_0_, f32[32,128]{1,0:T(8,128)S(1)} %collective-permute-done.19.refs_1_, f32[32,128]{1,0:T(8,128)S(1)} %get-tuple-element.75.refs_2_, f32[32,32]{1,0:T(8,128)S(1)} %get-tuple-element.72.refs_3_), custom_call_target="tpu_custom_call" | custom-call | flops 1048576 | bytes 262144 | tf_op jit(solution)/shard_map/solve_time/pallas_call | solution.py:421
  (14 shorter events, 0.1 us)
Async XLA Ops:
  5.0 2.7 %collective-permute-start.2 = (f32[32,1024]{1,0:T(8,128)S(1)}, f32[32,1024]{1,0:T(8,128)S(1)}, u32[]{:S(2)}, u32[]{:S(2)}) collective-permute-start(f32[32,1024]{1,0:T(8,128)S(1)} %get-tuple-element.43), channel_id=1, source_target_pairs={{0,2},{2,0},{1,3},{3,1},{4,6},{6,4},{5,7},{7,5},{8,10},{10,8},{9,1... | collective-permute-start | bytes 393224 | tf_op jit(solution)/shard_map/ppermute | solution.py:323
  6.5 1.2 %collective-permute-start.3 = (f32[40,128]{1,0:T(8,128)S(1)}, f32[40,128]{1,0:T(8,128)S(1)}, u32[]{:S(2)}, u32[]{:S(2)}) collective-permute-start(f32[40,128]{1,0:T(8,128)S(1)} %select_maximum_fusion.refs_0_.feat_ref), channel_id=1, source_target_pairs={{0,2},{2,0},{1,3},{3,1},{4,6},{6,4},{5,7},{7,5},{8,10},{10,8},{9,1... | collective-permute-start | bytes 61448 | tf_op jit(solution)/shard_map/ppermute | solution.py:323
  7.7 7.0 %collective-permute-start.4 = (f32[32,1152]{1,0:T(8,128)S(1)}, f32[32,1152]{1,0:T(8,128)S(1)}, u32[]{:S(2)}, u32[]{:S(2)}) collective-permute-start(f32[32,1152]{1,0:T(8,128)S(1)} %pad_maximum_fusion), channel_id=1, source_target_pairs={{0,1},{1,0},{2,3},{3,2},{4,5},{5,4},{6,7},{7,6},{8,9},{9,8},{10,11... | collective-permute-start | bytes 442376 | tf_op jit(solution)/shard_map/ppermute | solution.py:326
  13.0 1.6 %collective-permute-start = (f32[32,1024]{1,0:T(8,128)S(1)}, f32[32,1024]{1,0:T(8,128)S(1)}, u32[]{:S(2)}, u32[]{:S(2)}) collective-permute-start(f32[32,1024]{1,0:T(8,128)S(1)} %get-tuple-element.42), channel_id=1, source_target_pairs={{0,2},{2,0},{1,3},{3,1},{4,6},{6,4},{5,7},{7,5},{8,10},{10,8},{9,1... | collective-permute-start | bytes 393224 | tf_op jit(solution)/shard_map/ppermute | solution.py:323
  14.6 4.8 %collective-permute-start.1 = (f32[32,1024]{1,0:T(8,128)S(1)}, f32[32,1024]{1,0:T(8,128)S(1)}, u32[]{:S(2)}, u32[]{:S(2)}) collective-permute-start(f32[32,1024]{1,0:T(8,128)S(1)} %add.20.refs_0_.mine_ref), channel_id=1, source_target_pairs={{0,1},{1,0},{2,3},{3,2},{4,5},{5,4},{6,7},{7,6},{8,9},{9,8},{10,11... | collective-permute-start | bytes 393224 | tf_op jit(solution)/shard_map/ppermute | solution.py:326
  14.7 1.8 %collective-permute-start.5 = (f32[32,1024]{1,0:T(8,128)S(1)}, f32[32,1024]{1,0:T(8,128)S(1)}, u32[]{:S(2)}, u32[]{:S(2)}) collective-permute-start(f32[32,1024]{1,0:T(8,128)S(1)} %add_piece.2.refs_0_), channel_id=1, source_target_pairs={{0,2},{2,0},{1,3},{3,1},{4,6},{6,4},{5,7},{7,5},{8,10},{10,8},{9,1... | collective-permute-start | bytes 393224 | tf_op jit(solution)/shard_map/ppermute | solution.py:323
  19.4 2.7 %collective-permute-start.6 = (f32[32,1024]{1,0:T(8,128)S(1)}, f32[32,1024]{1,0:T(8,128)S(1)}, u32[]{:S(2)}, u32[]{:S(2)}) collective-permute-start(f32[32,1024]{1,0:T(8,128)S(1)} %add_piece.3.refs_0_.refs_2_), channel_id=1, source_target_pairs={{0,2},{2,0},{1,3},{3,1},{4,6},{6,4},{5,7},{7,5},{8,10},{10,8},{9,1... | collective-permute-start | bytes 393224 | tf_op jit(solution)/shard_map/ppermute | solution.py:323
  23.7 4.8 %collective-permute-start.7 = (f32[40,256]{1,0:T(8,128)S(1)}, f32[40,256]{1,0:T(8,128)S(1)}, u32[]{:S(2)}, u32[]{:S(2)}) collective-permute-start(f32[40,256]{1,0:T(8,128)S(1)} %get-tuple-element.55), channel_id=1, source_target_pairs={{0,8},{4,12},{8,0},{12,4},{16,24},{20,28},{24,16},{28,20},{32,40},... | collective-permute-start | bytes 122888 | tf_op jit(solution)/shard_map/ppermute | solution.py:329
  26.5 4.1 %collective-permute-start.8 = (f32[40,256]{1,0:T(8,128)S(1)}, f32[40,256]{1,0:T(8,128)S(1)}, u32[]{:S(2)}, u32[]{:S(2)}) collective-permute-start(f32[40,256]{1,0:T(8,128)S(1)} %get-tuple-element.58), channel_id=1, source_target_pairs={{0,12},{4,8},{8,4},{12,0},{16,28},{20,24},{24,20},{28,16},{32,44},... | collective-permute-start | bytes 122888 | tf_op jit(solution)/shard_map/ppermute | solution.py:329
  27.4 3.2 %collective-permute-start.9 = (f32[40,256]{1,0:T(8,128)S(1)}, f32[40,256]{1,0:T(8,128)S(1)}, u32[]{:S(2)}, u32[]{:S(2)}) collective-permute-start(f32[40,256]{1,0:T(8,128)S(1)} %get-tuple-element.59), channel_id=1, source_target_pairs={{0,4},{4,0},{8,12},{12,8},{16,20},{20,16},{24,28},{28,24},{32,36},... | collective-permute-start | bytes 122888 | tf_op jit(solution)/shard_map/ppermute | solution.py:329
  30.6 4.4 %collective-permute-start.10 = (f32[40,256]{1,0:T(8,128)S(1)}, f32[40,256]{1,0:T(8,128)S(1)}, u32[]{:S(2)}, u32[]{:S(2)}) collective-permute-start(f32[40,256]{1,0:T(8,128)S(1)} %add_add_fusion.a_ref), channel_id=1, source_target_pairs={{0,64},{4,68},{8,72},{12,76},{16,80},{20,84},{24,88},{28,92},{32,9... | collective-permute-start | bytes 122888 | tf_op jit(solution)/shard_map/ppermute | solution.py:329
  33.6 4.1 %collective-permute-start.11 = (f32[40,256]{1,0:T(8,128)S(1)}, f32[40,256]{1,0:T(8,128)S(1)}, u32[]{:S(2)}, u32[]{:S(2)}) collective-permute-start(f32[40,256]{1,0:T(8,128)S(1)} %add_add_fusion.a_ref), channel_id=1, source_target_pairs={{0,96},{4,100},{8,104},{12,108},{16,112},{20,116},{24,120},{28,124... | collective-permute-start | bytes 122888 | tf_op jit(solution)/shard_map/ppermute | solution.py:329
  34.4 3.3 %collective-permute-start.12 = (f32[40,256]{1,0:T(8,128)S(1)}, f32[40,256]{1,0:T(8,128)S(1)}, u32[]{:S(2)}, u32[]{:S(2)}) collective-permute-start(f32[40,256]{1,0:T(8,128)S(1)} %add_add_fusion.a_ref), channel_id=1, source_target_pairs={{0,32},{4,36},{8,40},{12,44},{16,48},{20,52},{24,56},{28,60},{32,0... | collective-permute-start | bytes 122888 | tf_op jit(solution)/shard_map/ppermute | solution.py:329
  38.2 4.1 %collective-permute-start.13 = (f32[40,256]{1,0:T(8,128)S(1)}, f32[40,256]{1,0:T(8,128)S(1)}, u32[]{:S(2)}, u32[]{:S(2)}) collective-permute-start(f32[40,256]{1,0:T(8,128)S(1)} %get-tuple-element.61.refs_0_.own_ref), channel_id=1, source_target_pairs={{0,17},{1,16},{4,21},{5,20},{8,25},{9,24},{12,29},{13,28},{16,1},{... | collective-permute-start | bytes 122888 | tf_op jit(solution)/shard_map/ppermute | solution.py:333
  40.5 4.4 %collective-permute-start.14 = (f32[40,256]{1,0:T(8,128)S(1)}, f32[40,256]{1,0:T(8,128)S(1)}, u32[]{:S(2)}, u32[]{:S(2)}) collective-permute-start(f32[40,256]{1,0:T(8,128)S(1)} %get-tuple-element.61.refs_0_.own_ref), channel_id=1, source_target_pairs={{0,16},{4,20},{8,24},{12,28},{16,0},{20,4},{24,8},{28,12},{32,48},... | collective-permute-start | bytes 122888 | tf_op jit(solution)/shard_map/ppermute | solution.py:329
  41.6 3.3 %collective-permute-start.15 = (f32[8,128]{1,0:T(8,128)S(1)}, f32[8,128]{1,0:T(8,128)S(1)}, u32[]{:S(2)}, u32[]{:S(2)}) collective-permute-start(f32[8,128]{1,0:T(8,128)S(1)} %get-tuple-element.69), channel_id=1, source_target_pairs={{0,1},{1,0},{2,3},{3,2},{4,5},{5,4},{6,7},{7,6},{8,9},{9,8},{10,11... | collective-permute-start | bytes 12296 | tf_op jit(solution)/shard_map/ppermute | solution.py:326
  45.6 4.3 %collective-permute-start.16 = (f32[32,256]{1,0:T(8,128)S(1)}, f32[32,256]{1,0:T(8,128)S(1)}, u32[]{:S(2)}, u32[]{:S(2)}) collective-permute-start(f32[32,256]{1,0:T(8,128)S(1)} %solve_feat.1.a_ref), channel_id=1, source_target_pairs={{0,8},{4,12},{8,0},{12,4},{16,24},{20,28},{24,16},{28,20},{32,40},... | collective-permute-start | bytes 98312 | tf_op jit(solution)/shard_map/ppermute | solution.py:329
  46.9 4.0 %collective-permute-start.17 = (f32[32,256]{1,0:T(8,128)S(1)}, f32[32,256]{1,0:T(8,128)S(1)}, u32[]{:S(2)}, u32[]{:S(2)}) collective-permute-start(f32[32,256]{1,0:T(8,128)S(1)} %solve_feat.1.a_ref), channel_id=1, source_target_pairs={{0,12},{4,8},{8,4},{12,0},{16,28},{20,24},{24,20},{28,16},{32,44},... | collective-permute-start | bytes 98312 | tf_op jit(solution)/shard_map/ppermute | solution.py:329
  48.2 2.8 %collective-permute-start.18 = (f32[32,256]{1,0:T(8,128)S(1)}, f32[32,256]{1,0:T(8,128)S(1)}, u32[]{:S(2)}, u32[]{:S(2)}) collective-permute-start(f32[32,256]{1,0:T(8,128)S(1)} %solve_feat.1.a_ref), channel_id=1, source_target_pairs={{0,4},{4,0},{8,12},{12,8},{16,20},{20,16},{24,28},{28,24},{32,36},... | collective-permute-start | bytes 98312 | tf_op jit(solution)/shard_map/ppermute | solution.py:329
  51.0 6.5 %collective-permute-start.19 = (f32[32,128]{1,0:T(8,128)S(1)}, f32[32,128]{1,0:T(8,128)S(1)}, u32[]{:S(2)}, u32[]{:S(2)}) collective-permute-start(f32[32,128]{1,0:T(8,128)S(1)} %get-tuple-element.76.refs_0_), channel_id=1, source_target_pairs={{0,2},{2,0},{1,3},{3,1},{4,6},{6,4},{5,7},{7,5},{8,10},{10,8},{9,1... | collective-permute-start | bytes 49160 | tf_op jit(solution)/shard_map/ppermute | solution.py:323
